TPU v7x, 32 devices: a whole 2x2x4 slice. The times are simulated.
32 devices in a mesh: pool: 2 (over x), pw: 16 (over z, y, core).
Axes of the slice: x: 2, y: 2, z: 4, core: 2. Of those that a mesh axis runs over, the one named last changes fastest.
Arguments:
- orbitals: float32 [2, 2, 2, 192, 192, 192], P('pool', None, None, 'pw'), may hold values from -6 to 6
- responses: float32 [2, 2, 2, 192, 192, 192], P('pool', None, None, 'pw'), may hold values from -6 to 6
- energies: float32 [2, 2], P('pool'), may hold values from -0.6 to 0.4
- weights: float32 [2], P('pool'), may hold values from 0.5 to 1.5
- potential: float32 [192, 192, 192], P(None, 'pw'), may hold values from -3 to 3
- perturbation: float32 [192, 192, 192], P(None, 'pw'), may hold values from 0.2 to 2
Outputs:
- new_responses: float32 [2, 2, 2, 192, 192, 192], P('pool', None, None, 'pw')
- response_density: float32 [192, 192, 192], P('pw')
All inputs are finite; a program needn't handle non-finite values.
Results may differ from a plain program's by a relative error of at most 0.0003.
Values sent between devices are 32-bit elements; how exact they have to be, the bound alone decides.
No kernel may reach another device: no remote copies, remote signals or barrier semaphores. Data moves between devices by JAX's collectives and lax.ppermute only.
A program may use at most 192 MiB of HBM per device.

v0:
```python
import math

import jax
import jax.numpy as jnp
from jax import lax
from jax.sharding import PartitionSpec as P

RECIPROCAL_SQUARE = 0.023428


def tables(length):
    indices = jnp.arange(length, dtype=jnp.int32)
    angles = (indices[:, None] * indices[None, :] % length).astype(jnp.float32) * (
        2.0 * math.pi / length
    )
    factor = 1.0 / math.sqrt(length)
    return (jnp.cos(angles) * factor, jnp.sin(angles) * factor)


def apply_table(values, table_in, along_axis):
    rotated = jnp.tensordot(
        values, table_in, axes=((along_axis,), (0,)), precision=lax.Precision.HIGHEST
    )
    return jnp.moveaxis(rotated, -1, along_axis)


def transform(field_in, along_axis, cosine_table, sine_table, phase_sign):
    real_part = field_in[:, :, 0]
    imag_part = field_in[:, :, 1]
    real_cos = apply_table(real_part, cosine_table, along_axis)
    real_sin = apply_table(real_part, sine_table, along_axis)
    imag_cos = apply_table(imag_part, cosine_table, along_axis)
    imag_sin = apply_table(imag_part, sine_table, along_axis)
    return jnp.stack((real_cos - phase_sign * imag_sin, phase_sign * real_sin + imag_cos), axis=2)


def signed_freq(indices, length):
    return jnp.where(indices < length // 2, indices, indices - length).astype(jnp.float32)


def negated(values, along_axis):
    return jnp.roll(jnp.flip(values, along_axis), 1, along_axis)


def products(left_side, right_side):
    band_count = left_side.shape[0]
    highest = lax.Precision.HIGHEST
    left_real = left_side[:, 0].reshape(band_count, -1)
    left_imag = left_side[:, 1].reshape(band_count, -1)
    right_real = right_side[:, 0].reshape(band_count, -1)
    right_imag = right_side[:, 1].reshape(band_count, -1)
    real_sum = jnp.dot(left_real, right_real.T, precision=highest) + jnp.dot(
        left_imag, right_imag.T, precision=highest
    )
    imag_sum = jnp.dot(left_real, right_imag.T, precision=highest) - jnp.dot(
        left_imag, right_real.T, precision=highest
    )
    return (real_sum, imag_sum)


def body(orbitals, responses, energies, weights, potential, perturbation):
    length = orbitals.shape[-1]
    slab_rows = orbitals.shape[3]
    cosine_table, sine_table = tables(length)

    def to_space(field_in):
        return transform(
            transform(field_in, 4, cosine_table, sine_table, 1.0), 3, cosine_table, sine_table, 1.0
        )

    def finish_one(one_piece):
        return transform(one_piece, 2, cosine_table, sine_table, 1.0)

    orbital_space = finish_one(
        lax.all_to_all(to_space(orbitals), "pw", split_axis=4, concat_axis=3, tiled=True)
    )
    response_space = finish_one(
        lax.all_to_all(to_space(responses), "pw", split_axis=4, concat_axis=3, tiled=True)
    )
    partial_value = (
        2.0
        * weights[0]
        * jnp.sum(
            orbital_space[0, :, 0] * response_space[0, :, 0]
            + orbital_space[0, :, 1] * response_space[0, :, 1],
            axis=0,
        )
    )
    applied_space = potential * response_space + perturbation * orbital_space
    first_row = lax.axis_index("pw") * slab_rows
    row_freq = signed_freq(first_row + jnp.arange(slab_rows, dtype=jnp.int32), length)
    full_freq = signed_freq(jnp.arange(length, dtype=jnp.int32), length)
    kinetic = (
        0.5
        * RECIPROCAL_SQUARE
        * (
            row_freq[:, None, None] * row_freq[:, None, None]
            + full_freq[None, :, None] * full_freq[None, :, None]
            + full_freq[None, None, :] * full_freq[None, None, :]
        )
    )
    shifted = kinetic[None] - energies[0][:, None, None, None]
    direct = shifted[None, :, None] * responses
    sectioned = transform(
        transform(applied_space, 4, cosine_table, sine_table, -1.0),
        2,
        cosine_table,
        sine_table,
        -1.0,
    )
    residual = direct + transform(
        lax.all_to_all(sectioned, "pw", split_axis=3, concat_axis=4, tiled=True),
        3,
        cosine_table,
        sine_table,
        -1.0,
    )
    over_real, over_imag = lax.psum(products(orbitals[0], residual[0]), "pw")
    highest = lax.Precision.HIGHEST
    orbital_real = orbitals[0, :, 0]
    orbital_imag = orbitals[0, :, 1]
    combine_real = jnp.einsum(
        "mn,mxyz->nxyz", over_real, orbital_real, precision=highest
    ) - jnp.einsum("mn,mxyz->nxyz", over_imag, orbital_imag, precision=highest)
    combine_imag = jnp.einsum(
        "mn,mxyz->nxyz", over_imag, orbital_real, precision=highest
    ) + jnp.einsum("mn,mxyz->nxyz", over_real, orbital_imag, precision=highest)
    cell_count = float(length**3)
    projected = residual - jnp.stack((combine_real, combine_imag), axis=1)[None] / cell_count
    new_responses = responses - projected / (1.0 + kinetic)[None, None, None]
    summed = lax.psum(partial_value, "pool")
    mirrored = summed + negated(summed, 0)
    row_slab = lax.all_to_all(mirrored, "pw", split_axis=0, concat_axis=1, tiled=True)
    signsum = row_slab + negated(row_slab, 1)
    swapped = lax.all_to_all(signsum, "pw", split_axis=1, concat_axis=0, tiled=True)
    total_sym = signsum + jnp.transpose(swapped, (1, 0, 2))
    return (new_responses, total_sym / 8.0)


def solution(mesh):
    placed = (
        P("pool", None, None, "pw", None, None),
        P("pool", None, None, "pw", None, None),
        P("pool", None),
        P("pool"),
        P(None, "pw", None),
        P(None, "pw", None),
    )
    return jax.shard_map(
        body,
        mesh=mesh,
        in_specs=placed,
        out_specs=(P("pool", None, None, "pw", None, None), P("pw", None, None)),
        check_vma=False,
    )
```

profile of v0, /device:TPU:13, one launch (start us, length us, event | category | flops | bytes accessed | tf_op | source)
XLA Modules:
  0.0 1608.7 jit_solution(7493888581786955530)
XLA Ops:
  7.2 13.1 fusion.5
  20.3 10.2 fusion.103
  40.1 10.3 fusion.7
  50.4 10.5 fusion.100
  75.3 15.6 copy.169
  97.5 12.8 fusion.137
  110.3 12.8 fusion.116
  123.2 10.2 convolution_add_fusion
  143.2 10.3 convolution_subtract_fusion
  167.9 15.3 copy.181
  183.2 119.1 %all-to-all-done = f32[1,2,2,12,192,192]{5,2,3,1,0,4:T(2,128)} async-done(((f32[1,2,2,12,192,192]{5,2,3,1,0,4:T(2,128)}), f32[1,2,2,12,192,192]{5,2,3,1,0,4:T(2,128)}, u32[]{:S(2)}, u32[]{:S(2)}) %all-to-all-start) | async-done | bytes 7077920 | tf_op jit(solution)/shard_map/all_to_all | solution.py:78
  316.7 8.5 fusion.313
  325.3 11.9 copy.259
  337.1 9.2 fusion.39
  353.3 158.7 %all-to-all-done.1 = f32[1,2,2,12,192,192]{5,2,3,1,0,4:T(2,128)} async-done(((f32[1,2,2,12,192,192]{5,2,3,1,0,4:T(2,128)}), f32[1,2,2,12,192,192]{5,2,3,1,0,4:T(2,128)}, u32[]{:S(2)}, u32[]{:S(2)}) %all-to-all-start.1) | async-done | bytes 7077920 | tf_op jit(solution)/shard_map/all_to_all | solution.py:75
  520.9 8.6 fusion.312
  529.4 12.2 copy.263
  541.7 9.2 fusion.23
  557.9 11.8 copy.258
  569.8 12.0 copy.262
  581.8 9.0 fusion.93
  590.8 9.6 fusion.90
  605.5 12.8 fusion.14
  621.7 68.3 %all-reduce.3.cloned.1.call-done = f32[192,12,192]{0,2,1:T(8,128)} async-done(((f32[192,12,192]{0,2,1:T(8,128)}), f32[192,12,192]{0,2,1:T(8,128)}) %all-reduce.3.cloned.1.call-update) | async-done | bytes 1769488 | tf_op jit(solution)/shard_map/psum | solution.py:131
  693.7 25.2 %reverse.4 = f32[256,12,192]{0,2,1:T(8,128)} reverse(f32[256,12,192]{0,2,1:T(8,128)} %bitcast.432), dimensions={0} | reverse | bytes 4718592
  740.7 8.6 fusion
  749.4 12.1 fusion.55
  761.5 12.1 fusion.56
  773.6 30.5 %all-to-all-done.3 = f32[192,12,192]{2,1,0:T(8,128)S(1)} async-done(((f32[192,12,192]{2,1,0:T(8,128)}), f32[192,12,192]{2,1,0:T(8,128)S(1)}, u32[]{:S(2)}, u32[]{:S(2)}) %all-to-all-start.3) | async-done | bytes 1769504 | tf_op jit(solution)/shard_map/all_to_all | solution.py:133
  810.7 24.3 %slice.95 = f32[12,191,192]{2,1,0:T(8,128)} reverse(f32[12,191,192]{2,1,0:T(8,128)} %slice.111), dimensions={1} | reverse | bytes 3520512 | tf_op jit(solution)/shard_map/jit(_roll_static)/slice | solution.py:42
  846.5 13.9 multiply_subtract_fusion
  860.4 10.0 fusion.121
  870.5 10.2 fusion.144
  880.7 10.0 multiply_add_fusion
  890.8 9.9 subtract_bitcast_fusion.2
  900.6 10.1 add_bitcast_fusion.2
  915.1 15.6 copy.194
  937.3 10.1 copy.212
  947.4 17.1 %copy.275 = f32[1,2,2,12,192,192]{5,1,4,3,2,0:T(2,128)} copy(f32[1,2,2,12,192,192]{5,4,3,2,1,0:T(8,128)} %param.6) | data formatting | bytes 14155776 | tf_op args[0]
  969.4 8.5 slice_bitcast_fusion.6
  982.6 159.3 %all-to-all-done.2 = f32[1,2,2,192,12,192]{5,2,4,1,0,3:T(2,128)} async-done(((f32[1,2,2,192,12,192]{5,2,4,1,0,3:T(2,128)}), f32[1,2,2,192,12,192]{5,2,4,1,0,3:T(2,128)}, u32[]{:S(2)}, u32[]{:S(2)}) %all-to-all-start.2) | async-done | bytes 7077920 | tf_op jit(solution)/shard_map/all_to_all | solution.py:112
  1150.2 10.3 fusion.311
  1160.6 11.6 copy.265
  1172.2 9.2 fusion.15
  1188.5 11.6 copy.264
  1200.1 8.7 add_bitcast_fusion.1
  1208.9 9.2 subtract_bitcast_fusion.1
  1223.5 8.6 slice_bitcast_fusion.1
  1232.1 8.1 copy.201
  1240.2 8.2 copy.200
  1248.4 45.9 %fusion.107 = f32[2,2]{1,0:T(2,128)S(1)} fusion(f32[2,12,192,192]{3,0,2,1:T(2,128)} %copy.200, f32[2,2,12,192,192]{4,0,3,2,1:T(2,128)} %bitcast.426), kind=kOutput, calls=%fused_computation.122 | convolution fusion | flops 21233664 | bytes 9437200 | tf_op jit(solution)/shard_map/dot_general | solution.py:55
  1294.3 42.7 %fusion.106 = f32[2,2]{1,0:T(2,128)S(1)} fusion(f32[2,12,192,192]{3,0,2,1:T(2,128)S(1)} %bitcast.436, f32[2,2,12,192,192]{4,0,3,2,1:T(2,128)} %bitcast.427), kind=kOutput, calls=%fused_computation.121 | convolution fusion | flops 21233664 | bytes 8257552 | tf_op jit(solution)/shard_map/dot_general | solution.py:52
  1337.1 44.0 %fusion.111 = f32[2,2]{0,1:T(2,128)S(1)} fusion(f32[2,2]{1,0:T(2,128)S(1)} %fusion.107, f32[2,12,192,192]{3,0,2,1:T(2,128)S(1)} %bitcast.436, f32[2,2,12,192,192]{4,0,3,2,1:T(2,128)S(1)} %bitcast.430), kind=kOutput, calls=%fused_computation.126 | convolution fusion | flops 21233668 | bytes 9438224 | tf_op jit(solution)/shard_map/dot_general | solution.py:55
  1381.2 43.7 %fusion.113 = f32[2,2]{0,1:T(2,128)S(1)} fusion(f32[2,2]{1,0:T(2,128)S(1)} %fusion.106, f32[2,12,192,192]{3,0,2,1:T(2,128)S(1)} %bitcast.434, f32[2,2,12,192,192]{4,0,3,2,1:T(2,128)S(1)} %bitcast.431), kind=kOutput, calls=%fused_computation.128 | convolution fusion | flops 21233668 | bytes 9438224 | tf_op jit(solution)/shard_map/dot_general | solution.py:52
  1426.6 21.9 %all-reduce = (f32[2,2]{0,1:T(2,128)S(1)}, f32[2,2]{0,1:T(2,128)S(1)}) all-reduce(f32[2,2]{0,1:T(2,128)S(1)} %fusion.111, f32[2,2]{0,1:T(2,128)S(1)} %fusion.113), channel_id=1, replica_groups=mesh['pool'=2,'pw'=16] {'pw'}, use_global_device_ids=true, to_apply=%region_1.2 | all-reduce | flops 8 | bytes 64 | tf_op jit(solution)/shard_map/psum | solution.py:118
  1448.5 24.6 %fusion.67 = f32[2,12,192,192]{3,0,2,1:T(2,128)} fusion(f32[2,12,192,192]{3,2,1,0:T(8,128)} %get-tuple-element.12, f32[2,2]{0,1:T(2,128)S(1)} %get-tuple-element.11), kind=kOutput, calls=%fused_computation.97 | convolution fusion | flops 21233664 | bytes 7077904 | tf_op jit(solution)/shard_map/mn,mxyz->nxyz/dot_general | solution.py:127
  1473.2 19.7 %fusion.69 = f32[2,12,192,192]{3,0,2,1:T(2,128)} fusion(f32[2,12,192,192]{3,2,1,0:T(8,128)S(1)} %bitcast.401, f32[2,2]{0,1:T(2,128)S(1)} %get-tuple-element.10), kind=kOutput, calls=%fused_computation.99 | convolution fusion | flops 21233664 | bytes 7077904 | tf_op jit(solution)/shard_map/mn,mxyz->nxyz/dot_general | solution.py:124
  1492.9 19.9 %fusion.71 = f32[2,12,192,192]{3,0,2,1:T(2,128)} fusion(f32[2,12,192,192]{3,2,1,0:T(8,128)S(1)} %bitcast.399, f32[2,2]{0,1:T(2,128)S(1)} %get-tuple-element.10), kind=kOutput, calls=%fused_computation.101 | convolution fusion | flops 21233664 | bytes 7077904 | tf_op jit(solution)/shard_map/mn,mxyz->nxyz/dot_general | solution.py:125
  1512.8 19.6 %fusion.73 = f32[2,12,192,192]{3,0,2,1:T(2,128)} fusion(f32[2,12,192,192]{3,2,1,0:T(8,128)S(1)} %bitcast.399, f32[2,2]{0,1:T(2,128)S(1)} %get-tuple-element.11), kind=kOutput, calls=%fused_computation.103 | convolution fusion | flops 21233664 | bytes 7077904 | tf_op jit(solution)/shard_map/mn,mxyz->nxyz/dot_general | solution.py:122
  1532.4 7.8 copy.207
  1548.0 7.9 copy.206
  1563.7 12.3 add_bitcast_fusion
  1576.0 15.7 fusion.3
  1591.7 10.0 copy.219
  (157 shorter events, 202.1 us)
Async XLA Ops:
  7.2 13.1 copy-start
  90.9 211.4 %all-to-all-start = ((f32[1,2,2,12,192,192]{5,2,3,1,0,4:T(2,128)}), f32[1,2,2,12,192,192]{5,2,3,1,0,4:T(2,128)}, u32[]{:S(2)}, u32[]{:S(2)}) async-start(f32[1,2,2,12,192,192]{5,2,3,1,0,4:T(2,128)} %copy.169), calls=%async_computation | async-start | bytes 18874368 | tf_op jit(solution)/shard_map/all_to_all | solution.py:78
  97.5 25.7 %slice-start = ((s8[9437184]{0:T(1024)(128)(4,1)}), s8[4194304]{0:T(1024)(128)(4,1)S(1)}, s32[]{:S(2)}) async-start(s8[9437184]{0:T(1024)(128)(4,1)} %bitcast.396), calls=%async_computation.6 | async-start | bytes 8388608
  97.5 25.7 %slice-start.1 = ((s8[9437184]{0:T(1024)(128)(4,1)}), s8[4194304]{0:T(1024)(128)(4,1)S(1)}, s32[]{:S(2)}) async-start(s8[9437184]{0:T(1024)(128)(4,1)} %bitcast.396), calls=%async_computation.7 | async-start | bytes 8388608
  110.3 12.9 slice-start.2
  302.3 209.7 %all-to-all-start.1 = ((f32[1,2,2,12,192,192]{5,2,3,1,0,4:T(2,128)}), f32[1,2,2,12,192,192]{5,2,3,1,0,4:T(2,128)}, u32[]{:S(2)}, u32[]{:S(2)}) async-start(f32[1,2,2,12,192,192]{5,2,3,1,0,4:T(2,128)} %copy.181), calls=%async_computation.1 | async-start | bytes 18874368 | tf_op jit(solution)/shard_map/all_to_all | solution.py:75
  307.2 382.7 %all-reduce.3.cloned.1.call-start = ((), (), s32[]{:S(2)}) async-start(), calls=%async_computation.5 | async-start | bytes 4718592 | tf_op jit(solution)/shard_map/psum | solution.py:131
  337.1 9.2 copy-start.4
  541.7 9.3 copy-start.5
  581.8 9.0 copy-start.2
  581.8 18.6 %slice-start.15 = ((s8[4718592]{0:T(1024)(128)(4,1)}), s8[4194304]{0:T(1024)(128)(4,1)S(1)}, s32[]{:S(2)}) async-start(s8[4718592]{0:T(1024)(128)(4,1)} %bitcast.408), calls=%async_computation.21 | async-start | bytes 8388608
  581.8 18.6 %slice-start.17 = ((s8[4718592]{0:T(1024)(128)(4,1)}), s8[4194304]{0:T(1024)(128)(4,1)S(1)}, s32[]{:S(2)}) async-start(s8[4718592]{0:T(1024)(128)(4,1)} %bitcast.419), calls=%async_computation.23 | async-start | bytes 8388608
  590.8 14.7 copy-start.9
  590.8 9.6 slice-start.16
  590.8 9.6 slice-start.18
  600.5 5.1 copy-start.10
  605.5 12.8 copy-start.11
  693.6 27.6 %copy-start.14 = (f32[192,12,192]{0,2,1:T(8,128)S(1)}, f32[192,12,192]{0,2,1:T(8,128)}, u32[]{:S(2)}) copy-start(f32[192,12,192]{0,2,1:T(8,128)} %all-reduce.3.cloned.1.call-done) | copy-start | bytes 5308420
  693.7 27.6 %slice-start.21 = ((f32[192,12,192]{0,2,1:T(8,128)}), f32[1,12,192]{0,2,1:T(8,128)S(1)}, s32[]{:S(2)}) async-start(f32[192,12,192]{0,2,1:T(8,128)} %all-reduce.3.cloned.1.call-done), calls=%async_computation.27 | async-start | bytes 2359296 | tf_op jit(solution)/shard_map/jit(_roll_static)/slice | solution.py:42
  727.4 76.7 %all-to-all-start.3 = ((f32[192,12,192]{2,1,0:T(8,128)}), f32[192,12,192]{2,1,0:T(8,128)S(1)}, u32[]{:S(2)}, u32[]{:S(2)}) async-start(f32[192,12,192]{2,1,0:T(8,128)} %copy.213), calls=%async_computation.3 | async-start | bytes 6291456 | tf_op jit(solution)/shard_map/all_to_all | solution.py:133
  749.4 12.1 copy-start.1
  837.0 1.4 copy-start.12
  841.5 89.3 %all-to-all-start.4 = ((f32[12,192,192]{2,0,1:T(8,128)}), f32[12,192,192]{2,0,1:T(8,128)S(1)}, u32[]{:S(2)}, u32[]{:S(2)}) async-start(f32[12,192,192]{2,0,1:T(8,128)} %copy.216), calls=%async_computation.4 | async-start | bytes 6291456 | tf_op jit(solution)/shard_map/all_to_all | solution.py:135
  860.4 20.3 %slice-start.7 = ((s8[9437184]{0:T(1024)(128)(4,1)}), s8[4194304]{0:T(1024)(128)(4,1)S(1)}, s32[]{:S(2)}) async-start(s8[9437184]{0:T(1024)(128)(4,1)} %bitcast.402), calls=%async_computation.13 | async-start | bytes 8388608
  860.4 20.3 %slice-start.8 = ((s8[9437184]{0:T(1024)(128)(4,1)}), s8[4194304]{0:T(1024)(128)(4,1)S(1)}, s32[]{:S(2)}) async-start(s8[9437184]{0:T(1024)(128)(4,1)} %bitcast.402), calls=%async_computation.14 | async-start | bytes 8388608
  860.4 20.3 %slice-start.19 = ((s8[4718592]{0:T(1024)(128)(4,1)}), s8[4194304]{0:T(1024)(128)(4,1)S(1)}, s32[]{:S(2)}) async-start(s8[4718592]{0:T(1024)(128)(4,1)} %bitcast.421), calls=%async_computation.25 | async-start | bytes 8388608
  870.4 10.3 slice-start.9
  870.5 10.3 slice-start.20
  930.7 211.2 %all-to-all-start.2 = ((f32[1,2,2,192,12,192]{5,2,4,1,0,3:T(2,128)}), f32[1,2,2,192,12,192]{5,2,4,1,0,3:T(2,128)}, u32[]{:S(2)}, u32[]{:S(2)}) async-start(f32[1,2,2,192,12,192]{5,2,4,1,0,3:T(2,128)} %copy.194), calls=%async_computation.2 | async-start | bytes 18874368 | tf_op jit(solution)/shard_map/all_to_all | solution.py:112
  964.5 2.1 copy-start.16
  1172.2 9.2 copy-start.6
  1200.1 8.8 copy-start.3
  1200.1 18.0 %slice-start.10 = ((s8[9437184]{0:T(1024)(128)(4,1)}), s8[4194304]{0:T(1024)(128)(4,1)S(1)}, s32[]{:S(2)}) async-start(s8[9437184]{0:T(1024)(128)(4,1)} %bitcast.404), calls=%async_computation.16 | async-start | bytes 8388608
  1200.1 18.0 %slice-start.11 = ((s8[9437184]{0:T(1024)(128)(4,1)}), s8[4194304]{0:T(1024)(128)(4,1)S(1)}, s32[]{:S(2)}) async-start(s8[9437184]{0:T(1024)(128)(4,1)} %bitcast.404), calls=%async_computation.17 | async-start | bytes 8388608
  1200.1 18.0 %slice-start.13 = ((s8[4718592]{0:T(1024)(128)(4,1)}), s8[4194304]{0:T(1024)(128)(4,1)S(1)}, s32[]{:S(2)}) async-start(s8[4718592]{0:T(1024)(128)(4,1)} %bitcast.406), calls=%async_computation.19 | async-start | bytes 8388608
  1208.9 9.2 copy-start.7
  1208.9 9.2 slice-start.12
  1208.9 9.2 slice-start.14
  1218.2 5.3 copy-start.8
  1240.2 54.1 %slice-start.27 = ((s8[4718592]{0:T(1024)(128)(4,1)}), s8[524288]{0:T(1024)(128)(4,1)S(1)}, s32[]{:S(2)}) async-start(s8[4718592]{0:T(1024)(128)(4,1)} %bitcast.435), calls=%async_computation.33 | async-start | bytes 1048576
  1248.4 45.9 %slice-start.28 = ((s8[4718592]{0:T(1024)(128)(4,1)}), s8[4194304]{0:T(1024)(128)(4,1)S(1)}, s32[]{:S(2)}) async-start(s8[4718592]{0:T(1024)(128)(4,1)} %bitcast.435), calls=%async_computation.34 | async-start | bytes 8388608
  1248.4 88.7 %slice-start.22 = ((s8[9437184]{0:T(1024)(128)(4,1)}), s8[4194304]{0:T(1024)(128)(4,1)S(1)}, s32[]{:S(2)}) async-start(s8[9437184]{0:T(1024)(128)(4,1)} %bitcast.428), calls=%async_computation.28 | async-start | bytes 8388608
  1248.4 88.7 %slice-start.23 = ((s8[9437184]{0:T(1024)(128)(4,1)}), s8[4194304]{0:T(1024)(128)(4,1)S(1)}, s32[]{:S(2)}) async-start(s8[9437184]{0:T(1024)(128)(4,1)} %bitcast.428), calls=%async_computation.29 | async-start | bytes 8388608
  1294.3 42.8 %slice-start.24 = ((s8[9437184]{0:T(1024)(128)(4,1)}), s8[1048576]{0:T(1024)(128)(4,1)S(1)}, s32[]{:S(2)}) async-start(s8[9437184]{0:T(1024)(128)(4,1)} %bitcast.428), calls=%async_computation.30 | async-start | bytes 2097152
  1294.3 86.8 %slice-start.25 = ((s8[4718592]{0:T(1024)(128)(4,1)}), s8[4194304]{0:T(1024)(128)(4,1)S(1)}, s32[]{:S(2)}) async-start(s8[4718592]{0:T(1024)(128)(4,1)} %bitcast.433), calls=%async_computation.31 | async-start | bytes 8388608
  1337.1 44.0 %slice-start.26 = ((s8[4718592]{0:T(1024)(128)(4,1)}), s8[524288]{0:T(1024)(128)(4,1)S(1)}, s32[]{:S(2)}) async-start(s8[4718592]{0:T(1024)(128)(4,1)} %bitcast.433), calls=%async_computation.32 | async-start | bytes 1048576
  1381.2 43.7 %copy-start.13 = (f32[12,192,192]{2,1,0:T(8,128)S(1)}, f32[12,192,192]{2,1,0:T(8,128)}, u32[]{:S(2)}) copy-start(f32[12,192,192]{2,1,0:T(8,128)} %copy-done.12) | copy-start | bytes 5308420
  1424.9 48.3 %slice-start.5 = ((s8[4718592]{0:T(1024)(128)(4,1)}), s8[524288]{0:T(1024)(128)(4,1)S(1)}, s32[]{:S(2)}) async-start(s8[4718592]{0:T(1024)(128)(4,1)} %bitcast.400), calls=%async_computation.11 | async-start | bytes 1048576
  1448.5 24.6 %slice-start.6 = ((s8[4718592]{0:T(1024)(128)(4,1)}), s8[4194304]{0:T(1024)(128)(4,1)S(1)}, s32[]{:S(2)}) async-start(s8[4718592]{0:T(1024)(128)(4,1)} %bitcast.400), calls=%async_computation.12 | async-start | bytes 8388608
  1448.5 44.3 %slice-start.3 = ((s8[4718592]{0:T(1024)(128)(4,1)}), s8[4194304]{0:T(1024)(128)(4,1)S(1)}, s32[]{:S(2)}) async-start(s8[4718592]{0:T(1024)(128)(4,1)} %bitcast.398), calls=%async_computation.9 | async-start | bytes 8388608
  1473.1 19.7 %slice-start.4 = ((s8[4718592]{0:T(1024)(128)(4,1)}), s8[524288]{0:T(1024)(128)(4,1)S(1)}, s32[]{:S(2)}) async-start(s8[4718592]{0:T(1024)(128)(4,1)} %bitcast.398), calls=%async_computation.10 | async-start | bytes 1048576
  1563.7 12.3 copy-start.15
Sparse Core Ops, SparseCore 0:
  621.8 68.0 all-reduce.2
where the time goes:
time: 1630 us; the launch traced here: 1610 us
  matrix products  581 us (36%)
  waiting for transfers between devices  536 us (33%)
  local copies, waits for them, and re-layouts  355 us (22%)
  other arithmetic  69 us (4%)
  starting transfers between devices  30 us (2%)
  blocking collectives  21.9 us (1%)
    dot_general x36, matrix products, apply_table(): jnp.tensordot(values, table_in, axes=((along_axis,), (0,)), precision=lax...  321 us
    all_to_all x1, waiting for transfers between devices, body(): lax.all_to_all(sectioned, 'pw', split_axis=3, concat_axis=4, tiled=True)  159 us
    all_to_all x1, waiting for transfers between devices, body(): lax.all_to_all(to_space(orbitals), 'pw', split_axis=4, concat_axis=3, til...  159 us
    unnamed x103, local copies, waits for them, and re-layouts  144 us
    all_to_all x1, waiting for transfers between devices, body(): lax.all_to_all(to_space(responses), 'pw', split_axis=4, concat_axis=3, ti...  119 us
    psum x1, waiting for transfers between devices, body(): summed = lax.psum(partial_value, 'pool')  68.3 us
    another operation x3, local copies, waits for them, and re-layouts, transform(): jnp.stack((real_cos - phase_sign * imag_sin, phase_sign * real_sin + imag...  46.5 us
    dot_general x1, matrix products, products(): jnp.dot(left_imag, right_real.T, precision=highest)  45.9 us
  transfers between devices with their start and end apart: 6, of which 5 were waited for; matrix products, arithmetic and copies ran while one was open for 18% of the time, Pallas kernels for 0%

commit v1 on v0

--- a/solution.py
+++ b/solution.py
@@ -1,11 +1,515 @@
+import functools
 import math
 
 import jax
 import jax.numpy as jnp
+import ml_dtypes
+import numpy as np
 from jax import lax
+from jax.experimental import pallas as pl
+from jax.experimental.pallas import tpu as pltpu
 from jax.sharding import PartitionSpec as P
 
 RECIPROCAL_SQUARE = 0.023428
+VMEM_BYTES = 56 * 1024 * 1024
+
+
+def split_table(table):
+    high = table.astype(ml_dtypes.bfloat16)
+    low = (table - high.astype(np.float64)).astype(ml_dtypes.bfloat16)
+    return np.stack((high, low))
+
+
+@functools.cache
+def matrices(length, slab, members):
+    index = np.arange(length)
+    angles = (index[:, None] * index[None, :] % length) * (2.0 * math.pi / length)
+    cosine = np.cos(angles) / math.sqrt(length)
+    sine = np.sin(angles) / math.sqrt(length)
+    lanes = 128 * -(-length // 128)
+    pad = ((0, 0), (0, lanes - length))
+    inverse = np.block([[cosine, -sine], [sine, cosine]])
+    forward = np.block([[cosine, sine], [-sine, cosine]])
+    sent = np.arange(2 * length).reshape(2, members, slab).transpose(1, 0, 2).reshape(-1)
+    got = np.arange(2 * length).reshape(2, members, slab // 2, 2).transpose(0, 3, 1, 2).reshape(-1)
+    mirror = np.eye(length) + np.eye(length)[(-index) % length]
+    both = np.zeros((members, 2, slab, 2, length))
+    for which in range(2):
+        both[:, which, :, which, :] = mirror.reshape(members, slab, length)
+    return {
+        "cosine": split_table(np.pad(cosine, pad)),
+        "sine": split_table(np.pad(sine, pad)),
+        "inverse_send": split_table(inverse[sent]),
+        "inverse_receive": split_table(inverse[:, got]),
+        "forward_send": split_table(forward[sent]),
+        "forward_receive": split_table(forward[:, got]),
+        "mirror_pair": both.reshape(2 * length, 2 * length).astype(ml_dtypes.bfloat16),
+    }
+
+
+def halves(values):
+    high = values.astype(jnp.bfloat16)
+    return high, (values - high.astype(jnp.float32)).astype(jnp.bfloat16)
+
+
+def dot(left, right):
+    return lax.dot_general(
+        left, right, (((1,), (0,)), ((), ())), preferred_element_type=jnp.float32
+    )
+
+
+def dot_right(values, table):
+    high, low = halves(values)
+    return dot(high, table[0]) + (dot(high, table[1]) + dot(low, table[0]))
+
+
+def dot_left(table, values):
+    high, low = halves(values)
+    return dot(table[0], high) + (dot(table[0], low) + dot(table[1], high))
+
+
+def dot_mirror(table, values):
+    high, low = halves(values)
+    low_rest = (values - high.astype(jnp.float32) - low.astype(jnp.float32)).astype(jnp.bfloat16)
+    return dot(table, high) + (dot(table, low) + dot(table, low_rest))
+
+
+def merge_tails(first, second):
+    return first + pltpu.roll(second, 64, 1)
+
+
+def to_half_kernel(field, cosine, sine, send, out):
+    pair, length = field.shape[3], field.shape[4]
+    members, rows = out.shape[0], out.shape[3]
+    values = field[...].reshape(2 * pair * length, length)
+    by_cos = dot_right(values, cosine)
+    by_sin = dot_right(values, sine)
+    mid = pair * length
+    real = by_cos[:mid] - by_sin[mid:]
+    imag = by_sin[:mid] + by_cos[mid:]
+    tails = []
+    for one in range(pair):
+        part = slice(one * length, (one + 1) * length)
+        done = dot_left(send, jnp.concatenate((real[part], imag[part]), axis=0))
+        out[:, 0, one] = done[:, :128].reshape(members, rows, 128)
+        tails.append(done[:, 128:])
+    out[:, 0, 2] = merge_tails(*tails).reshape(members, rows, 128)
+
+
+def received(ref, start, stride, count):
+    return ref[pl.ds(start, count, stride=stride), :]
+
+
+def plane(got, chunks, place, slab, count, with_main, with_tail):
+    stride = chunks * 2 * slab
+    found = []
+    for part in range(2):
+        row = part * slab + place
+        if with_main:
+            mains = [received(got, one * 2 * slab + row, stride, count) for one in range(2)]
+        if with_tail:
+            tail = received(got, (chunks - 1) * 2 * slab + row, stride, count)
+            tails = [tail, pltpu.roll(tail, 64, 1)]
+        for one in range(2):
+            pieces = ([mains[one]] if with_main else []) + ([tails[one]] if with_tail else [])
+            found.append(jnp.concatenate(pieces, axis=1) if len(pieces) > 1 else pieces[0])
+    return jnp.concatenate(found, axis=0)
+
+
+def to_space_kernel(slab, got, receive, space):
+    count = got.shape[0] // (6 * slab)
+    for one in range(2):
+        place = 2 * pl.program_id(0) + one
+        values = plane(got, 3, place, slab, count, True, True)
+        space[one] = dot_left(receive, values)[:, : space.shape[2]]
+
+
+def folded(values):
+    return values.reshape(-1, 8, values.shape[-1]).sum(axis=0)
+
+
+def apply_kernel(
+    slab, band, weights, got, spaces, potential, perturbation, before,
+    receive, cosine, sine, send, mirror, out_main, out_tail, inner, density, *high_half
+):
+    length = potential.shape[1]
+    members, rows = out_main.shape[0], out_main.shape[3]
+    count = got.shape[0] // (6 * slab)
+    step = pl.program_id(0)
+    twice_weight = 2.0 * weights[0]
+
+    @pl.when(step == 0)
+    def _():
+        inner[...] = jnp.zeros_like(inner)
+
+    tails = []
+    sums = []
+    for one in range(2):
+        values = plane(got, 3, 2 * step + one, slab, count, True, True)
+        response = dot_left(receive, values)[:, :length]
+        real, imag = response[:length], response[length:]
+        own_real, own_imag = spaces[band, one, :length], spaces[band, one, length:]
+        local = twice_weight * (own_real * real + own_imag * imag)
+        if before is not None:
+            local = local + before[one]
+        sums.append(local)
+        field, change = potential[one], perturbation[one]
+        real = field * real + change * own_real
+        imag = field * imag + change * own_imag
+        for other in range(2):
+            left_real, left_imag = spaces[other, one, :length], spaces[other, one, length:]
+            inner[0, other] += folded(left_real * real + left_imag * imag)
+            inner[1, other] += folded(left_real * imag - left_imag * real)
+        both = jnp.concatenate((real, imag), axis=0)
+        by_cos = dot_right(both, cosine)
+        by_sin = dot_right(both, sine)
+        turned = jnp.concatenate(
+            (by_cos[:length] + by_sin[length:], by_cos[length:] - by_sin[:length]), axis=0
+        )
+        done = dot_left(send, turned)
+        out_main[:, 0, one] = done[:, :128].reshape(members, rows, 128)
+        tails.append(done[:, 128:])
+    tail = merge_tails(*tails).reshape(members, rows, 128)
+    if out_tail is None:
+        out_main[:, 0, 2] = tail
+    else:
+        out_tail[:, 0] = tail
+    if not high_half:
+        for one in range(2):
+            density[one] = sums[one]
+        return
+    summed = dot_mirror(mirror[...], jnp.concatenate(sums, axis=0))
+    density[...] = summed[:, :128].reshape(density.shape)
+    half = length // 2
+    lanes = jnp.concatenate((summed[:, half:], summed[:, :half]), axis=1)[:, :128]
+    high_half[0][...] = lanes.reshape(density.shape)
+
+
+def frequencies(length, first, lanes, first_lane):
+    rows = lax.broadcasted_iota(jnp.int32, (length, lanes), 0)
+    columns = lax.broadcasted_iota(jnp.int32, (length, lanes), 1) + first_lane
+    row = jnp.where(rows < length // 2, rows, rows - length).astype(jnp.float32)
+    column = jnp.where(columns < length // 2, columns, columns - length).astype(jnp.float32)
+    outer = jnp.where(first < length // 2, first, first - length).astype(jnp.float32)
+    return 0.5 * RECIPROCAL_SQUARE * (outer * outer + row * row + column * column)
+
+
+def inner_kernel(slab, me, energies, orbitals, responses, inner):
+    length = orbitals.shape[4]
+    step = pl.program_id(0)
+
+    @pl.when(step == 0)
+    def _():
+        inner[...] = jnp.zeros_like(inner)
+
+    for one in range(2):
+        kinetic = frequencies(length, me[0] * slab + 2 * step + one, length, 0)
+        for band in range(2):
+            shifted = kinetic - energies[0, band]
+            real = shifted * responses[0, band, 0, one]
+            imag = shifted * responses[0, band, 1, one]
+            for other in range(2):
+                left_real, left_imag = orbitals[0, other, 0, one], orbitals[0, other, 1, one]
+                inner[0, other, band] += folded(left_real * real + left_imag * imag)
+                inner[1, other, band] += folded(left_real * imag - left_imag * real)
+
+
+def direct_kernel(slab, me, energies, inner, orbitals, responses, out):
+    length = orbitals.shape[4]
+    cells = float(length**3)
+    for one in range(2):
+        kinetic = frequencies(length, me[0] * slab + 2 * pl.program_id(0) + one, length, 0)
+        inverse = 1.0 / (1.0 + kinetic)
+        for band in range(2):
+            shifted = kinetic - energies[0, band]
+            real = shifted * responses[0, band, 0, one]
+            imag = shifted * responses[0, band, 1, one]
+            for other in range(2):
+                left_real, left_imag = orbitals[0, other, 0, one], orbitals[0, other, 1, one]
+                by_real = inner[0, other, band] / cells
+                by_imag = inner[1, other, band] / cells
+                real = real - (left_real * by_real - left_imag * by_imag)
+                imag = imag - (left_real * by_imag + left_imag * by_real)
+            out[0, band, 0, one] = responses[0, band, 0, one] - real * inverse
+            out[0, band, 1, one] = responses[0, band, 1, one] - imag * inverse
+
+
+def finish_kernel(slab, chunks, tail, me, got, receive, base, out):
+    length = base.shape[4]
+    count = got.shape[0] // (chunks * 2 * slab)
+    for one in range(2):
+        place = 2 * pl.program_id(0) + one
+        values = plane(got, chunks, place, slab, count, not tail, tail)
+        applied = dot_left(receive, values)
+        kinetic = frequencies(length, me[0] * slab + place, 128, 128 if tail else 0)
+        inverse = 1.0 / (1.0 + kinetic)
+        for part in range(2):
+            piece = applied[part * length : (part + 1) * length]
+            out[0, 0, part, one] = base[0, 0, part, one] - piece * inverse
+
+
+def mirror_kernel(slab, got, mirror, single, out, natural):
+    length = natural.shape[1]
+    planes = [
+        received(got, 2 * pl.program_id(0) + one, slab, length) for one in range(2)
+    ]
+    out[...] = dot_mirror(mirror[...], jnp.concatenate(planes, axis=0)).reshape(out.shape)
+    for one in range(2):
+        natural[one] = dot_mirror(single[...], planes[one])
+
+
+def swap_kernel(slab, got, natural, out):
+    length = natural.shape[1]
+    for one in range(2):
+        swapped = received(got, 2 * pl.program_id(0) + one, slab, length)
+        out[one] = (natural[one] + swapped) * 0.125
+
+
+def cost(flops, moved):
+    return pl.CostEstimate(flops=int(flops), bytes_accessed=int(moved), transcendentals=0)
+
+
+def whole():
+    return pl.BlockSpec(memory_space=pltpu.VMEM)
+
+
+def scalars():
+    return pl.BlockSpec(memory_space=pltpu.SMEM)
+
+
+def call(kernel, name, grid, ins, outs, shapes, estimate, aliases=None):
+    return pl.pallas_call(
+        kernel,
+        grid=(grid,),
+        in_specs=ins,
+        out_specs=outs,
+        out_shape=shapes,
+        compiler_params=pltpu.CompilerParams(
+            dimension_semantics=("arbitrary",), vmem_limit_bytes=VMEM_BYTES
+        ),
+        cost_estimate=estimate,
+        input_output_aliases=aliases or {},
+        name=name,
+    )
+
+
+def f32(*shape):
+    return jax.ShapeDtypeStruct(shape, jnp.float32)
+
+
+def packed_body(orbitals, responses, energies, weights, potential, perturbation):
+    length = orbitals.shape[-1]
+    slab = orbitals.shape[3]
+    members = length // slab
+    pairs = slab // 2
+    rows = 2 * slab
+    half = length // 2
+    table = {key: jnp.asarray(value) for key, value in matrices(length, slab, members).items()}
+    single = jnp.asarray(
+        (np.eye(length) + np.eye(length)[(-np.arange(length)) % length]).astype(ml_dtypes.bfloat16)
+    )
+    me = lax.axis_index("pw").astype(jnp.int32).reshape(1)
+    pool = lax.axis_index("pool")
+    flat = (members * pairs * 3 * rows, 128)
+    field_bytes = 4 * members * pairs * 3 * rows * 128
+    stage_flops = 6 * 2 * 2 * length * length * length * slab * 2
+
+    half_spec = pl.BlockSpec((members, 1, 3, rows, 128), lambda p: (0, p, 0, 0, 0))
+    half_shape = f32(members, pairs, 3, rows, 128)
+
+    def exchange(values, after=None):
+        values = values.reshape(members, -1, 128)
+        if after is not None:
+            values, _ = lax.optimization_barrier((values, after))
+        return lax.all_to_all(values, "pw", split_axis=0, concat_axis=0, tiled=True)
+
+    def to_half(field, band):
+        return call(
+            to_half_kernel,
+            "to_half",
+            pairs,
+            [
+                pl.BlockSpec((1, 1, 2, 2, length, length), lambda p: (0, band, 0, p, 0, 0)),
+                whole(),
+                whole(),
+                whole(),
+            ],
+            half_spec,
+            half_shape,
+            cost(2 * stage_flops, 2 * field_bytes),
+        )(field, table["cosine"], table["sine"], table["inverse_send"])
+
+    def to_space(got):
+        return call(
+            functools.partial(to_space_kernel, slab),
+            "to_space",
+            pairs,
+            [whole(), whole()],
+            pl.BlockSpec((2, 2 * length, length), lambda p: (p, 0, 0)),
+            f32(slab, 2 * length, length),
+            cost(stage_flops, 2 * field_bytes),
+        )(got.reshape(flat), table["inverse_receive"])
+
+    plane_spec = pl.BlockSpec((2, length, length), lambda p: (p, 0, 0))
+    send_specs = [
+        pl.BlockSpec((members, 1, 2, rows, 128), lambda p: (0, p, 0, 0, 0)),
+        pl.BlockSpec((members, 1, rows, 128), lambda p: (0, p, 0, 0)),
+    ]
+    send_shapes = [
+        f32(members, pairs, 2, rows, 128),
+        f32(members, pairs, rows, 128),
+    ]
+    density_spec = pl.BlockSpec((members, 2 * slab, 128), lambda p: (0, p, 0))
+    density_shape = f32(members, slab * slab, 128)
+    inner_spec = pl.BlockSpec((2, 2, 8, length), lambda p: (0, 0, 0, 0))
+
+    def apply_first(got, spaces, field, change):
+        def kernel(weights, got, first, second, field, change, *tables_and_outs):
+            receive, cosine, sine, send, main, inner, density = tables_and_outs
+            apply_kernel(
+                slab, 0, weights, got, Both(first, second), field, change, None,
+                receive, cosine, sine, send, None, main, None, inner, density,
+            )
+
+        return call(
+            kernel,
+            "apply_first",
+            pairs,
+            [scalars(), whole(), space_spec, space_spec, plane_spec, plane_spec] + [whole()] * 4,
+            [half_spec, inner_spec, plane_spec],
+            [half_shape, f32(2, 2, 8, length), f32(slab, length, length)],
+            cost(3 * stage_flops, 5 * field_bytes),
+        )(
+            weights, got.reshape(flat), *spaces, field, change,
+            table["inverse_receive"], table["cosine"], table["sine"], table["forward_send"],
+        )
+
+    def apply_last(got, spaces, field, change, before):
+        def kernel(weights, got, first, second, field, change, before, *tables_and_outs):
+            receive, cosine, sine, send, mirror, main, tail, inner, low, high = tables_and_outs
+            apply_kernel(
+                slab, 1, weights, got, Both(first, second), field, change, before,
+                receive, cosine, sine, send, mirror, main, tail, inner, low, high,
+            )
+
+        return call(
+            kernel,
+            "apply_last",
+            pairs,
+            [scalars(), whole(), space_spec, space_spec] + [plane_spec] * 3 + [whole()] * 5,
+            send_specs + [inner_spec, density_spec, density_spec],
+            send_shapes + [f32(2, 2, 8, length), density_shape, density_shape],
+            cost(3 * stage_flops, 5 * field_bytes),
+        )(
+            weights, got.reshape(flat), *spaces, field, change, before,
+            table["inverse_receive"], table["cosine"], table["sine"], table["forward_send"],
+            table["mirror_pair"],
+        )
+
+    space_spec = pl.BlockSpec((2, 2 * length, length), lambda p: (p, 0, 0))
+    bands_spec = pl.BlockSpec((1, 2, 2, 2, length, length), lambda p: (0, 0, 0, p, 0, 0))
+
+    def finish(base, got, band, chunks, tail):
+        lane_block = 1 if tail else 0
+        one_spec = pl.BlockSpec(
+            (1, 1, 2, 2, length, 128), lambda p: (0, band, 0, p, 0, lane_block)
+        )
+        return call(
+            functools.partial(finish_kernel, slab, chunks, tail),
+            "finish",
+            pairs,
+            [scalars(), whole(), whole(), one_spec],
+            one_spec,
+            f32(*base.shape),
+            cost(stage_flops, 2 * field_bytes),
+            {3: 0},
+        )(me, got.reshape(-1, 128), table["forward_receive"], base)
+
+    field = jnp.transpose(potential, (1, 0, 2))
+    change = jnp.transpose(perturbation, (1, 0, 2))
+    got_one = exchange(to_half(orbitals, 0))
+    got_two = exchange(to_half(orbitals, 1), got_one)
+    got_first = exchange(to_half(responses, 0), got_two)
+    direct_inner = call(
+        functools.partial(inner_kernel, slab),
+        "inner",
+        pairs,
+        [scalars(), scalars(), bands_spec, bands_spec],
+        pl.BlockSpec((2, 2, 2, 8, length), lambda p: (0, 0, 0, 0, 0)),
+        f32(2, 2, 2, 8, length),
+        cost(32 * field_bytes, 4 * field_bytes),
+    )(me, energies, orbitals, responses)
+    got_last = exchange(to_half(responses, 1), (got_first, direct_inner))
+    spaces = [to_space(got_one), to_space(got_two)]
+    send_first, inner_first, before = apply_first(got_first, spaces, field, change)
+    back_first = exchange(send_first, got_last)
+    last_main, last_tail, inner_last, low, high = apply_last(
+        got_last, spaces, field, change, before
+    )
+    kept = jnp.where(pool == 0, low, high)
+    given = jnp.where(pool == 0, high, low)
+    swap = [(0, 1), (1, 0)]
+    local_inner = direct_inner + jnp.stack((inner_first, inner_last), axis=2)
+    local_inner = jnp.sum(local_inner, axis=(3, 4)).reshape(8)
+    riding = jnp.pad(local_inner, (0, slab * slab - 8)).reshape(1, -1, 1)
+    used = lax.broadcasted_iota(jnp.int32, density_shape.shape, 2) < half
+    summed = jnp.where(used, kept + lax.ppermute(given, "pool", swap), riding)
+    got_density = exchange(summed, back_first)
+    inner = jnp.sum(got_density[:, :8, half], axis=0).reshape(2, 2, 2)
+    back_tail = exchange(last_tail, got_density)
+    base = call(
+        functools.partial(direct_kernel, slab),
+        "direct",
+        pairs,
+        [scalars(), scalars(), scalars(), bands_spec, bands_spec],
+        bands_spec,
+        f32(*responses.shape),
+        cost(32 * field_bytes, 6 * field_bytes),
+    )(me, energies, inner, orbitals, responses)
+    natural_spec = pl.BlockSpec((2, length, 128), lambda p: (p, 0, 0))
+    mirrored, natural = call(
+        functools.partial(mirror_kernel, slab),
+        "mirror",
+        pairs,
+        [whole(), whole(), whole()],
+        [density_spec, natural_spec],
+        [density_shape, f32(slab, length, 128)],
+        cost(2e9, 4e6),
+    )(got_density.reshape(-1, 128), table["mirror_pair"], single)
+    got_mirrored = exchange(mirrored, (back_tail, base))
+    base = finish(base, back_first, 0, 3, False)
+    base = finish(base, back_first, 0, 3, True)
+    back_main = exchange(last_main, (got_mirrored, base))
+    symmetric = call(
+        functools.partial(swap_kernel, slab),
+        "swap",
+        pairs,
+        [whole(), natural_spec],
+        natural_spec,
+        f32(slab, length, 128),
+        cost(1e6, 4e6),
+    )(got_mirrored.reshape(-1, 128), natural)
+    other = lax.ppermute(symmetric, "pool", swap)
+    kept, other = symmetric[..., :half], other[..., :half]
+    response_density = jnp.where(
+        pool == 0,
+        jnp.concatenate((kept, other), axis=2),
+        jnp.concatenate((other, kept), axis=2),
+    )
+    base = finish(base, back_tail, 1, 1, True)
+    base, response_density, back_main = lax.optimization_barrier(
+        (base, response_density, back_main)
+    )
+    base = finish(base, back_main, 1, 2, False)
+    return base, response_density
+
+
+class Both:
+    def __init__(self, *refs):
+        self.refs = refs
+
+    def __getitem__(self, index):
+        return self.refs[index[0]][index[1:]]
 
 
 def tables(length):
@@ -58,7 +562,7 @@
     return (real_sum, imag_sum)
 
 
-def body(orbitals, responses, energies, weights, potential, perturbation):
+def plain_body(orbitals, responses, energies, weights, potential, perturbation):
     length = orbitals.shape[-1]
     slab_rows = orbitals.shape[3]
     cosine_table, sine_table = tables(length)
@@ -137,6 +641,14 @@
     return (new_responses, total_sym / 8.0)
 
 
+def body(orbitals, responses, energies, weights, potential, perturbation):
+    slab, length = orbitals.shape[3], orbitals.shape[-1]
+    fits = slab % 4 == 0 and length == 192 and orbitals.shape[0] == 1 and orbitals.shape[1] == 2
+    return (packed_body if fits else plain_body)(
+        orbitals, responses, energies, weights, potential, perturbation
+    )
+
+
 def solution(mesh):
     placed = (
         P("pool", None, None, "pw", None, None),

time: 1630 us -> 611 us (0.37); the launches traced: 1610 us -> 610 us
  matrix products: 581 us -> 0 us
  local copies, waits for them, and re-layouts: 355 us -> 8.65 us
  waiting for transfers between devices: 536 us -> 302 us
  Pallas kernels: 0 us -> 211 us
  other arithmetic: 69 us -> 9.11 us
    dot_general x44 -> x0, matrix products: 581 us -> none  [the longest x36 321 us: apply_table(): jnp.tensordot(values, table_in, axes=((along_axis,), (0,)), precision=lax...]
    pallas_call x0 -> x16, Pallas kernels: none -> 211 us  [the longest x4 74.7 us: to_half(): call(to_half_kernel, 'to_half', pairs, [pl.BlockSpec((1, 1, 2, 2, length,...]
    all_to_all x5 -> x8, waiting for transfers between devices: 468 us -> 258 us  [exchange(): return lax.all_to_all(values, 'pw', split_axis=0, concat_axis=0, tiled=True)]
    unnamed x103 -> x20, local copies, waits for them, and re-layouts: 144 us -> 7.79 us
    another operation x7 -> x0, local copies, waits for them, and re-layouts: 79.9 us -> none  [the longest x3 46.5 us: transform(): jnp.stack((real_cos - phase_sign * imag_sin, phase_sign * real_sin + imag...]
    psum x1 -> x0, waiting for transfers between devices: 68.3 us -> none  [body(): summed = lax.psum(partial_value, 'pool')]
    slice x9 -> x0, local copies, waits for them, and re-layouts: 57.1 us -> none  [the longest x6 29.7 us: negated(): return jnp.roll(jnp.flip(values, along_axis), 1, along_axis)]
    ppermute x0 -> x2, waiting for transfers between devices: none -> 44.6 us  [the longest x1 26 us: packed_body(): summed = jnp.where(used, kept + lax.ppermute(given, 'pool', swap), riding)]
  transfers between devices with their start and end apart: 6 -> 10, of which waited for: 5 -> 10; matrix products, arithmetic and copies ran while one was open for 18% -> 2% of each run, Pallas kernels for 0% -> 30%
where the time goes in v1:
time: 611 us; the launch traced here: 610 us
  waiting for transfers between devices  302 us (49%)
  Pallas kernels  211 us (35%)
  starting transfers between devices  44.4 us (7%)
  blocking collectives  32.7 us (5%)
  other arithmetic  9.11 us (1%)
  local copies, waits for them, and re-layouts  8.65 us (1%)
    all_to_all x8, waiting for transfers between devices, exchange(): return lax.all_to_all(values, 'pw', split_axis=0, concat_axis=0, tiled=True)  258 us
    pallas_call x4, Pallas kernels, to_half(): call(to_half_kernel, 'to_half', pairs, [pl.BlockSpec((1, 1, 2, 2, length,...  74.7 us
    all_to_all x8, starting transfers between devices, exchange(): return lax.all_to_all(values, 'pw', split_axis=0, concat_axis=0, tiled=True)  42 us
    all_to_all x1, blocking collectives, exchange(): return lax.all_to_all(values, 'pw', split_axis=0, concat_axis=0, tiled=True)  32.7 us
    pallas_call x4, Pallas kernels, finish(): call(functools.partial(finish_kernel, slab, chunks, tail), 'finish', pair...  31.7 us
    pallas_call x1, Pallas kernels, apply_first(): call(kernel, 'apply_first', pairs, [scalars(), whole(), space_spec, space...  27.8 us
    pallas_call x1, Pallas kernels, apply_last(): call(kernel, 'apply_last', pairs, [scalars(), whole(), space_spec, space_...  27.6 us
    ppermute x1, waiting for transfers between devices, packed_body(): summed = jnp.where(used, kept + lax.ppermute(given, 'pool', swap), riding)  26 us
  transfers between devices with their start and end apart: 10, of which 10 were waited for; matrix products, arithmetic and copies ran while one was open for 2% of the time, Pallas kernels for 30%

profile of v1, /device:TPU:13, one launch (start us, length us, event | category | flops | bytes accessed | tf_op | source)
XLA Modules:
  0.0 609.9 jit_solution(9336785621031005272)
XLA Ops:
  0.6 18.7 %to_half.7 = f32[16,6,3,24,128]{4,3,2,1,0:T(8,128)} custom-call(f32[1,2,2,12,192,192]{5,4,3,2,1,0:T(8,128)} %orbitals.3, bf16[2,192,256]{2,1,0:T(8,128)(2,1)} %constant.32.clone.cosine.tables_and_outs_1_, bf16[2,192,256]{2,1,0:T(8,128)(2,1)} %constant.33.clone.sine.tables_and_outs_2_, bf16[2,384,384]{2,1,0:T(8,128)(2,1)} %constant.34.clone.send), custom_call_target="tpu_custom_call" | custom-call | flops 8153726976 | bytes 7077888 | tf_op jit(solution)/shard_map/to_half/pallas_call | solution.py:327
  19.3 6.6 %all-to-all-start = ((f32[16,432,128]{2,1,0:T(8,128)}), f32[16,432,128]{2,1,0:T(8,128)S(1)}, u32[]{:S(2)}, u32[]{:S(2)}) async-start(f32[16,432,128]{2,1,0:T(8,128)} %bitcast.35), calls=%async_computation | async-start | bytes 7077888 | tf_op jit(solution)/shard_map/all_to_all | solution.py:324
  25.8 18.7 %to_half.6 = f32[16,6,3,24,128]{4,3,2,1,0:T(8,128)} custom-call(f32[1,2,2,12,192,192]{5,4,3,2,1,0:T(8,128)} %orbitals.3, bf16[2,192,256]{2,1,0:T(8,128)(2,1)} %constant.32.clone.cosine.tables_and_outs_1_, bf16[2,192,256]{2,1,0:T(8,128)(2,1)} %constant.33.clone.sine.tables_and_outs_2_, bf16[2,384,384]{2,1,0:T(8,128)(2,1)} %constant.34.clone.send), custom_call_target="tpu_custom_call" | custom-call | flops 8153726976 | bytes 7077888 | tf_op jit(solution)/shard_map/to_half/pallas_call | solution.py:327
  44.5 59.6 %all-to-all-done = f32[16,432,128]{2,1,0:T(8,128)S(1)} async-done(((f32[16,432,128]{2,1,0:T(8,128)}), f32[16,432,128]{2,1,0:T(8,128)S(1)}, u32[]{:S(2)}, u32[]{:S(2)}) %all-to-all-start) | async-done | bytes 3538976 | tf_op jit(solution)/shard_map/all_to_all | solution.py:324
  104.2 0.0 copy-start.4
  104.2 1.7 copy-done.4
  105.9 4.9 all-to-all-start.1
  110.8 18.6 %to_half.5 = f32[16,6,3,24,128]{4,3,2,1,0:T(8,128)} custom-call(f32[1,2,2,12,192,192]{5,4,3,2,1,0:T(8,128)} %responses.3, bf16[2,192,256]{2,1,0:T(8,128)(2,1)} %constant.32.clone.cosine.tables_and_outs_1_, bf16[2,192,256]{2,1,0:T(8,128)(2,1)} %constant.33.clone.sine.tables_and_outs_2_, bf16[2,384,384]{2,1,0:T(8,128)(2,1)} %constant.34.clone.send), custom_call_target="tpu_custom_call" | custom-call | flops 8153726976 | bytes 7077888 | tf_op jit(solution)/shard_map/to_half/pallas_call | solution.py:327
  129.5 59.8 %all-to-all-done.1 = f32[16,432,128]{2,1,0:T(8,128)} async-done(((f32[16,432,128]{2,1,0:T(8,128)}), f32[16,432,128]{2,1,0:T(8,128)}, u32[]{:S(2)}, u32[]{:S(2)}) %all-to-all-start.1) | async-done | bytes 3538976 | tf_op jit(solution)/shard_map/all_to_all | solution.py:324
  189.2 4.9 all-to-all-start.2
  194.1 10.1 %inner.1 = f32[2,2,2,8,192]{4,3,2,1,0:T(8,128)} custom-call(s32[1]{0:T(128)} %bitcast.me, f32[1,2]{1,0:T(1,128)} %energies.3, f32[1,2,2,12,192,192]{5,4,3,2,1,0:T(8,128)} %orbitals.3, f32[1,2,2,12,192,192]{5,4,3,2,1,0:T(8,128)} %responses.3), custom_call_target="tpu_custom_call" | custom-call | flops 113246208 | bytes 14155776 | tf_op jit(solution)/shard_map/inner/pallas_call | solution.py:433
  204.3 18.7 %to_half.4 = f32[16,6,3,24,128]{4,3,2,1,0:T(8,128)} custom-call(f32[1,2,2,12,192,192]{5,4,3,2,1,0:T(8,128)} %responses.3, bf16[2,192,256]{2,1,0:T(8,128)(2,1)} %constant.32.clone.cosine.tables_and_outs_1_, bf16[2,192,256]{2,1,0:T(8,128)(2,1)} %constant.33.clone.sine.tables_and_outs_2_, bf16[2,384,384]{2,1,0:T(8,128)(2,1)} %constant.34.clone.send), custom_call_target="tpu_custom_call" | custom-call | flops 8153726976 | bytes 7077888 | tf_op jit(solution)/shard_map/to_half/pallas_call | solution.py:327
  223.0 49.5 %all-to-all-done.2 = f32[16,432,128]{2,1,0:T(8,128)S(1)} async-done(((f32[16,432,128]{2,1,0:T(8,128)}), f32[16,432,128]{2,1,0:T(8,128)S(1)}, u32[]{:S(2)}, u32[]{:S(2)}) %all-to-all-start.2) | async-done | bytes 3538976 | tf_op jit(solution)/shard_map/all_to_all | solution.py:324
  272.5 0.0 copy-start.6
  272.5 1.8 copy-done.6
  274.3 4.9 all-to-all-start.3
  279.8 8.2 %to_space.2.first = f32[12,384,192]{2,1,0:T(8,128)} custom-call(f32[6912,128]{1,0:T(8,128)} %bitcast.29, bf16[2,384,384]{2,1,0:T(8,128)(2,1)} %constant.35.clone.receive.tables_and_outs_0_), custom_call_target="tpu_custom_call" | custom-call | flops 4076863488 | bytes 7077888 | tf_op jit(solution)/shard_map/to_space/pallas_call | solution.py:343
  288.1 8.3 %to_space.3.second = f32[12,384,192]{2,1,0:T(8,128)} custom-call(f32[6912,128]{1,0:T(8,128)} %bitcast.7.got, bf16[2,384,384]{2,1,0:T(8,128)(2,1)} %constant.35.clone.receive.tables_and_outs_0_), custom_call_target="tpu_custom_call" | custom-call | flops 4076863488 | bytes 7077888 | tf_op jit(solution)/shard_map/to_space/pallas_call | solution.py:343
  296.3 27.8 %apply_first.1 = (f32[16,6,3,24,128]{4,3,2,1,0:T(8,128)}, f32[2,2,8,192]{3,2,1,0:T(8,128)}, f32[12,192,192]{2,1,0:T(8,128)}) custom-call(f32[1]{0:T(128)S(6)} %copy.28.weights, f32[6912,128]{1,0:T(8,128)} %bitcast.31, f32[12,384,192]{2,1,0:T(8,128)} %to_space.2.first, f32[12,384,192]{2,1,0:T(8,128)} %to_space.3.second, f32[12,192,192]{2,1,0:T(8,128)} %bitcast.42, ...), custom_call_target="tpu_custom_call" | custom-call | flops 12230590464 | bytes 17694720 | tf_op jit(solution)/shard_map/apply_first/pallas_call | solution.py:374
  324.1 33.4 %all-to-all-done.3 = f32[16,432,128]{2,1,0:T(8,128)S(1)} async-done(((f32[16,432,128]{2,1,0:T(8,128)}), f32[16,432,128]{2,1,0:T(8,128)S(1)}, u32[]{:S(2)}, u32[]{:S(2)}) %all-to-all-start.3) | async-done | bytes 3538976 | tf_op jit(solution)/shard_map/all_to_all | solution.py:324
  357.5 0.0 copy-start.5
  357.5 1.8 copy-done.5
  359.3 4.9 all-to-all-start.4
  364.2 27.6 %apply_last.1 = (f32[16,6,2,24,128]{4,3,2,1,0:T(8,128)}, f32[16,6,24,128]{3,2,1,0:T(8,128)}, f32[2,2,8,192]{3,2,1,0:T(8,128)}, f32[16,144,128]{2,1,0:T(8,128)}, f32[16,144,128]{2,1,0:T(8,128)}) custom-call(f32[1]{0:T(128)S(6)} %copy.28.weights, f32[6912,128]{1,0:T(8,128)} %bitcast.30, f32[12,384,192]{2,1,0:T(8,128)} %to_space.2.first, ...), custom_call_target="tpu_custom_call" | custom-call | flops 12230590464 | bytes 17694720 | tf_op jit(solution)/shard_map/apply_last/pallas_call | solution.py:395
  391.8 0.0 copy-start.7
  391.8 0.0 copy-start.8
  391.8 0.0 copy-start.9
  391.8 2.4 broadcast_select_fusion
  394.2 1.2 collective-permute-start
  395.5 0.0 copy-done.7
  395.5 0.0 copy-done.8
  395.5 0.0 copy-done.9
  395.5 0.1 fusion
  395.6 0.1 copy.22
  395.7 0.1 reshape.74
  395.8 26.0 %collective-permute-done = f32[16,144,128]{2,1,0:T(8,128)} collective-permute-done((f32[16,144,128]{2,1,0:T(8,128)}, f32[16,144,128]{2,1,0:T(8,128)}, u32[]{:S(2)}, u32[]{:S(2)}) %collective-permute-start) | collective-permute-done | bytes 1179680 | tf_op jit(solution)/shard_map/ppermute | solution.py:456
  421.8 2.8 add_select_fusion
  424.6 17.9 %all-to-all-done.4 = f32[16,432,128]{2,1,0:T(8,128)S(1)} async-done(((f32[16,432,128]{2,1,0:T(8,128)}), f32[16,432,128]{2,1,0:T(8,128)S(1)}, u32[]{:S(2)}, u32[]{:S(2)}) %all-to-all-start.4) | async-done | bytes 3538976 | tf_op jit(solution)/shard_map/all_to_all | solution.py:324
  442.5 0.0 copy-start
  442.5 32.7 %all_to_all.45 = f32[16,144,128]{2,1,0:T(8,128)} all-to-all(f32[16,144,128]{2,1,0:T(8,128)} %add_select_fusion), channel_id=1, replica_groups=mesh['pool'=2,'pw'=16] {'pw'}, dimensions={0} | all-to-all | bytes 2359296 | tf_op jit(solution)/shard_map/all_to_all | solution.py:324
  475.1 0.0 copy-done
  475.1 6.1 all-to-all-start.6
  481.2 1.0 slice_reduce_fusion
  482.3 0.7 reshape.78.inner
  482.9 12.3 %direct.1.base = f32[1,2,2,12,192,192]{5,4,3,2,1,0:T(8,128)} custom-call(s32[1]{0:T(128)} %bitcast.me, f32[1,2]{1,0:T(1,128)} %energies.3, f32[2,2,2]{2,1,0:T(2,128)} %reshape.78.inner, f32[1,2,2,12,192,192]{5,4,3,2,1,0:T(8,128)} %orbitals.3, f32[1,2,2,12,192,192]{5,4,3,2,1,0:T(8,128)} %responses.3), custom_call_target="tpu_custom_call" | custom-call | flops 113246208 | bytes 21233664 | tf_op jit(solution)/shard_map/direct/pallas_call | solution.py:460
  495.2 5.8 mirror.2
  501.0 8.1 %all-to-all-done.6 = f32[16,144,128]{2,1,0:T(8,128)} async-done(((f32[16,144,128]{2,1,0:T(8,128)}), f32[16,144,128]{2,1,0:T(8,128)}, u32[]{:S(2)}, u32[]{:S(2)}) %all-to-all-start.6) | async-done | bytes 1179680 | tf_op jit(solution)/shard_map/all_to_all | solution.py:324
  509.1 4.8 all-to-all-start.7
  513.9 8.0 %finish.4.base = f32[1,2,2,12,192,192]{5,4,3,2,1,0:T(8,128)} custom-call(s32[1]{0:T(128)} %bitcast.me, f32[6912,128]{1,0:T(8,128)} %bitcast.23, bf16[2,384,384]{2,1,0:T(8,128)(2,1)} %constant.37.clone.receive, f32[1,2,2,12,192,192]{5,4,3,2,1,0:T(8,128)} %direct.1.base), custom_call_target="tpu_custom_call", output_to_operand_aliasing={{}: (3, {})} | custom-call | flops 4076863488 | bytes 7077888 | tf_op jit(solution)/shard_map/finish/pallas_call | solution.py:417
  521.9 8.2 %finish.5.base = f32[1,2,2,12,192,192]{5,4,3,2,1,0:T(8,128)} custom-call(s32[1]{0:T(128)} %bitcast.me, f32[6912,128]{1,0:T(8,128)} %bitcast.24, bf16[2,384,384]{2,1,0:T(8,128)(2,1)} %constant.37.clone.receive, f32[1,2,2,12,192,192]{5,4,3,2,1,0:T(8,128)} %finish.4.base), custom_call_target="tpu_custom_call", output_to_operand_aliasing={{}: (3, {})} | custom-call | flops 4076863488 | bytes 7077888 | tf_op jit(solution)/shard_map/finish/pallas_call | solution.py:417
  530.1 11.6 %all-to-all-done.7 = f32[16,144,128]{2,1,0:T(8,128)S(1)} async-done(((f32[16,144,128]{2,1,0:T(8,128)}), f32[16,144,128]{2,1,0:T(8,128)S(1)}, u32[]{:S(2)}, u32[]{:S(2)}) %all-to-all-start.7) | async-done | bytes 1179680 | tf_op jit(solution)/shard_map/all_to_all | solution.py:324
  541.7 0.0 copy-start.3
  541.7 1.0 copy-done.3
  542.7 4.9 all-to-all-start.8
  547.6 4.9 swap.1
  552.5 1.2 collective-permute-start.1
  553.7 0.0 copy-start.2
  553.7 7.6 %finish.6.base = f32[1,2,2,12,192,192]{5,4,3,2,1,0:T(8,128)} custom-call(s32[1]{0:T(128)} %bitcast.me, f32[2304,128]{1,0:T(8,128)} %bitcast.15.got, bf16[2,384,384]{2,1,0:T(8,128)(2,1)} %constant.37.clone.receive, f32[1,2,2,12,192,192]{5,4,3,2,1,0:T(8,128)} %finish.5.base), custom_call_target="tpu_custom_call", output_to_operand_aliasing={{}: (3, {})} | custom-call | flops 4076863488 | bytes 7077888 | tf_op jit(solution)/shard_map/finish/pallas_call | solution.py:417
  561.3 18.6 %collective-permute-done.1 = f32[12,192,128]{2,1,0:T(8,128)S(1)} collective-permute-done((f32[12,192,128]{2,1,0:T(8,128)}, f32[12,192,128]{2,1,0:T(8,128)S(1)}, u32[]{:S(2)}, u32[]{:S(2)}) %collective-permute-start.1) | collective-permute-done | bytes 1179680 | tf_op jit(solution)/shard_map/ppermute | solution.py:492
  579.9 0.0 copy-done.2
  579.9 2.7 maximum_select_fusion
  582.6 18.1 %all-to-all-done.8 = f32[16,288,128]{2,1,0:T(8,128)S(1)} async-done(((f32[16,288,128]{2,1,0:T(8,128)}), f32[16,288,128]{2,1,0:T(8,128)S(1)}, u32[]{:S(2)}, u32[]{:S(2)}) %all-to-all-start.8) | async-done | bytes 2359328 | tf_op jit(solution)/shard_map/all_to_all | solution.py:324
  600.6 1.4 copy-done.1
  602.1 7.9 %finish.7 = f32[1,2,2,12,192,192]{5,4,3,2,1,0:T(8,128)} custom-call(s32[1]{0:T(128)} %bitcast.me, f32[4608,128]{1,0:T(8,128)} %bitcast.25, bf16[2,384,384]{2,1,0:T(8,128)(2,1)} %constant.37.clone.receive, f32[1,2,2,12,192,192]{5,4,3,2,1,0:T(8,128)} %finish.6.base), custom_call_target="tpu_custom_call", output_to_operand_aliasing={{}: (3, {})} | custom-call | flops 4076863488 | bytes 7077888 | tf_op jit(solution)/shard_map/finish/pallas_call | solution.py:417
  (3 shorter events, 0.0 us)
Async XLA Ops:
  19.3 84.9 %all-to-all-start = ((f32[16,432,128]{2,1,0:T(8,128)}), f32[16,432,128]{2,1,0:T(8,128)S(1)}, u32[]{:S(2)}, u32[]{:S(2)}) async-start(f32[16,432,128]{2,1,0:T(8,128)} %bitcast.35), calls=%async_computation | async-start | bytes 7077888 | tf_op jit(solution)/shard_map/all_to_all | solution.py:324
  104.2 1.8 copy-start.4
  105.9 83.3 %all-to-all-start.1 = ((f32[16,432,128]{2,1,0:T(8,128)}), f32[16,432,128]{2,1,0:T(8,128)}, u32[]{:S(2)}, u32[]{:S(2)}) async-start(f32[16,432,128]{2,1,0:T(8,128)} %bitcast.34), calls=%async_computation.1 | async-start | bytes 7077888 | tf_op jit(solution)/shard_map/all_to_all | solution.py:324
  189.2 83.2 %all-to-all-start.2 = ((f32[16,432,128]{2,1,0:T(8,128)}), f32[16,432,128]{2,1,0:T(8,128)S(1)}, u32[]{:S(2)}, u32[]{:S(2)}) async-start(f32[16,432,128]{2,1,0:T(8,128)} %bitcast.33), calls=%async_computation.2 | async-start | bytes 7077888 | tf_op jit(solution)/shard_map/all_to_all | solution.py:324
  272.5 1.8 copy-start.6
  274.3 83.2 %all-to-all-start.3 = ((f32[16,432,128]{2,1,0:T(8,128)}), f32[16,432,128]{2,1,0:T(8,128)S(1)}, u32[]{:S(2)}, u32[]{:S(2)}) async-start(f32[16,432,128]{2,1,0:T(8,128)} %bitcast.32), calls=%async_computation.3 | async-start | bytes 7077888 | tf_op jit(solution)/shard_map/all_to_all | solution.py:324
  357.5 1.8 copy-start.5
  359.3 83.2 %all-to-all-start.4 = ((f32[16,432,128]{2,1,0:T(8,128)}), f32[16,432,128]{2,1,0:T(8,128)S(1)}, u32[]{:S(2)}, u32[]{:S(2)}) async-start(f32[16,432,128]{2,1,0:T(8,128)} %bitcast.28), calls=%async_computation.4 | async-start | bytes 7077888 | tf_op jit(solution)/shard_map/all_to_all | solution.py:324
  391.8 3.7 copy-start.7
  391.8 3.7 copy-start.8
  391.8 3.7 copy-start.9
  394.2 27.5 %collective-permute-start = (f32[16,144,128]{2,1,0:T(8,128)}, f32[16,144,128]{2,1,0:T(8,128)}, u32[]{:S(2)}, u32[]{:S(2)}) collective-permute-start(f32[16,144,128]{2,1,0:T(8,128)} %broadcast_select_fusion), channel_id=1, source_target_pairs={{0,16},{16,0},{1,17},{17,1},{2,18},{18,2},{3,19},{19,3},{4,20},{20... | collective-permute-start | bytes 3538952 | tf_op jit(solution)/shard_map/ppermute | solution.py:456
  442.5 32.7 %copy-start = (f32[16,432,128]{2,1,0:T(8,128)}, f32[16,432,128]{2,1,0:T(8,128)S(1)}, u32[]{:S(2)}) copy-start(f32[16,432,128]{2,1,0:T(8,128)S(1)} %all-to-all-done.4) | copy-start | bytes 10616836
  475.1 34.0 %all-to-all-start.6 = ((f32[16,144,128]{2,1,0:T(8,128)}), f32[16,144,128]{2,1,0:T(8,128)}, u32[]{:S(2)}, u32[]{:S(2)}) async-start(f32[16,144,128]{2,1,0:T(8,128)} %bitcast.39), calls=%async_computation.6 | async-start | bytes 2359296 | tf_op jit(solution)/shard_map/all_to_all | solution.py:324
  509.1 32.6 %all-to-all-start.7 = ((f32[16,144,128]{2,1,0:T(8,128)}), f32[16,144,128]{2,1,0:T(8,128)S(1)}, u32[]{:S(2)}, u32[]{:S(2)}) async-start(f32[16,144,128]{2,1,0:T(8,128)} %get-tuple-element.37), calls=%async_computation.7 | async-start | bytes 2359296 | tf_op jit(solution)/shard_map/all_to_all | solution.py:324
  541.7 1.0 copy-start.3
  542.7 57.9 %all-to-all-start.8 = ((f32[16,288,128]{2,1,0:T(8,128)}), f32[16,288,128]{2,1,0:T(8,128)S(1)}, u32[]{:S(2)}, u32[]{:S(2)}) async-start(f32[16,288,128]{2,1,0:T(8,128)} %bitcast.36), calls=%async_computation.8 | async-start | bytes 4718592 | tf_op jit(solution)/shard_map/all_to_all | solution.py:324
  552.5 27.4 %collective-permute-start.1 = (f32[12,192,128]{2,1,0:T(8,128)}, f32[12,192,128]{2,1,0:T(8,128)S(1)}, u32[]{:S(2)}, u32[]{:S(2)}) collective-permute-start(f32[12,192,128]{2,1,0:T(8,128)} %swap.1), channel_id=1, source_target_pairs={{0,16},{16,0},{1,17},{17,1},{2,18},{18,2},{3,19},{19,3},{4,20},{20... | collective-permute-start | bytes 3538952 | tf_op jit(solution)/shard_map/ppermute | solution.py:492
  553.7 26.2 %copy-start.2 = (f32[12,192,128]{2,1,0:T(8,128)S(1)}, f32[12,192,128]{2,1,0:T(8,128)}, u32[]{:S(2)}) copy-start(f32[12,192,128]{2,1,0:T(8,128)} %swap.1) | copy-start | bytes 3538948
  600.6 1.4 copy-start.1

commit v2 on v1

--- a/solution.py
+++ b/solution.py
@@ -11,13 +11,18 @@
 from jax.sharding import PartitionSpec as P
 
 RECIPROCAL_SQUARE = 0.023428
-VMEM_BYTES = 56 * 1024 * 1024
+VMEM_BYTES = 62 * 1024 * 1024
 
 
 def split_table(table):
     high = table.astype(ml_dtypes.bfloat16)
     low = (table - high.astype(np.float64)).astype(ml_dtypes.bfloat16)
     return np.stack((high, low))
+
+
+def long_table(table):
+    high, low = split_table(table)
+    return np.concatenate((high, high, low), axis=1)
 
 
 @functools.cache
@@ -31,19 +36,33 @@
     inverse = np.block([[cosine, -sine], [sine, cosine]])
     forward = np.block([[cosine, sine], [-sine, cosine]])
     sent = np.arange(2 * length).reshape(2, members, slab).transpose(1, 0, 2).reshape(-1)
-    got = np.arange(2 * length).reshape(2, members, slab // 2, 2).transpose(0, 3, 1, 2).reshape(-1)
+    got = np.arange(2 * length).reshape(2, members, slab // 2, 2).transpose(3, 0, 1, 2)
+    got = got.reshape(2, -1)
+    first = np.arange(2 * length).reshape(2, 2, length // 2)[:, 0].reshape(-1)
+    parity = np.arange(2 * length).reshape(length, 2).T
     mirror = np.eye(length) + np.eye(length)[(-index) % length]
     both = np.zeros((members, 2, slab, 2, length))
     for which in range(2):
         both[:, which, :, which, :] = mirror.reshape(members, slab, length)
+    both = both.reshape(2 * length, 2, length)
+    alone = np.pad(mirror.reshape(members, slab, length), ((0, 0), (0, 4), (0, 0)))
+    alone = alone.reshape(-1, length)
+    loose = index.reshape(members, slab).T.reshape(-1)
     return {
         "cosine": split_table(np.pad(cosine, pad)),
-        "sine": split_table(np.pad(sine, pad)),
-        "inverse_send": split_table(inverse[sent]),
-        "inverse_receive": split_table(inverse[:, got]),
-        "forward_send": split_table(forward[sent]),
-        "forward_receive": split_table(forward[:, got]),
-        "mirror_pair": both.reshape(2 * length, 2 * length).astype(ml_dtypes.bfloat16),
+        "mixed": np.stack(
+            [split_table(np.pad(sine + sign * cosine, pad)) for sign in (-1.0, 1.0)]
+        ),
+        "inverse_send": np.stack([long_table(inverse[sent[:length]][:, one]) for one in parity]),
+        "inverse_receive": np.stack([long_table(inverse[first][:, one]) for one in got]),
+        "forward_send": long_table(forward[sent]),
+        "forward_receive": np.stack([long_table(forward[first][:, one]) for one in got]),
+        "pair": both.reshape(2 * length, -1).astype(ml_dtypes.bfloat16),
+        "alone": alone.astype(ml_dtypes.bfloat16),
+        "loose_pair": both[:, :, loose].reshape(2 * length, -1).astype(ml_dtypes.bfloat16),
+        "loose_alone": alone[:, loose].astype(ml_dtypes.bfloat16),
+        "loose_mirror": mirror[:, loose].astype(ml_dtypes.bfloat16),
+        "loose_order": np.eye(length)[:, loose].astype(ml_dtypes.bfloat16),
     }
 
 
@@ -65,7 +84,27 @@
 
 def dot_left(table, values):
     high, low = halves(values)
-    return dot(table[0], high) + (dot(table[0], low) + dot(table[1], high))
+    return dot(table, jnp.concatenate((high, low, high), axis=0))
+
+
+def turn_lanes(real, imag, cosine, mixed, sign):
+    common = dot_right(real + imag, cosine)
+    if sign > 0:
+        return common - dot_right(imag, mixed.at[1]), common + dot_right(real, mixed.at[0])
+    return common + dot_right(imag, mixed.at[0]), common - dot_right(real, mixed.at[1])
+
+
+def half_lengths(even, odd):
+    return even + odd, even - odd
+
+
+def dot_receive(table, found):
+    first, second = half_lengths(*(dot_left(table[one], found[one]) for one in range(2)))
+    mid = first.shape[0] // 2
+    return (
+        jnp.concatenate((first[:mid], second[:mid]), axis=0),
+        jnp.concatenate((first[mid:], second[mid:]), axis=0),
+    )
 
 
 def dot_mirror(table, values):
@@ -78,50 +117,70 @@
     return first + pltpu.roll(second, 64, 1)
 
 
-def to_half_kernel(field, cosine, sine, send, out):
+def to_half_kernel(field, cosine, mixed, send, out, turned):
     pair, length = field.shape[3], field.shape[4]
-    members, rows = out.shape[0], out.shape[3]
-    values = field[...].reshape(2 * pair * length, length)
-    by_cos = dot_right(values, cosine)
-    by_sin = dot_right(values, sine)
-    mid = pair * length
-    real = by_cos[:mid] - by_sin[mid:]
-    imag = by_sin[:mid] + by_cos[mid:]
+    members, rows = out.shape[0], out.shape[-2]
+    mid = members // 2
+    out = out.at[:, 0, 0] if len(out.shape) == 6 else out.at[:, 0]
+    parts = [field[0, 0, part].reshape(pair * length, length) for part in range(2)]
+    parts = turn_lanes(*parts, cosine, mixed, 1)
+    for part in range(2):
+        turned[part, 0] = parts[part][:, :128]
+        turned[part, 1] = parts[part][:, 128:]
     tails = []
     for one in range(pair):
-        part = slice(one * length, (one + 1) * length)
-        done = dot_left(send, jnp.concatenate((real[part], imag[part]), axis=0))
-        out[:, 0, one] = done[:, :128].reshape(members, rows, 128)
-        tails.append(done[:, 128:])
-    out[:, 0, 2] = merge_tails(*tails).reshape(members, rows, 128)
+        found = []
+        for parity in range(2):
+            rows_of = pl.ds(one * length + parity, length // 2, stride=2)
+            found.append(
+                jnp.concatenate(
+                    [
+                        jnp.concatenate((turned[part, 0, rows_of], turned[part, 1, rows_of]), axis=1)
+                        for part in range(2)
+                    ],
+                    axis=0,
+                )
+            )
+        done = half_lengths(*(dot_left(send[parity], found[parity]) for parity in range(2)))
+        for half in range(2):
+            to = slice(half * mid, (half + 1) * mid)
+            out[to, one] = done[half][:, :128].reshape(mid, rows, 128)
+        tails.append([piece[:, 128:] for piece in done])
+    for half in range(2):
+        to = slice(half * mid, (half + 1) * mid)
+        out[to, 2] = merge_tails(tails[0][half], tails[1][half]).reshape(mid, rows, 128)
 
 
 def received(ref, start, stride, count):
     return ref[pl.ds(start, count, stride=stride), :]
 
 
-def plane(got, chunks, place, slab, count, with_main, with_tail):
-    stride = chunks * 2 * slab
-    found = []
+def plane(got, start, stride, place, slab, with_main, with_tail):
+    count = got.shape[0] // stride
+    found = [[], []]
     for part in range(2):
-        row = part * slab + place
+        row = start + part * slab + place
+        mains, tails = [None, None], [None, None]
         if with_main:
             mains = [received(got, one * 2 * slab + row, stride, count) for one in range(2)]
+            row = row + 4 * slab
         if with_tail:
-            tail = received(got, (chunks - 1) * 2 * slab + row, stride, count)
+            tail = received(got, row, stride, count)
             tails = [tail, pltpu.roll(tail, 64, 1)]
         for one in range(2):
-            pieces = ([mains[one]] if with_main else []) + ([tails[one]] if with_tail else [])
-            found.append(jnp.concatenate(pieces, axis=1) if len(pieces) > 1 else pieces[0])
-    return jnp.concatenate(found, axis=0)
-
-
-def to_space_kernel(slab, got, receive, space):
-    count = got.shape[0] // (6 * slab)
+            pieces = [piece for piece in (mains[one], tails[one]) if piece is not None]
+            found[one].append(jnp.concatenate(pieces, axis=1) if len(pieces) > 1 else pieces[0])
+    return [jnp.concatenate(one, axis=0) for one in found]
+
+
+def to_space_kernel(slab, start, stride, got, receive, space):
+    length = space.shape[2]
     for one in range(2):
         place = 2 * pl.program_id(0) + one
-        values = plane(got, 3, place, slab, count, True, True)
-        space[one] = dot_left(receive, values)[:, : space.shape[2]]
+        values = plane(got, start, stride, place, slab, True, True)
+        real, imag = dot_receive(receive, values)
+        space[one, :length] = real[:, :length]
+        space[one, length:] = imag[:, :length]
 
 
 def folded(values):
@@ -129,12 +188,11 @@
 
 
 def apply_kernel(
-    slab, band, weights, got, spaces, potential, perturbation, before,
-    receive, cosine, sine, send, mirror, out_main, out_tail, inner, density, *high_half
+    slab, start, stride, band, weights, got, spaces, potential, perturbation, before,
+    receive, cosine, mixed, send, out_main, out_tail, inner, density
 ):
     length = potential.shape[1]
     members, rows = out_main.shape[0], out_main.shape[3]
-    count = got.shape[0] // (6 * slab)
     step = pl.program_id(0)
     twice_weight = 2.0 * weights[0]
 
@@ -145,9 +203,8 @@
     tails = []
     sums = []
     for one in range(2):
-        values = plane(got, 3, 2 * step + one, slab, count, True, True)
-        response = dot_left(receive, values)[:, :length]
-        real, imag = response[:length], response[length:]
+        values = plane(got, start, stride, 2 * step + one, slab, True, True)
+        real, imag = (piece[:, :length] for piece in dot_receive(receive, values))
         own_real, own_imag = spaces[band, one, :length], spaces[band, one, length:]
         local = twice_weight * (own_real * real + own_imag * imag)
         if before is not None:
@@ -160,13 +217,8 @@
             left_real, left_imag = spaces[other, one, :length], spaces[other, one, length:]
             inner[0, other] += folded(left_real * real + left_imag * imag)
             inner[1, other] += folded(left_real * imag - left_imag * real)
-        both = jnp.concatenate((real, imag), axis=0)
-        by_cos = dot_right(both, cosine)
-        by_sin = dot_right(both, sine)
-        turned = jnp.concatenate(
-            (by_cos[:length] + by_sin[length:], by_cos[length:] - by_sin[:length]), axis=0
-        )
-        done = dot_left(send, turned)
+        turned = jnp.concatenate(turn_lanes(real, imag, cosine, mixed, -1), axis=0)
+        done = dot_left(send[...], turned)
         out_main[:, 0, one] = done[:, :128].reshape(members, rows, 128)
         tails.append(done[:, 128:])
     tail = merge_tails(*tails).reshape(members, rows, 128)
@@ -174,15 +226,72 @@
         out_main[:, 0, 2] = tail
     else:
         out_tail[:, 0] = tail
-    if not high_half:
-        for one in range(2):
-            density[one] = sums[one]
-        return
-    summed = dot_mirror(mirror[...], jnp.concatenate(sums, axis=0))
-    density[...] = summed[:, :128].reshape(density.shape)
-    half = length // 2
-    lanes = jnp.concatenate((summed[:, half:], summed[:, :half]), axis=1)[:, :128]
-    high_half[0][...] = lanes.reshape(density.shape)
+    for one in range(2):
+        density[one] = sums[one]
+
+
+def lanes_from(*pieces):
+    lane = lax.broadcasted_iota(jnp.int32, pieces[0][0].shape, 1)
+    width = 128 // len(pieces)
+    moved = [pltpu.roll(values, by, 1) if by else values for values, by in pieces]
+    made = moved[-1]
+    for place in range(len(pieces) - 2, -1, -1):
+        made = jnp.where(lane < (place + 1) * width, moved[place], made)
+    return made
+
+
+def pack(planes, pair, alone, out):
+    members = out.shape[0]
+    tails = []
+    for first in range(0, 12, 4):
+        one, two, three, four = (planes(first + by) for by in range(4))
+        mains = (lanes_from((one, 0), (two, 64)), lanes_from((three, 0), (four, 64)))
+        tails.append(lanes_from((one, 64), (two, 96), (three, 0), (four, 32)))
+        out[:, 6 * first : 6 * first + 24] = dot_mirror(
+            pair[...], jnp.concatenate(mains, axis=0)
+        ).reshape(members, 24, 128)
+    out[:, 72:96] = dot_mirror(pair[...], jnp.concatenate(tails[:2], axis=0)).reshape(
+        members, 24, 128
+    )
+    out[:, 96:112] = dot_mirror(alone[...], tails[2]).reshape(members, 16, 128)
+
+
+def unpack(got, place):
+    members = got.shape[0] // 112
+    found = []
+    for quad in range(3):
+        one = received(got, 24 * quad + place, 112, members)
+        two = received(got, 24 * quad + 12 + place, 112, members)
+        tail = received(got, 72 + 12 * quad + place, 112, members)
+        found += [
+            lanes_from((one, 0), (tail, 64)),
+            lanes_from((one, 64), (tail, 32)),
+            lanes_from((two, 0), (tail, 0)),
+            lanes_from((two, 64), (tail, 96)),
+        ]
+    return jnp.concatenate(found, axis=0)
+
+
+def pack_kernel(pool, density, pair, alone, kept, given):
+    length = density.shape[1]
+    own = pool[0] == 0
+
+    def halves_of(place):
+        main = density[place, :, :128]
+        tail = jnp.concatenate(
+            (density[place, :, 128:], jnp.zeros((length, 64), jnp.float32)), axis=1
+        )
+        return lanes_from((main, 0), (tail, 64)), lanes_from((main, 64), (tail, 32))
+
+    def one_half(which):
+        def planes(place):
+            low, high = halves_of(place)
+            return jnp.where(own, low, high) if which else jnp.where(own, high, low)
+
+        return planes
+
+    pack(one_half(True), pair, alone, kept)
+    pack(one_half(False), pair, alone, given)
 
 
 def frequencies(length, first, lanes, first_lane):
@@ -234,35 +343,28 @@
             out[0, band, 1, one] = responses[0, band, 1, one] - imag * inverse
 
 
-def finish_kernel(slab, chunks, tail, me, got, receive, base, out):
+def finish_kernel(slab, start, stride, tail, me, got, receive, base, out):
     length = base.shape[4]
-    count = got.shape[0] // (chunks * 2 * slab)
     for one in range(2):
         place = 2 * pl.program_id(0) + one
-        values = plane(got, chunks, place, slab, count, not tail, tail)
-        applied = dot_left(receive, values)
+        values = plane(got, start, stride, place, slab, not tail, tail)
+        applied = dot_receive(receive, values)
         kinetic = frequencies(length, me[0] * slab + place, 128, 128 if tail else 0)
         inverse = 1.0 / (1.0 + kinetic)
         for part in range(2):
-            piece = applied[part * length : (part + 1) * length]
-            out[0, 0, part, one] = base[0, 0, part, one] - piece * inverse
-
-
-def mirror_kernel(slab, got, mirror, single, out, natural):
-    length = natural.shape[1]
-    planes = [
-        received(got, 2 * pl.program_id(0) + one, slab, length) for one in range(2)
-    ]
-    out[...] = dot_mirror(mirror[...], jnp.concatenate(planes, axis=0)).reshape(out.shape)
-    for one in range(2):
-        natural[one] = dot_mirror(single[...], planes[one])
-
-
-def swap_kernel(slab, got, natural, out):
-    length = natural.shape[1]
-    for one in range(2):
-        swapped = received(got, 2 * pl.program_id(0) + one, slab, length)
-        out[one] = (natural[one] + swapped) * 0.125
+            out[0, 0, part, one] = base[0, 0, part, one] - applied[part] * inverse
+
+
+def mirror_kernel(got, single, pair, alone, out, natural, loose):
+    for place in range(12):
+        loose[place] = unpack(got, place)
+        natural[place] = dot_mirror(single[...], loose[place])
+    pack(lambda place: loose[place], pair, alone, out)
+
+
+def swap_kernel(got, order, natural, out):
+    for place in range(12):
+        out[place] = (natural[place] + dot_mirror(order[...], unpack(got, place))) * 0.125
 
 
 def cost(flops, moved):
@@ -277,7 +379,7 @@
     return pl.BlockSpec(memory_space=pltpu.SMEM)
 
 
-def call(kernel, name, grid, ins, outs, shapes, estimate, aliases=None):
+def call(kernel, name, grid, ins, outs, shapes, estimate, aliases=None, scratch=()):
     return pl.pallas_call(
         kernel,
         grid=(grid,),
@@ -289,6 +391,7 @@
         ),
         cost_estimate=estimate,
         input_output_aliases=aliases or {},
+        scratch_shapes=scratch,
         name=name,
     )
 
@@ -303,14 +406,9 @@
     members = length // slab
     pairs = slab // 2
     rows = 2 * slab
-    half = length // 2
     table = {key: jnp.asarray(value) for key, value in matrices(length, slab, members).items()}
-    single = jnp.asarray(
-        (np.eye(length) + np.eye(length)[(-np.arange(length)) % length]).astype(ml_dtypes.bfloat16)
-    )
     me = lax.axis_index("pw").astype(jnp.int32).reshape(1)
-    pool = lax.axis_index("pool")
-    flat = (members * pairs * 3 * rows, 128)
+    pool = lax.axis_index("pool").astype(jnp.int32).reshape(1)
     field_bytes = 4 * members * pairs * 3 * rows * 128
     stage_flops = 6 * 2 * 2 * length * length * length * slab * 2
 
@@ -323,9 +421,16 @@
             values, _ = lax.optimization_barrier((values, after))
         return lax.all_to_all(values, "pw", split_axis=0, concat_axis=0, tiled=True)
 
-    def to_half(field, band):
+    def to_half(field, band, into=None, slot=None):
+        def kernel(field, cosine, mixed, send, *rest):
+            to_half_kernel(field, cosine, mixed, send, *rest[-2:])
+
+        spec, shape = half_spec, half_shape
+        if slot is not None:
+            spec = pl.BlockSpec((members, 1, 1, 3, rows, 128), lambda p: (0, p, slot, 0, 0, 0))
+            shape = f32(members, pairs, 2, 3, rows, 128)
         return call(
-            to_half_kernel,
+            kernel,
             "to_half",
             pairs,
             [
@@ -333,22 +438,28 @@
                 whole(),
                 whole(),
                 whole(),
-            ],
-            half_spec,
-            half_shape,
+            ]
+            + ([] if into is None else [pl.BlockSpec(memory_space=pl.ANY)]),
+            spec,
+            shape,
             cost(2 * stage_flops, 2 * field_bytes),
-        )(field, table["cosine"], table["sine"], table["inverse_send"])
-
-    def to_space(got):
+            {} if into is None else {4: 0},
+            [pltpu.VMEM((2, 2, 2 * length, 128), jnp.float32)],
+        )(
+            field, table["cosine"], table["mixed"], table["inverse_send"],
+            *(() if into is None else (into,)),
+        )
+
+    def to_space(got, start, stride):
         return call(
-            functools.partial(to_space_kernel, slab),
+            functools.partial(to_space_kernel, slab, start, stride),
             "to_space",
             pairs,
             [whole(), whole()],
             pl.BlockSpec((2, 2 * length, length), lambda p: (p, 0, 0)),
             f32(slab, 2 * length, length),
             cost(stage_flops, 2 * field_bytes),
-        )(got.reshape(flat), table["inverse_receive"])
+        )(got.reshape(-1, 128), table["inverse_receive"])
 
     plane_spec = pl.BlockSpec((2, length, length), lambda p: (p, 0, 0))
     send_specs = [
@@ -359,16 +470,15 @@
         f32(members, pairs, 2, rows, 128),
         f32(members, pairs, rows, 128),
     ]
-    density_spec = pl.BlockSpec((members, 2 * slab, 128), lambda p: (0, p, 0))
-    density_shape = f32(members, slab * slab, 128)
+    block_shape = f32(members, 112, 128)
     inner_spec = pl.BlockSpec((2, 2, 8, length), lambda p: (0, 0, 0, 0))
 
     def apply_first(got, spaces, field, change):
         def kernel(weights, got, first, second, field, change, *tables_and_outs):
-            receive, cosine, sine, send, main, inner, density = tables_and_outs
+            receive, cosine, mixed, send, main, inner, density = tables_and_outs
             apply_kernel(
-                slab, 0, weights, got, Both(first, second), field, change, None,
-                receive, cosine, sine, send, None, main, None, inner, density,
+                slab, 3 * rows, 6 * rows, 0, weights, got, Both(first, second), field, change, None,
+                receive, cosine, mixed, send, main, None, inner, density,
             )
 
         return call(
@@ -380,42 +490,41 @@
             [half_shape, f32(2, 2, 8, length), f32(slab, length, length)],
             cost(3 * stage_flops, 5 * field_bytes),
         )(
-            weights, got.reshape(flat), *spaces, field, change,
-            table["inverse_receive"], table["cosine"], table["sine"], table["forward_send"],
+            weights, got.reshape(-1, 128), *spaces, field, change,
+            table["inverse_receive"], table["cosine"], table["mixed"], table["forward_send"],
         )
 
     def apply_last(got, spaces, field, change, before):
         def kernel(weights, got, first, second, field, change, before, *tables_and_outs):
-            receive, cosine, sine, send, mirror, main, tail, inner, low, high = tables_and_outs
+            receive, cosine, mixed, send, main, tail, inner, density = tables_and_outs
             apply_kernel(
-                slab, 1, weights, got, Both(first, second), field, change, before,
-                receive, cosine, sine, send, mirror, main, tail, inner, low, high,
+                slab, 0, 3 * rows, 1, weights, got, Both(first, second), field, change, before,
+                receive, cosine, mixed, send, main, tail, inner, density,
             )
 
         return call(
             kernel,
             "apply_last",
             pairs,
-            [scalars(), whole(), space_spec, space_spec] + [plane_spec] * 3 + [whole()] * 5,
-            send_specs + [inner_spec, density_spec, density_spec],
-            send_shapes + [f32(2, 2, 8, length), density_shape, density_shape],
+            [scalars(), whole(), space_spec, space_spec] + [plane_spec] * 3 + [whole()] * 4,
+            send_specs + [inner_spec, plane_spec],
+            send_shapes + [f32(2, 2, 8, length), f32(slab, length, length)],
             cost(3 * stage_flops, 5 * field_bytes),
         )(
-            weights, got.reshape(flat), *spaces, field, change, before,
-            table["inverse_receive"], table["cosine"], table["sine"], table["forward_send"],
-            table["mirror_pair"],
+            weights, got.reshape(-1, 128), *spaces, field, change, before,
+            table["inverse_receive"], table["cosine"], table["mixed"], table["forward_send"],
         )
 
     space_spec = pl.BlockSpec((2, 2 * length, length), lambda p: (p, 0, 0))
     bands_spec = pl.BlockSpec((1, 2, 2, 2, length, length), lambda p: (0, 0, 0, p, 0, 0))
 
-    def finish(base, got, band, chunks, tail):
+    def finish(base, got, band, start, stride, tail):
         lane_block = 1 if tail else 0
         one_spec = pl.BlockSpec(
             (1, 1, 2, 2, length, 128), lambda p: (0, band, 0, p, 0, lane_block)
         )
         return call(
-            functools.partial(finish_kernel, slab, chunks, tail),
+            functools.partial(finish_kernel, slab, start, stride, tail),
             "finish",
             pairs,
             [scalars(), whole(), whole(), one_spec],
@@ -428,8 +537,8 @@
     field = jnp.transpose(potential, (1, 0, 2))
     change = jnp.transpose(perturbation, (1, 0, 2))
     got_one = exchange(to_half(orbitals, 0))
-    got_two = exchange(to_half(orbitals, 1), got_one)
-    got_first = exchange(to_half(responses, 0), got_two)
+    half_two = to_half(orbitals, 1, None, 0)
+    got_two = exchange(to_half(responses, 0, half_two, 1), got_one)
     direct_inner = call(
         functools.partial(inner_kernel, slab),
         "inner",
@@ -439,23 +548,30 @@
         f32(2, 2, 2, 8, length),
         cost(32 * field_bytes, 4 * field_bytes),
     )(me, energies, orbitals, responses)
-    got_last = exchange(to_half(responses, 1), (got_first, direct_inner))
-    spaces = [to_space(got_one), to_space(got_two)]
-    send_first, inner_first, before = apply_first(got_first, spaces, field, change)
+    got_last = exchange(to_half(responses, 1), (got_two, direct_inner))
+    spaces = [to_space(got_one, 0, 3 * rows), to_space(got_two, 0, 6 * rows)]
+    send_first, inner_first, before = apply_first(got_two, spaces, field, change)
     back_first = exchange(send_first, got_last)
-    last_main, last_tail, inner_last, low, high = apply_last(
+    last_main, last_tail, inner_last, density = apply_last(
         got_last, spaces, field, change, before
     )
-    kept = jnp.where(pool == 0, low, high)
-    given = jnp.where(pool == 0, high, low)
+    kept, given = call(
+        pack_kernel,
+        "pack",
+        1,
+        [scalars(), whole(), whole(), whole()],
+        [whole(), whole()],
+        [block_shape, block_shape],
+        cost(4e9, 5e6),
+    )(pool, density, table["pair"], table["alone"])
     swap = [(0, 1), (1, 0)]
     local_inner = direct_inner + jnp.stack((inner_first, inner_last), axis=2)
-    local_inner = jnp.sum(local_inner, axis=(3, 4)).reshape(8)
-    riding = jnp.pad(local_inner, (0, slab * slab - 8)).reshape(1, -1, 1)
-    used = lax.broadcasted_iota(jnp.int32, density_shape.shape, 2) < half
-    summed = jnp.where(used, kept + lax.ppermute(given, "pool", swap), riding)
+    riding = jnp.sum(local_inner, axis=(3, 4)).reshape(1, 1, 8)
+    riding = jnp.pad(riding, ((0, 0), (0, 0), (0, 120)))
+    row = lax.broadcasted_iota(jnp.int32, block_shape.shape, 1)
+    summed = jnp.where(row < 108, kept + lax.ppermute(given, "pool", swap), riding)
     got_density = exchange(summed, back_first)
-    inner = jnp.sum(got_density[:, :8, half], axis=0).reshape(2, 2, 2)
+    inner = jnp.sum(got_density[:, 108, :8], axis=0).reshape(2, 2, 2)
     back_tail = exchange(last_tail, got_density)
     base = call(
         functools.partial(direct_kernel, slab),
@@ -466,41 +582,40 @@
         f32(*responses.shape),
         cost(32 * field_bytes, 6 * field_bytes),
     )(me, energies, inner, orbitals, responses)
-    natural_spec = pl.BlockSpec((2, length, 128), lambda p: (p, 0, 0))
     mirrored, natural = call(
-        functools.partial(mirror_kernel, slab),
+        mirror_kernel,
         "mirror",
-        pairs,
-        [whole(), whole(), whole()],
-        [density_spec, natural_spec],
-        [density_shape, f32(slab, length, 128)],
-        cost(2e9, 4e6),
-    )(got_density.reshape(-1, 128), table["mirror_pair"], single)
+        1,
+        [whole()] * 4,
+        [whole(), whole()],
+        [block_shape, f32(slab, length, 128)],
+        cost(4e9, 4e6),
+        scratch=[pltpu.VMEM((slab, length, 128), jnp.float32)],
+    )(got_density.reshape(-1, 128), table["loose_mirror"], table["loose_pair"], table["loose_alone"])
     got_mirrored = exchange(mirrored, (back_tail, base))
-    base = finish(base, back_first, 0, 3, False)
-    base = finish(base, back_first, 0, 3, True)
+    base = finish(base, back_first, 0, 0, 3 * rows, False)
+    base = finish(base, back_first, 0, 2 * rows, 3 * rows, True)
     back_main = exchange(last_main, (got_mirrored, base))
     symmetric = call(
-        functools.partial(swap_kernel, slab),
+        swap_kernel,
         "swap",
-        pairs,
-        [whole(), natural_spec],
-        natural_spec,
+        1,
+        [whole()] * 3,
+        whole(),
         f32(slab, length, 128),
-        cost(1e6, 4e6),
-    )(got_mirrored.reshape(-1, 128), natural)
+        cost(1e9, 4e6),
+    )(got_mirrored.reshape(-1, 128), table["loose_order"], natural)
     other = lax.ppermute(symmetric, "pool", swap)
-    kept, other = symmetric[..., :half], other[..., :half]
-    response_density = jnp.where(
-        pool == 0,
-        jnp.concatenate((kept, other), axis=2),
-        jnp.concatenate((other, kept), axis=2),
-    )
-    base = finish(base, back_tail, 1, 1, True)
+    low = jnp.where(pool == 0, symmetric, other)
+    high = jnp.where(pool == 0, other, symmetric)
+    response_density = jnp.concatenate(
+        (low[..., :64], high[..., :64], low[..., 64:96], high[..., 64:96]), axis=2
+    )
+    base = finish(base, back_tail, 1, 0, rows, True)
     base, response_density, back_main = lax.optimization_barrier(
         (base, response_density, back_main)
     )
-    base = finish(base, back_main, 1, 2, False)
+    base = finish(base, back_main, 1, 0, 2 * rows, False)
     return base, response_density
 
 
@@ -643,7 +758,7 @@
 
 def body(orbitals, responses, energies, weights, potential, perturbation):
     slab, length = orbitals.shape[3], orbitals.shape[-1]
-    fits = slab % 4 == 0 and length == 192 and orbitals.shape[0] == 1 and orbitals.shape[1] == 2
+    fits = slab == 12 and length == 192 and orbitals.shape[0] == 1 and orbitals.shape[1] == 2
     return (packed_body if fits else plain_body)(
         orbitals, responses, energies, weights, potential, perturbation
     )

time: 611 us -> 576 us (0.943)
  Pallas kernels: 211 us -> 171 us
  waiting for transfers between devices: 302 us -> 329 us
  local copies, waits for them, and re-layouts: 8.65 us -> 1.62 us
    pallas_call x12 -> x13, Pallas kernels: 134 us -> 102 us  [the longest x4 44.5 us: to_half(): call(kernel, 'to_half', pairs, [pl.BlockSpec((1, 1, 2, 2, length, length)...]
    all_to_all x8 -> x7, waiting for transfers between devices: 258 us -> 289 us  [exchange(): return lax.all_to_all(values, 'pw', split_axis=0, concat_axis=0, tiled=True)]
    unnamed x20 -> x10, local copies, waits for them, and re-layouts: 7.79 us -> 0.02 us
    all_to_all x8 -> x7, starting transfers between devices: 42 us -> 36.1 us  [exchange(): return lax.all_to_all(values, 'pw', split_axis=0, concat_axis=0, tiled=True)]
  transfers between devices with their start and end apart: 10 -> 9, of which waited for: 10 -> 9; matrix products, arithmetic and copies ran while one was open for 2% -> 1% of each run, Pallas kernels for 30% -> 27%
where the time goes in v2:
time: 576 us; the launch traced here: 574 us
  waiting for transfers between devices  329 us (57%)
  Pallas kernels  171 us (30%)
  starting transfers between devices  38.5 us (7%)
  blocking collectives  26.8 us (5%)
  other arithmetic  6.13 us (1%)
    all_to_all x7, waiting for transfers between devices, exchange(): return lax.all_to_all(values, 'pw', split_axis=0, concat_axis=0, tiled=True)  289 us
    pallas_call x4, Pallas kernels, to_half(): call(kernel, 'to_half', pairs, [pl.BlockSpec((1, 1, 2, 2, length, length)...  44.5 us
    all_to_all x7, starting transfers between devices, exchange(): return lax.all_to_all(values, 'pw', split_axis=0, concat_axis=0, tiled=True)  36.1 us
    pallas_call x4, Pallas kernels, finish(): call(functools.partial(finish_kernel, slab, start, stride, tail), 'finish...  28 us
    all_to_all x1, blocking collectives, exchange(): return lax.all_to_all(values, 'pw', split_axis=0, concat_axis=0, tiled=True)  26.8 us
    pallas_call x1, Pallas kernels, apply_first(): call(kernel, 'apply_first', pairs, [scalars(), whole(), space_spec, space...  23.7 us
    pallas_call x1, Pallas kernels, apply_last(): call(kernel, 'apply_last', pairs, [scalars(), whole(), space_spec, space_...  22.4 us
    ppermute x1, waiting for transfers between devices, packed_body(): lax.ppermute(given, 'pool', swap)  20.4 us
  transfers between devices with their start and end apart: 9, of which 9 were waited for; matrix products, arithmetic and copies ran while one was open for 1% of the time, Pallas kernels for 27%

profile of v2, /device:TPU:13, one launch (start us, length us, event | category | flops | bytes accessed | tf_op | source)
XLA Modules:
  0.0 574.2 jit_solution(7894039141918883967)
XLA Ops:
  0.6 11.1 %to_half.7 = f32[16,6,3,24,128]{4,3,2,1,0:T(8,128)} custom-call(f32[1,2,2,12,192,192]{5,4,3,2,1,0:T(8,128)} %orbitals.3, bf16[2,192,256]{2,1,0:T(8,128)(2,1)} %constant.41.clone.cosine.tables_and_outs_1_, bf16[2,2,192,256]{3,2,1,0:T(8,128)(2,1)} %constant.42.clone.mixed.tables_and_outs_2_, bf16[2,192,576]{2,1,0:T(8,128)(2,1)} %constant.43.clone.send), custom_call_target="tpu_custom_call" | custom-call | flops 8153726976 | bytes 7077888 | tf_op jit(solution)/shard_map/to_half/pallas_call | solution.py:432
  11.8 6.5 %all-to-all-start = ((f32[16,432,128]{2,1,0:T(8,128)}), f32[16,432,128]{2,1,0:T(8,128)}, u32[]{:S(2)}, u32[]{:S(2)}) async-start(f32[16,432,128]{2,1,0:T(8,128)} %bitcast.31), calls=%async_computation | async-start | bytes 7077888 | tf_op jit(solution)/shard_map/all_to_all | solution.py:422
  18.3 11.1 %to_half.5.rest_0_ = f32[16,6,2,3,24,128]{5,4,3,2,1,0:T(8,128)} custom-call(f32[1,2,2,12,192,192]{5,4,3,2,1,0:T(8,128)} %orbitals.3, bf16[2,192,256]{2,1,0:T(8,128)(2,1)} %constant.41.clone.cosine.tables_and_outs_1_, bf16[2,2,192,256]{3,2,1,0:T(8,128)(2,1)} %constant.42.clone.mixed.tables_and_outs_2_, bf16[2,192,576]{2,1,0:T(8,128)(2,1)} %constant.43.clone.send), custom_call_target="tpu_custom_call" | custom-call | flops 8153726976 | bytes 7077888 | tf_op jit(solution)/shard_map/to_half/pallas_call | solution.py:432
  29.4 11.1 %to_half.6 = f32[16,6,2,3,24,128]{5,4,3,2,1,0:T(8,128)} custom-call(f32[1,2,2,12,192,192]{5,4,3,2,1,0:T(8,128)} %responses.3, bf16[2,192,256]{2,1,0:T(8,128)(2,1)} %constant.41.clone.cosine.tables_and_outs_1_, bf16[2,2,192,256]{3,2,1,0:T(8,128)(2,1)} %constant.42.clone.mixed.tables_and_outs_2_, ...), custom_call_target="tpu_custom_call", output_to_operand_aliasing={{}: (4, {})} | custom-call | flops 8153726976 | bytes 7077888 | tf_op jit(solution)/shard_map/to_half/pallas_call | solution.py:432
  40.5 56.2 %all-to-all-done = f32[16,432,128]{2,1,0:T(8,128)} async-done(((f32[16,432,128]{2,1,0:T(8,128)}), f32[16,432,128]{2,1,0:T(8,128)}, u32[]{:S(2)}, u32[]{:S(2)}) %all-to-all-start) | async-done | bytes 3538976 | tf_op jit(solution)/shard_map/all_to_all | solution.py:422
  96.7 4.9 all-to-all-start.1
  101.6 10.1 %inner.1 = f32[2,2,2,8,192]{4,3,2,1,0:T(8,128)} custom-call(s32[1]{0:T(128)} %bitcast.me, f32[1,2]{1,0:T(1,128)} %energies.3, f32[1,2,2,12,192,192]{5,4,3,2,1,0:T(8,128)} %orbitals.3, f32[1,2,2,12,192,192]{5,4,3,2,1,0:T(8,128)} %responses.3), custom_call_target="tpu_custom_call" | custom-call | flops 113246208 | bytes 14155776 | tf_op jit(solution)/shard_map/inner/pallas_call | solution.py:542
  111.8 11.1 %to_half.4 = f32[16,6,3,24,128]{4,3,2,1,0:T(8,128)} custom-call(f32[1,2,2,12,192,192]{5,4,3,2,1,0:T(8,128)} %responses.3, bf16[2,192,256]{2,1,0:T(8,128)(2,1)} %constant.41.clone.cosine.tables_and_outs_1_, bf16[2,2,192,256]{3,2,1,0:T(8,128)(2,1)} %constant.42.clone.mixed.tables_and_outs_2_, bf16[2,192,576]{2,1,0:T(8,128)(2,1)} %constant.43.clone.send), custom_call_target="tpu_custom_call" | custom-call | flops 8153726976 | bytes 7077888 | tf_op jit(solution)/shard_map/to_half/pallas_call | solution.py:432
  122.9 133.0 %all-to-all-done.1 = f32[16,864,128]{2,1,0:T(8,128)} async-done(((f32[16,864,128]{2,1,0:T(8,128)}), f32[16,864,128]{2,1,0:T(8,128)}, u32[]{:S(2)}, u32[]{:S(2)}) %all-to-all-start.1) | async-done | bytes 7077920 | tf_op jit(solution)/shard_map/all_to_all | solution.py:422
  255.9 4.9 all-to-all-start.2
  261.4 7.0 %to_space.2.first = f32[12,384,192]{2,1,0:T(8,128)} custom-call(f32[6912,128]{1,0:T(8,128)} %bitcast.5.got, bf16[2,192,576]{2,1,0:T(8,128)(2,1)} %constant.44.clone.receive.tables_and_outs_0_), custom_call_target="tpu_custom_call" | custom-call | flops 4076863488 | bytes 7077888 | tf_op jit(solution)/shard_map/to_space/pallas_call | solution.py:454
  268.4 8.3 %to_space.3.second = f32[12,384,192]{2,1,0:T(8,128)} custom-call(f32[13824,128]{1,0:T(8,128)} %bitcast.6.got, bf16[2,192,576]{2,1,0:T(8,128)(2,1)} %constant.44.clone.receive.tables_and_outs_0_), custom_call_target="tpu_custom_call" | custom-call | flops 4076863488 | bytes 7077888 | tf_op jit(solution)/shard_map/to_space/pallas_call | solution.py:454
  276.7 23.7 %apply_first.1 = (f32[16,6,3,24,128]{4,3,2,1,0:T(8,128)}, f32[2,2,8,192]{3,2,1,0:T(8,128)}, f32[12,192,192]{2,1,0:T(8,128)}) custom-call(f32[1]{0:T(128)S(6)} %copy.34.weights, f32[13824,128]{1,0:T(8,128)} %bitcast.6.got, f32[12,384,192]{2,1,0:T(8,128)} %to_space.2.first, f32[12,384,192]{2,1,0:T(8,128)} %to_space.3.second, f32[12,192,192]{2,1,0:T(8,128)} %bitcast.37, ...), custom_call_target="tpu_custom_call" | custom-call | flops 12230590464 | bytes 17694720 | tf_op jit(solution)/shard_map/apply_first/pallas_call | solution.py:484
  300.4 38.8 %all-to-all-done.2 = f32[16,432,128]{2,1,0:T(8,128)} async-done(((f32[16,432,128]{2,1,0:T(8,128)}), f32[16,432,128]{2,1,0:T(8,128)}, u32[]{:S(2)}, u32[]{:S(2)}) %all-to-all-start.2) | async-done | bytes 3538976 | tf_op jit(solution)/shard_map/all_to_all | solution.py:422
  339.2 4.9 all-to-all-start.3
  344.1 22.4 %apply_last.1 = (f32[16,6,2,24,128]{4,3,2,1,0:T(8,128)}, f32[16,6,24,128]{3,2,1,0:T(8,128)}, f32[2,2,8,192]{3,2,1,0:T(8,128)}, f32[12,192,192]{2,1,0:T(8,128)}) custom-call(f32[1]{0:T(128)S(6)} %copy.34.weights, f32[6912,128]{1,0:T(8,128)} %bitcast.4.got, f32[12,384,192]{2,1,0:T(8,128)} %to_space.2.first, f32[12,384,192]{2,1,0:T(8,128)} %to_space.3.second, ...), custom_call_target="tpu_custom_call" | custom-call | flops 12230590464 | bytes 17694720 | tf_op jit(solution)/shard_map/apply_last/pallas_call | solution.py:505
  366.6 0.0 copy-start.2
  366.6 0.0 copy-start.3
  366.6 0.0 copy-start.4
  366.6 6.1 %pack.1 = (f32[16,112,128]{2,1,0:T(8,128)}, f32[16,112,128]{2,1,0:T(8,128)}) custom-call(s32[1]{0:T(128)} %bitcast.10.pool, f32[12,192,192]{2,1,0:T(8,128)} %get-tuple-element.27.density, bf16[384,384]{1,0:T(8,128)(2,1)} %constant.47.clone.pair, bf16[256,192]{1,0:T(8,128)(2,1)} %constant.48.clone.alone), custom_call_target="tpu_custom_call" | custom-call | flops 4000000000 | bytes 5000000 | tf_op jit(solution)/shard_map/pack/pallas_call | solution.py:558
  372.7 1.2 collective-permute-start
  373.9 0.0 copy-done.2
  373.9 0.0 copy-done.3
  373.9 0.0 copy-done.4
  374.0 0.1 fusion
  374.1 0.1 copy.27
  374.2 0.1 reshape.70
  374.3 20.4 %collective-permute-done = f32[16,112,128]{2,1,0:T(8,128)S(1)} collective-permute-done((f32[16,112,128]{2,1,0:T(8,128)}, f32[16,112,128]{2,1,0:T(8,128)S(1)}, u32[]{:S(2)}, u32[]{:S(2)}) %collective-permute-start) | collective-permute-done | bytes 917536 | tf_op jit(solution)/shard_map/ppermute | solution.py:572
  394.6 1.3 add_select_fusion
  395.9 26.6 %all-to-all-done.3 = f32[16,432,128]{2,1,0:T(8,128)} async-done(((f32[16,432,128]{2,1,0:T(8,128)}), f32[16,432,128]{2,1,0:T(8,128)}, u32[]{:S(2)}, u32[]{:S(2)}) %all-to-all-start.3) | async-done | bytes 3538976 | tf_op jit(solution)/shard_map/all_to_all | solution.py:422
  422.5 26.8 %all_to_all.40 = f32[16,112,128]{2,1,0:T(8,128)} all-to-all(f32[16,112,128]{2,1,0:T(8,128)S(1)} %add_select_fusion), channel_id=1, replica_groups=mesh['pool'=2,'pw'=16] {'pw'}, dimensions={0} | all-to-all | bytes 1835008 | tf_op jit(solution)/shard_map/all_to_all | solution.py:422
  449.4 5.0 all-to-all-start.5
  454.4 0.9 slice_reduce_fusion
  455.2 0.7 reshape.74.inner
  455.9 12.3 %direct.1.base = f32[1,2,2,12,192,192]{5,4,3,2,1,0:T(8,128)} custom-call(s32[1]{0:T(128)} %bitcast.me, f32[1,2]{1,0:T(1,128)} %energies.3, f32[2,2,2]{2,1,0:T(2,128)} %reshape.74.inner, f32[1,2,2,12,192,192]{5,4,3,2,1,0:T(8,128)} %orbitals.3, f32[1,2,2,12,192,192]{5,4,3,2,1,0:T(8,128)} %responses.3), custom_call_target="tpu_custom_call" | custom-call | flops 113246208 | bytes 21233664 | tf_op jit(solution)/shard_map/direct/pallas_call | solution.py:576
  468.2 4.6 mirror.1
  472.8 9.3 %all-to-all-done.5 = f32[16,144,128]{2,1,0:T(8,128)S(1)} async-done(((f32[16,144,128]{2,1,0:T(8,128)}), f32[16,144,128]{2,1,0:T(8,128)S(1)}, u32[]{:S(2)}, u32[]{:S(2)}) %all-to-all-start.5) | async-done | bytes 1179680 | tf_op jit(solution)/shard_map/all_to_all | solution.py:422
  482.1 0.0 copy-start
  482.1 4.9 all-to-all-start.6
  487.0 7.2 %finish.4.base = f32[1,2,2,12,192,192]{5,4,3,2,1,0:T(8,128)} custom-call(s32[1]{0:T(128)} %bitcast.me, f32[6912,128]{1,0:T(8,128)} %bitcast.16.got, bf16[2,192,576]{2,1,0:T(8,128)(2,1)} %constant.46.clone.receive, f32[1,2,2,12,192,192]{5,4,3,2,1,0:T(8,128)} %direct.1.base), custom_call_target="tpu_custom_call", output_to_operand_aliasing={{}: (3, {})} | custom-call | flops 4076863488 | bytes 7077888 | tf_op jit(solution)/shard_map/finish/pallas_call | solution.py:526
  494.2 0.0 copy-done
  494.2 7.3 %finish.5.base = f32[1,2,2,12,192,192]{5,4,3,2,1,0:T(8,128)} custom-call(s32[1]{0:T(128)} %bitcast.me, f32[6912,128]{1,0:T(8,128)} %bitcast.16.got, bf16[2,192,576]{2,1,0:T(8,128)(2,1)} %constant.46.clone.receive, f32[1,2,2,12,192,192]{5,4,3,2,1,0:T(8,128)} %finish.4.base), custom_call_target="tpu_custom_call", output_to_operand_aliasing={{}: (3, {})} | custom-call | flops 4076863488 | bytes 7077888 | tf_op jit(solution)/shard_map/finish/pallas_call | solution.py:526
  501.5 7.7 %all-to-all-done.6 = f32[16,112,128]{2,1,0:T(8,128)} async-done(((f32[16,112,128]{2,1,0:T(8,128)}), f32[16,112,128]{2,1,0:T(8,128)}, u32[]{:S(2)}, u32[]{:S(2)}) %all-to-all-start.6) | async-done | bytes 917536 | tf_op jit(solution)/shard_map/all_to_all | solution.py:422
  509.2 5.0 all-to-all-start.7
  514.1 3.8 swap.1
  517.9 1.2 collective-permute-start.1
  519.1 0.0 copy-start.1
  519.1 6.6 %finish.6.base = f32[1,2,2,12,192,192]{5,4,3,2,1,0:T(8,128)} custom-call(s32[1]{0:T(128)} %bitcast.me, f32[2304,128]{1,0:T(8,128)} %bitcast.28, bf16[2,192,576]{2,1,0:T(8,128)(2,1)} %constant.46.clone.receive, f32[1,2,2,12,192,192]{5,4,3,2,1,0:T(8,128)} %finish.5.base), custom_call_target="tpu_custom_call", output_to_operand_aliasing={{}: (3, {})} | custom-call | flops 4076863488 | bytes 7077888 | tf_op jit(solution)/shard_map/finish/pallas_call | solution.py:526
  525.8 19.7 %collective-permute-done.1 = f32[12,192,128]{2,1,0:T(8,128)} collective-permute-done((f32[12,192,128]{2,1,0:T(8,128)}, f32[12,192,128]{2,1,0:T(8,128)}, u32[]{:S(2)}, u32[]{:S(2)}) %collective-permute-start.1) | collective-permute-done | bytes 1179680 | tf_op jit(solution)/shard_map/ppermute | solution.py:608
  545.4 0.0 copy-done.1
  545.4 1.4 broadcast_select_fusion.1
  546.9 0.4 slice.24
  547.3 0.4 slice.23
  547.6 2.4 pad_maximum_fusion
  550.0 17.2 %all-to-all-done.7 = f32[16,288,128]{2,1,0:T(8,128)} async-done(((f32[16,288,128]{2,1,0:T(8,128)}), f32[16,288,128]{2,1,0:T(8,128)}, u32[]{:S(2)}, u32[]{:S(2)}) %all-to-all-start.7) | async-done | bytes 2359328 | tf_op jit(solution)/shard_map/all_to_all | solution.py:422
  567.2 6.9 %finish.7 = f32[1,2,2,12,192,192]{5,4,3,2,1,0:T(8,128)} custom-call(s32[1]{0:T(128)} %bitcast.me, f32[4608,128]{1,0:T(8,128)} %bitcast.21.got, bf16[2,192,576]{2,1,0:T(8,128)(2,1)} %constant.46.clone.receive, f32[1,2,2,12,192,192]{5,4,3,2,1,0:T(8,128)} %finish.6.base), custom_call_target="tpu_custom_call", output_to_operand_aliasing={{}: (3, {})} | custom-call | flops 4076863488 | bytes 7077888 | tf_op jit(solution)/shard_map/finish/pallas_call | solution.py:526
  (2 shorter events, 0.0 us)
Async XLA Ops:
  11.8 84.9 %all-to-all-start = ((f32[16,432,128]{2,1,0:T(8,128)}), f32[16,432,128]{2,1,0:T(8,128)}, u32[]{:S(2)}, u32[]{:S(2)}) async-start(f32[16,432,128]{2,1,0:T(8,128)} %bitcast.31), calls=%async_computation | async-start | bytes 7077888 | tf_op jit(solution)/shard_map/all_to_all | solution.py:422
  96.7 159.2 %all-to-all-start.1 = ((f32[16,864,128]{2,1,0:T(8,128)}), f32[16,864,128]{2,1,0:T(8,128)}, u32[]{:S(2)}, u32[]{:S(2)}) async-start(f32[16,864,128]{2,1,0:T(8,128)} %bitcast.27), calls=%async_computation.1 | async-start | bytes 14155776 | tf_op jit(solution)/shard_map/all_to_all | solution.py:422
  255.9 83.3 %all-to-all-start.2 = ((f32[16,432,128]{2,1,0:T(8,128)}), f32[16,432,128]{2,1,0:T(8,128)}, u32[]{:S(2)}, u32[]{:S(2)}) async-start(f32[16,432,128]{2,1,0:T(8,128)} %bitcast.30), calls=%async_computation.2 | async-start | bytes 7077888 | tf_op jit(solution)/shard_map/all_to_all | solution.py:422
  339.2 83.3 %all-to-all-start.3 = ((f32[16,432,128]{2,1,0:T(8,128)}), f32[16,432,128]{2,1,0:T(8,128)}, u32[]{:S(2)}, u32[]{:S(2)}) async-start(f32[16,432,128]{2,1,0:T(8,128)} %bitcast.29), calls=%async_computation.3 | async-start | bytes 7077888 | tf_op jit(solution)/shard_map/all_to_all | solution.py:422
  366.6 7.4 %copy-start.2 = (f32[2,2,2,8,192]{4,3,2,1,0:T(8,128)S(1)}, f32[2,2,2,8,192]{4,3,2,1,0:T(8,128)}, u32[]{:S(2)}) copy-start(f32[2,2,2,8,192]{4,3,2,1,0:T(8,128)} %inner.1) | copy-start | bytes 147460
  366.6 7.4 %copy-start.3 = (f32[2,2,8,192]{3,2,1,0:T(8,128)S(1)}, f32[2,2,8,192]{3,2,1,0:T(8,128)}, u32[]{:S(2)}) copy-start(f32[2,2,8,192]{3,2,1,0:T(8,128)} %get-tuple-element.30) | copy-start | bytes 73732
  366.6 7.4 %copy-start.4 = (f32[2,2,8,192]{3,2,1,0:T(8,128)S(1)}, f32[2,2,8,192]{3,2,1,0:T(8,128)}, u32[]{:S(2)}) copy-start(f32[2,2,8,192]{3,2,1,0:T(8,128)} %get-tuple-element.31) | copy-start | bytes 73732
  372.7 21.9 %collective-permute-start = (f32[16,112,128]{2,1,0:T(8,128)}, f32[16,112,128]{2,1,0:T(8,128)S(1)}, u32[]{:S(2)}, u32[]{:S(2)}) collective-permute-start(f32[16,112,128]{2,1,0:T(8,128)} %get-tuple-element.29), channel_id=1, source_target_pairs={{0,16},{16,0},{1,17},{17,1},{2,18},{18,2},{3,19},{19,3},{4,20},{20... | collective-permute-start | bytes 2752520 | tf_op jit(solution)/shard_map/ppermute | solution.py:572
  449.4 32.8 %all-to-all-start.5 = ((f32[16,144,128]{2,1,0:T(8,128)}), f32[16,144,128]{2,1,0:T(8,128)S(1)}, u32[]{:S(2)}, u32[]{:S(2)}) async-start(f32[16,144,128]{2,1,0:T(8,128)} %bitcast.33), calls=%async_computation.5 | async-start | bytes 2359296 | tf_op jit(solution)/shard_map/all_to_all | solution.py:422
  482.1 12.1 %copy-start = (f32[16,144,128]{2,1,0:T(8,128)}, f32[16,144,128]{2,1,0:T(8,128)S(1)}, u32[]{:S(2)}) copy-start(f32[16,144,128]{2,1,0:T(8,128)S(1)} %all-to-all-done.5) | copy-start | bytes 3538948
  482.1 27.0 %all-to-all-start.6 = ((f32[16,112,128]{2,1,0:T(8,128)}), f32[16,112,128]{2,1,0:T(8,128)}, u32[]{:S(2)}, u32[]{:S(2)}) async-start(f32[16,112,128]{2,1,0:T(8,128)} %get-tuple-element.37), calls=%async_computation.6 | async-start | bytes 1835008 | tf_op jit(solution)/shard_map/all_to_all | solution.py:422
  509.2 58.1 %all-to-all-start.7 = ((f32[16,288,128]{2,1,0:T(8,128)}), f32[16,288,128]{2,1,0:T(8,128)}, u32[]{:S(2)}, u32[]{:S(2)}) async-start(f32[16,288,128]{2,1,0:T(8,128)} %bitcast.32), calls=%async_computation.7 | async-start | bytes 4718592 | tf_op jit(solution)/shard_map/all_to_all | solution.py:422
  517.9 27.5 %collective-permute-start.1 = (f32[12,192,128]{2,1,0:T(8,128)}, f32[12,192,128]{2,1,0:T(8,128)}, u32[]{:S(2)}, u32[]{:S(2)}) collective-permute-start(f32[12,192,128]{2,1,0:T(8,128)} %swap.1), channel_id=1, source_target_pairs={{0,16},{16,0},{1,17},{17,1},{2,18},{18,2},{3,19},{19,3},{4,20},{20... | collective-permute-start | bytes 3538952 | tf_op jit(solution)/shard_map/ppermute | solution.py:608
  519.1 26.3 %copy-start.1 = (f32[12,192,128]{2,1,0:T(8,128)S(1)}, f32[12,192,128]{2,1,0:T(8,128)}, u32[]{:S(2)}) copy-start(f32[12,192,128]{2,1,0:T(8,128)} %swap.1) | copy-start | bytes 3538948

commit v3 on v2

--- a/solution.py
+++ b/solution.py
@@ -11,7 +11,7 @@
 from jax.sharding import PartitionSpec as P
 
 RECIPROCAL_SQUARE = 0.023428
-VMEM_BYTES = 62 * 1024 * 1024
+VMEM_BYTES = 63 * 1024 * 1024
 
 
 def split_table(table):
@@ -36,7 +36,7 @@
     inverse = np.block([[cosine, -sine], [sine, cosine]])
     forward = np.block([[cosine, sine], [-sine, cosine]])
     sent = np.arange(2 * length).reshape(2, members, slab).transpose(1, 0, 2).reshape(-1)
-    got = np.arange(2 * length).reshape(2, members, slab // 2, 2).transpose(3, 0, 1, 2)
+    got = np.arange(2 * length).reshape(2, members, slab // 4, 2, 2).transpose(4, 0, 3, 1, 2)
     got = got.reshape(2, -1)
     first = np.arange(2 * length).reshape(2, 2, length // 2)[:, 0].reshape(-1)
     parity = np.arange(2 * length).reshape(length, 2).T
@@ -48,6 +48,15 @@
     alone = np.pad(mirror.reshape(members, slab, length), ((0, 0), (0, 4), (0, 0)))
     alone = alone.reshape(-1, length)
     loose = index.reshape(members, slab).T.reshape(-1)
+    fold = np.minimum(index, length - index)
+    swapped = np.zeros((2, length, slab + 1, members))
+    swapped[0, index, fold % slab, fold // slab] = 1.0
+    swapped[0, length // 2] = 0.0
+    swapped[0, length // 2, slab, members // 2] = 1.0
+    folded = (length - fold) % length
+    swapped[1, index, folded % slab, folded // slab] = 1.0
+    swapped[1, 0] = 0.0
+    swapped[1, 0, slab, 0] = 1.0
     return {
         "cosine": split_table(np.pad(cosine, pad)),
         "mixed": np.stack(
@@ -62,7 +71,7 @@
         "loose_pair": both[:, :, loose].reshape(2 * length, -1).astype(ml_dtypes.bfloat16),
         "loose_alone": alone[:, loose].astype(ml_dtypes.bfloat16),
         "loose_mirror": mirror[:, loose].astype(ml_dtypes.bfloat16),
-        "loose_order": np.eye(length)[:, loose].astype(ml_dtypes.bfloat16),
+        "swapped": swapped.reshape(2 * length, -1).astype(ml_dtypes.bfloat16),
     }
 
 
@@ -121,7 +130,7 @@
     pair, length = field.shape[3], field.shape[4]
     members, rows = out.shape[0], out.shape[-2]
     mid = members // 2
-    out = out.at[:, 0, 0] if len(out.shape) == 6 else out.at[:, 0]
+    out = out.at[:, 0, 0]
     parts = [field[0, 0, part].reshape(pair * length, length) for part in range(2)]
     parts = turn_lanes(*parts, cosine, mixed, 1)
     for part in range(2):
@@ -155,17 +164,23 @@
     return ref[pl.ds(start, count, stride=stride), :]
 
 
-def plane(got, start, stride, place, slab, with_main, with_tail):
-    count = got.shape[0] // stride
+def plane(parts_of, place, slab, with_main, with_tail):
+    def rows_at(row):
+        pieces = [
+            received(ref, start + row, stride, ref.shape[0] // stride)
+            for ref, start, stride in parts_of
+        ]
+        return jnp.concatenate(pieces, axis=0)
+
     found = [[], []]
     for part in range(2):
-        row = start + part * slab + place
+        row = part * slab + place
         mains, tails = [None, None], [None, None]
         if with_main:
-            mains = [received(got, one * 2 * slab + row, stride, count) for one in range(2)]
+            mains = [rows_at(one * 2 * slab + row) for one in range(2)]
             row = row + 4 * slab
         if with_tail:
-            tail = received(got, row, stride, count)
+            tail = rows_at(row)
             tails = [tail, pltpu.roll(tail, 64, 1)]
         for one in range(2):
             pieces = [piece for piece in (mains[one], tails[one]) if piece is not None]
@@ -173,11 +188,13 @@
     return [jnp.concatenate(one, axis=0) for one in found]
 
 
-def to_space_kernel(slab, start, stride, got, receive, space):
+def to_space_kernel(slab, starts, strides, *refs):
+    *gots, receive, space = refs
     length = space.shape[2]
+    parts_of = list(zip(gots if len(gots) > 1 else gots * 2, starts, strides))
     for one in range(2):
         place = 2 * pl.program_id(0) + one
-        values = plane(got, start, stride, place, slab, True, True)
+        values = plane(parts_of, place, slab, True, True)
         real, imag = dot_receive(receive, values)
         space[one, :length] = real[:, :length]
         space[one, length:] = imag[:, :length]
@@ -188,7 +205,7 @@
 
 
 def apply_kernel(
-    slab, start, stride, band, weights, got, spaces, potential, perturbation, before,
+    slab, starts, stride, band, weights, got, spaces, potential, perturbation, before,
     receive, cosine, mixed, send, out_main, out_tail, inner, density
 ):
     length = potential.shape[1]
@@ -203,7 +220,8 @@
     tails = []
     sums = []
     for one in range(2):
-        values = plane(got, start, stride, 2 * step + one, slab, True, True)
+        parts_of = [(got, start, stride) for start in starts]
+        values = plane(parts_of, 2 * step + one, slab, True, True)
         real, imag = (piece[:, :length] for piece in dot_receive(receive, values))
         own_real, own_imag = spaces[band, one, :length], spaces[band, one, length:]
         local = twice_weight * (own_real * real + own_imag * imag)
@@ -230,45 +248,47 @@
         density[one] = sums[one]
 
 
-def lanes_from(*pieces):
-    lane = lax.broadcasted_iota(jnp.int32, pieces[0][0].shape, 1)
-    width = 128 // len(pieces)
-    moved = [pltpu.roll(values, by, 1) if by else values for values, by in pieces]
-    made = moved[-1]
-    for place in range(len(pieces) - 2, -1, -1):
-        made = jnp.where(lane < (place + 1) * width, moved[place], made)
-    return made
-
-
-def pack(planes, pair, alone, out):
+def lanes_of(values):
+    return lax.broadcasted_iota(jnp.int32, values.shape, 1)
+
+
+def moved(values, by):
+    return pltpu.roll(values, by % 128, 1) if by % 128 else values
+
+
+def pack(planes, count, width, pair, alone, out):
     members = out.shape[0]
-    tails = []
-    for first in range(0, 12, 4):
-        one, two, three, four = (planes(first + by) for by in range(4))
-        mains = (lanes_from((one, 0), (two, 64)), lanes_from((three, 0), (four, 64)))
-        tails.append(lanes_from((one, 64), (two, 96), (three, 0), (four, 32)))
-        out[:, 6 * first : 6 * first + 24] = dot_mirror(
-            pair[...], jnp.concatenate(mains, axis=0)
+    blocks = []
+    for block in range(-(-count * width // 128)):
+        made = None
+        for place in range(count):
+            start = place * width - 128 * block
+            if start >= 128 or start + width <= 0:
+                continue
+            values = moved(planes(place), start)
+            made = values if made is None else jnp.where(lanes_of(values) < start, made, values)
+        blocks.append(made)
+    for first in range(0, len(blocks) - 1, 2):
+        out[:, 12 * first : 12 * first + 24] = dot_mirror(
+            pair[...], jnp.concatenate(blocks[first : first + 2], axis=0)
         ).reshape(members, 24, 128)
-    out[:, 72:96] = dot_mirror(pair[...], jnp.concatenate(tails[:2], axis=0)).reshape(
-        members, 24, 128
-    )
-    out[:, 96:112] = dot_mirror(alone[...], tails[2]).reshape(members, 16, 128)
-
-
-def unpack(got, place):
-    members = got.shape[0] // 112
+    out[:, 12 * len(blocks) - 12 :] = dot_mirror(alone[...], blocks[-1]).reshape(members, 16, 128)
+
+
+def unpack(got, place, count, width, rows):
+    members = got.shape[0] // rows
+    blocks = [
+        received(got, 12 * block + place, rows, members)
+        for block in range(-(-count * width // 128))
+    ]
     found = []
-    for quad in range(3):
-        one = received(got, 24 * quad + place, 112, members)
-        two = received(got, 24 * quad + 12 + place, 112, members)
-        tail = received(got, 72 + 12 * quad + place, 112, members)
-        found += [
-            lanes_from((one, 0), (tail, 64)),
-            lanes_from((one, 64), (tail, 32)),
-            lanes_from((two, 0), (tail, 0)),
-            lanes_from((two, 64), (tail, 96)),
-        ]
+    for one in range(count):
+        block, start = divmod(one * width, 128)
+        values = moved(blocks[block], -start)
+        if start + width > 128:
+            rest = moved(blocks[block + 1], -start)
+            values = jnp.where(lanes_of(values) < 128 - start, values, rest)
+        found.append(values)
     return jnp.concatenate(found, axis=0)
 
 
@@ -276,22 +296,19 @@
     length = density.shape[1]
     own = pool[0] == 0
 
-    def halves_of(place):
-        main = density[place, :, :128]
-        tail = jnp.concatenate(
-            (density[place, :, 128:], jnp.zeros((length, 64), jnp.float32)), axis=1
-        )
-        return lanes_from((main, 0), (tail, 64)), lanes_from((main, 64), (tail, 32))
-
     def one_half(which):
         def planes(place):
-            low, high = halves_of(place)
+            low = density[place, :, :128]
+            rest = jnp.concatenate(
+                (density[place, :, 128:], jnp.zeros((length, 64), jnp.float32)), axis=1
+            )
+            high = jnp.where(lanes_of(low) < 32, moved(low, 32), moved(rest, 32))
             return jnp.where(own, low, high) if which else jnp.where(own, high, low)
 
         return planes
 
-    pack(one_half(True), pair, alone, kept)
-    pack(one_half(False), pair, alone, given)
+    pack(one_half(True), 12, 96, pair, alone, kept)
+    pack(one_half(False), 12, 96, pair, alone, given)
 
 
 def frequencies(length, first, lanes, first_lane):
@@ -343,28 +360,42 @@
             out[0, band, 1, one] = responses[0, band, 1, one] - imag * inverse
 
 
-def finish_kernel(slab, start, stride, tail, me, got, receive, base, out):
+def finish_kernel(slab, starts, stride, tail, me, got, receive, base, out):
     length = base.shape[4]
+    first = 2 * pl.program_id(0)
+    parts_of = [(got, start, stride) for start in starts]
+    planes = [plane(parts_of, first + one, slab, not tail, tail) for one in range(2)]
+    values = [jnp.concatenate(both, axis=1) for both in zip(*planes)]
+    applied = dot_receive(receive, values)
     for one in range(2):
-        place = 2 * pl.program_id(0) + one
-        values = plane(got, start, stride, place, slab, not tail, tail)
-        applied = dot_receive(receive, values)
-        kinetic = frequencies(length, me[0] * slab + place, 128, 128 if tail else 0)
+        kinetic = frequencies(length, me[0] * slab + first + one, 128, 128 if tail else 0)
         inverse = 1.0 / (1.0 + kinetic)
         for part in range(2):
-            out[0, 0, part, one] = base[0, 0, part, one] - applied[part] * inverse
-
-
-def mirror_kernel(got, single, pair, alone, out, natural, loose):
+            piece = applied[part][:, 128 * one : 128 * (one + 1)]
+            out[0, 0, part, one] = base[0, 0, part, one] - piece * inverse
+
+
+def mirror_kernel(me, got, single, pair, alone, out, natural, loose):
+    below = me[0] < out.shape[0] // 2
     for place in range(12):
-        loose[place] = unpack(got, place)
+        loose[place] = unpack(got, place, 12, 96, 112)
         natural[place] = dot_mirror(single[...], loose[place])
-    pack(lambda place: loose[place], pair, alone, out)
+
+    def planes(place):
+        values = loose[place % 12]
+        other = moved(values, -48)
+        return jnp.where(below, values, other) if place < 12 else jnp.where(below, other, values)
+
+    pack(planes, 13, 48, pair, alone, out)
 
 
 def swap_kernel(got, order, natural, out):
+    length = natural.shape[1]
     for place in range(12):
-        out[place] = (natural[place] + dot_mirror(order[...], unpack(got, place))) * 0.125
+        halves_of = dot_mirror(order[...], unpack(got, place, 13, 48, 64))
+        low, high = halves_of[:length], moved(halves_of[length:], 48)
+        swapped = jnp.where(lanes_of(low) < 48, low, high)
+        out[place] = (natural[place] + swapped) * 0.125
 
 
 def cost(flops, moved):
@@ -421,28 +452,34 @@
             values, _ = lax.optimization_barrier((values, after))
         return lax.all_to_all(values, "pw", split_axis=0, concat_axis=0, tiled=True)
 
-    def to_half(field, band, into=None, slot=None):
+    def to_half(field, band, slots, group=None, into=None, slot=0):
         def kernel(field, cosine, mixed, send, *rest):
             to_half_kernel(field, cosine, mixed, send, *rest[-2:])
 
-        spec, shape = half_spec, half_shape
-        if slot is not None:
-            spec = pl.BlockSpec((members, 1, 1, 3, rows, 128), lambda p: (0, p, slot, 0, 0, 0))
-            shape = f32(members, pairs, 2, 3, rows, 128)
+        if group is None:
+            grid = pairs
+            pair_at = lambda p: p
+            block_at = lambda p: (0, p // 2, slot + p % 2, 0, 0, 0)
+        else:
+            grid = pairs // 2
+            pair_at = lambda p: 2 * p + group
+            block_at = lambda p: (0, p, slot, 0, 0, 0)
         return call(
             kernel,
             "to_half",
-            pairs,
+            grid,
             [
-                pl.BlockSpec((1, 1, 2, 2, length, length), lambda p: (0, band, 0, p, 0, 0)),
+                pl.BlockSpec(
+                    (1, 1, 2, 2, length, length), lambda p: (0, band, 0, pair_at(p), 0, 0)
+                ),
                 whole(),
                 whole(),
                 whole(),
             ]
             + ([] if into is None else [pl.BlockSpec(memory_space=pl.ANY)]),
-            spec,
-            shape,
-            cost(2 * stage_flops, 2 * field_bytes),
+            pl.BlockSpec((members, 1, 1, 3, rows, 128), block_at),
+            f32(members, pairs // 2, slots, 3, rows, 128),
+            cost(2 * stage_flops * grid / pairs, 2 * field_bytes * grid / pairs),
             {} if into is None else {4: 0},
             [pltpu.VMEM((2, 2, 2 * length, 128), jnp.float32)],
         )(
@@ -450,16 +487,16 @@
             *(() if into is None else (into,)),
         )
 
-    def to_space(got, start, stride):
+    def to_space(gots, starts, strides):
         return call(
-            functools.partial(to_space_kernel, slab, start, stride),
+            functools.partial(to_space_kernel, slab, starts, strides),
             "to_space",
             pairs,
-            [whole(), whole()],
+            [whole()] * (len(gots) + 1),
             pl.BlockSpec((2, 2 * length, length), lambda p: (p, 0, 0)),
             f32(slab, 2 * length, length),
             cost(stage_flops, 2 * field_bytes),
-        )(got.reshape(-1, 128), table["inverse_receive"])
+        )(*(got.reshape(-1, 128) for got in gots), table["inverse_receive"])
 
     plane_spec = pl.BlockSpec((2, length, length), lambda p: (p, 0, 0))
     send_specs = [
@@ -477,7 +514,7 @@
         def kernel(weights, got, first, second, field, change, *tables_and_outs):
             receive, cosine, mixed, send, main, inner, density = tables_and_outs
             apply_kernel(
-                slab, 3 * rows, 6 * rows, 0, weights, got, Both(first, second), field, change, None,
+                slab, (9 * rows, 12 * rows), 15 * rows, 0, weights, got, Both(first, second), field, change, None,
                 receive, cosine, mixed, send, main, None, inner, density,
             )
 
@@ -498,7 +535,7 @@
         def kernel(weights, got, first, second, field, change, before, *tables_and_outs):
             receive, cosine, mixed, send, main, tail, inner, density = tables_and_outs
             apply_kernel(
-                slab, 0, 3 * rows, 1, weights, got, Both(first, second), field, change, before,
+                slab, (0, 3 * rows), 6 * rows, 1, weights, got, Both(first, second), field, change, before,
                 receive, cosine, mixed, send, main, tail, inner, density,
             )
 
@@ -518,13 +555,13 @@
     space_spec = pl.BlockSpec((2, 2 * length, length), lambda p: (p, 0, 0))
     bands_spec = pl.BlockSpec((1, 2, 2, 2, length, length), lambda p: (0, 0, 0, p, 0, 0))
 
-    def finish(base, got, band, start, stride, tail):
+    def finish(base, got, band, starts, stride, tail):
         lane_block = 1 if tail else 0
         one_spec = pl.BlockSpec(
             (1, 1, 2, 2, length, 128), lambda p: (0, band, 0, p, 0, lane_block)
         )
         return call(
-            functools.partial(finish_kernel, slab, start, stride, tail),
+            functools.partial(finish_kernel, slab, starts, stride, tail),
             "finish",
             pairs,
             [scalars(), whole(), whole(), one_spec],
@@ -536,9 +573,10 @@
 
     field = jnp.transpose(potential, (1, 0, 2))
     change = jnp.transpose(perturbation, (1, 0, 2))
-    got_one = exchange(to_half(orbitals, 0))
-    half_two = to_half(orbitals, 1, None, 0)
-    got_two = exchange(to_half(responses, 0, half_two, 1), got_one)
+    got_one = exchange(to_half(orbitals, 0, 1, 0))
+    half_two = to_half(orbitals, 0, 5, 1)
+    half_two = to_half(orbitals, 1, 5, None, half_two, 1)
+    got_two = exchange(to_half(responses, 0, 5, None, half_two, 3), got_one)
     direct_inner = call(
         functools.partial(inner_kernel, slab),
         "inner",
@@ -548,8 +586,11 @@
         f32(2, 2, 2, 8, length),
         cost(32 * field_bytes, 4 * field_bytes),
     )(me, energies, orbitals, responses)
-    got_last = exchange(to_half(responses, 1), (got_two, direct_inner))
-    spaces = [to_space(got_one, 0, 3 * rows), to_space(got_two, 0, 6 * rows)]
+    got_last = exchange(to_half(responses, 1, 2), (got_two, direct_inner))
+    spaces = [
+        to_space([got_one, got_two], (0, 0), (3 * rows, 15 * rows)),
+        to_space([got_two], (3 * rows, 6 * rows), (15 * rows, 15 * rows)),
+    ]
     send_first, inner_first, before = apply_first(got_two, spaces, field, change)
     back_first = exchange(send_first, got_last)
     last_main, last_tail, inner_last, density = apply_last(
@@ -586,15 +627,17 @@
         mirror_kernel,
         "mirror",
         1,
-        [whole()] * 4,
+        [scalars()] + [whole()] * 4,
         [whole(), whole()],
-        [block_shape, f32(slab, length, 128)],
+        [f32(members, 64, 128), f32(slab, length, 128)],
         cost(4e9, 4e6),
         scratch=[pltpu.VMEM((slab, length, 128), jnp.float32)],
-    )(got_density.reshape(-1, 128), table["loose_mirror"], table["loose_pair"], table["loose_alone"])
+    )(
+        me, got_density.reshape(-1, 128),
+        table["loose_mirror"], table["loose_pair"], table["loose_alone"],
+    )
     got_mirrored = exchange(mirrored, (back_tail, base))
-    base = finish(base, back_first, 0, 0, 3 * rows, False)
-    base = finish(base, back_first, 0, 2 * rows, 3 * rows, True)
+    base = finish(base, back_first, 0, (0, 3 * rows), 6 * rows, False)
     back_main = exchange(last_main, (got_mirrored, base))
     symmetric = call(
         swap_kernel,
@@ -604,18 +647,17 @@
         whole(),
         f32(slab, length, 128),
         cost(1e9, 4e6),
-    )(got_mirrored.reshape(-1, 128), table["loose_order"], natural)
+    )(got_mirrored.reshape(-1, 128), table["swapped"], natural)
     other = lax.ppermute(symmetric, "pool", swap)
     low = jnp.where(pool == 0, symmetric, other)
     high = jnp.where(pool == 0, other, symmetric)
-    response_density = jnp.concatenate(
-        (low[..., :64], high[..., :64], low[..., 64:96], high[..., 64:96]), axis=2
-    )
-    base = finish(base, back_tail, 1, 0, rows, True)
+    response_density = jnp.concatenate((low[..., :96], high[..., :96]), axis=2)
+    base = finish(base, back_first, 0, (2 * rows, 5 * rows), 6 * rows, True)
+    base = finish(base, back_tail, 1, (0, rows), 2 * rows, True)
     base, response_density, back_main = lax.optimization_barrier(
         (base, response_density, back_main)
     )
-    base = finish(base, back_main, 1, 0, 2 * rows, False)
+    base = finish(base, back_main, 1, (0, 2 * rows), 4 * rows, False)
     return base, response_density
 
 

time: 576 us -> 564 us (0.979)
  waiting for transfers between devices: 329 us -> 313 us
    all_to_all x7, waiting for transfers between devices: 289 us -> 280 us  [exchange(): return lax.all_to_all(values, 'pw', split_axis=0, concat_axis=0, tiled=True)]
    ppermute x1, waiting for transfers between devices: 19.7 us -> 12.7 us  [packed_body(): other = lax.ppermute(symmetric, 'pool', swap)]
    pallas_call x11 -> x12, Pallas kernels: 92.4 us -> 96.4 us  [the longest x5 47 us: to_half(): call(kernel, 'to_half', grid, [pl.BlockSpec((1, 1, 2, 2, length, length),...]
  transfers between devices with their start and end apart: 9 -> 9, of which waited for: 9 -> 9; matrix products, arithmetic and copies ran while one was open for 1% -> 1% of each run, Pallas kernels for 27% -> 29%
where the time goes in v3:
time: 564 us; the launch traced here: 563 us
  waiting for transfers between devices  313 us (55%)
  Pallas kernels  175 us (31%)
  starting transfers between devices  38.8 us (7%)
  blocking collectives  26.7 us (5%)
    all_to_all x7, waiting for transfers between devices, exchange(): return lax.all_to_all(values, 'pw', split_axis=0, concat_axis=0, tiled=True)  280 us
    pallas_call x5, Pallas kernels, to_half(): call(kernel, 'to_half', grid, [pl.BlockSpec((1, 1, 2, 2, length, length),...  47 us
    all_to_all x7, starting transfers between devices, exchange(): return lax.all_to_all(values, 'pw', split_axis=0, concat_axis=0, tiled=True)  36.3 us
    pallas_call x4, Pallas kernels, finish(): call(functools.partial(finish_kernel, slab, starts, stride, tail), 'finis...  28.1 us
    all_to_all x1, blocking collectives, exchange(): return lax.all_to_all(values, 'pw', split_axis=0, concat_axis=0, tiled=True)  26.7 us
    pallas_call x1, Pallas kernels, apply_first(): call(kernel, 'apply_first', pairs, [scalars(), whole(), space_spec, space...  23.6 us
    pallas_call x1, Pallas kernels, apply_last(): call(kernel, 'apply_last', pairs, [scalars(), whole(), space_spec, space_...  22.9 us
    ppermute x1, waiting for transfers between devices, packed_body(): lax.ppermute(given, 'pool', swap)  20.4 us
  transfers between devices with their start and end apart: 9, of which 9 were waited for; matrix products, arithmetic and copies ran while one was open for 1% of the time, Pallas kernels for 29%

profile of v3, /device:TPU:13, one launch (start us, length us, event | category | flops | bytes accessed | tf_op | source)
XLA Modules:
  0.0 562.6 jit_solution(14765805319839164471)
XLA Ops:
  0.6 6.7 %to_half.9 = f32[16,3,1,3,24,128]{5,4,3,2,1,0:T(8,128)} custom-call(f32[1,2,2,12,192,192]{5,4,3,2,1,0:T(8,128)} %orbitals.3, bf16[2,192,256]{2,1,0:T(8,128)(2,1)} %constant.41.clone.cosine.tables_and_outs_1_, bf16[2,2,192,256]{3,2,1,0:T(8,128)(2,1)} %constant.42.clone.mixed.tables_and_outs_2_, bf16[2,192,576]{2,1,0:T(8,128)(2,1)} %constant.43.clone.send), custom_call_target="tpu_custom_call" | custom-call | flops 4076863488 | bytes 3538944 | tf_op jit(solution)/shard_map/to_half/pallas_call | solution.py:467
  7.3 6.5 %all-to-all-start = ((f32[16,216,128]{2,1,0:T(8,128)}), f32[16,216,128]{2,1,0:T(8,128)}, u32[]{:S(2)}, u32[]{:S(2)}) async-start(f32[16,216,128]{2,1,0:T(8,128)} %bitcast.27), calls=%async_computation | async-start | bytes 3538944 | tf_op jit(solution)/shard_map/all_to_all | solution.py:453
  13.9 6.7 %to_half.6.rest_0_ = f32[16,3,5,3,24,128]{5,4,3,2,1,0:T(8,128)} custom-call(f32[1,2,2,12,192,192]{5,4,3,2,1,0:T(8,128)} %orbitals.3, bf16[2,192,256]{2,1,0:T(8,128)(2,1)} %constant.41.clone.cosine.tables_and_outs_1_, bf16[2,2,192,256]{3,2,1,0:T(8,128)(2,1)} %constant.42.clone.mixed.tables_and_outs_2_, bf16[2,192,576]{2,1,0:T(8,128)(2,1)} %constant.43.clone.send), custom_call_target="tpu_custom_call" | custom-call | flops 4076863488 | bytes 3538944 | tf_op jit(solution)/shard_map/to_half/pallas_call | solution.py:467
  20.6 11.2 %to_half.7.rest_0_ = f32[16,3,5,3,24,128]{5,4,3,2,1,0:T(8,128)} custom-call(f32[1,2,2,12,192,192]{5,4,3,2,1,0:T(8,128)} %orbitals.3, bf16[2,192,256]{2,1,0:T(8,128)(2,1)} %constant.41.clone.cosine.tables_and_outs_1_, bf16[2,2,192,256]{3,2,1,0:T(8,128)(2,1)} %constant.42.clone.mixed.tables_and_outs_2_, ...), custom_call_target="tpu_custom_call", output_to_operand_aliasing={{}: (4, {})} | custom-call | flops 8153726976 | bytes 7077888 | tf_op jit(solution)/shard_map/to_half/pallas_call | solution.py:467
  31.8 11.2 %to_half.8 = f32[16,3,5,3,24,128]{5,4,3,2,1,0:T(8,128)} custom-call(f32[1,2,2,12,192,192]{5,4,3,2,1,0:T(8,128)} %responses.3, bf16[2,192,256]{2,1,0:T(8,128)(2,1)} %constant.41.clone.cosine.tables_and_outs_1_, bf16[2,2,192,256]{3,2,1,0:T(8,128)(2,1)} %constant.42.clone.mixed.tables_and_outs_2_, ...), custom_call_target="tpu_custom_call", output_to_operand_aliasing={{}: (4, {})} | custom-call | flops 8153726976 | bytes 7077888 | tf_op jit(solution)/shard_map/to_half/pallas_call | solution.py:467
  43.0 11.4 %all-to-all-done = f32[16,216,128]{2,1,0:T(8,128)} async-done(((f32[16,216,128]{2,1,0:T(8,128)}), f32[16,216,128]{2,1,0:T(8,128)}, u32[]{:S(2)}, u32[]{:S(2)}) %all-to-all-start) | async-done | bytes 1769504 | tf_op jit(solution)/shard_map/all_to_all | solution.py:453
  54.4 4.9 all-to-all-start.1
  59.3 10.1 %inner.1 = f32[2,2,2,8,192]{4,3,2,1,0:T(8,128)} custom-call(s32[1]{0:T(128)} %bitcast.me, f32[1,2]{1,0:T(1,128)} %energies.3, f32[1,2,2,12,192,192]{5,4,3,2,1,0:T(8,128)} %orbitals.3, f32[1,2,2,12,192,192]{5,4,3,2,1,0:T(8,128)} %responses.3), custom_call_target="tpu_custom_call" | custom-call | flops 113246208 | bytes 14155776 | tf_op jit(solution)/shard_map/inner/pallas_call | solution.py:580
  69.4 11.2 %to_half.5 = f32[16,3,2,3,24,128]{5,4,3,2,1,0:T(8,128)} custom-call(f32[1,2,2,12,192,192]{5,4,3,2,1,0:T(8,128)} %responses.3, bf16[2,192,256]{2,1,0:T(8,128)(2,1)} %constant.41.clone.cosine.tables_and_outs_1_, bf16[2,2,192,256]{3,2,1,0:T(8,128)(2,1)} %constant.42.clone.mixed.tables_and_outs_2_, bf16[2,192,576]{2,1,0:T(8,128)(2,1)} %constant.43.clone.send), custom_call_target="tpu_custom_call" | custom-call | flops 8153726976 | bytes 7077888 | tf_op jit(solution)/shard_map/to_half/pallas_call | solution.py:467
  80.7 170.8 %all-to-all-done.1 = f32[16,1080,128]{2,1,0:T(8,128)} async-done(((f32[16,1080,128]{2,1,0:T(8,128)}), f32[16,1080,128]{2,1,0:T(8,128)}, u32[]{:S(2)}, u32[]{:S(2)}) %all-to-all-start.1) | async-done | bytes 8847392 | tf_op jit(solution)/shard_map/all_to_all | solution.py:453
  251.5 4.9 all-to-all-start.2
  257.0 8.5 %to_space.3.second = f32[12,384,192]{2,1,0:T(8,128)} custom-call(f32[17280,128]{1,0:T(8,128)} %bitcast.6.refs_1_.refs_0_.got, bf16[2,192,576]{2,1,0:T(8,128)(2,1)} %constant.44.clone.refs_2_.refs_1_.tables_and_outs_0_), custom_call_target="tpu_custom_call" | custom-call | flops 4076863488 | bytes 7077888 | tf_op jit(solution)/shard_map/to_space/pallas_call | solution.py:491
  265.5 8.9 %to_space.2.first = f32[12,384,192]{2,1,0:T(8,128)} custom-call(f32[3456,128]{1,0:T(8,128)} %bitcast.5.refs_0_, f32[17280,128]{1,0:T(8,128)} %bitcast.6.refs_1_.refs_0_.got, bf16[2,192,576]{2,1,0:T(8,128)(2,1)} %constant.44.clone.refs_2_.refs_1_.tables_and_outs_0_), custom_call_target="tpu_custom_call" | custom-call | flops 4076863488 | bytes 7077888 | tf_op jit(solution)/shard_map/to_space/pallas_call | solution.py:491
  274.4 23.6 %apply_first.1 = (f32[16,6,3,24,128]{4,3,2,1,0:T(8,128)}, f32[2,2,8,192]{3,2,1,0:T(8,128)}, f32[12,192,192]{2,1,0:T(8,128)}) custom-call(f32[1]{0:T(128)S(6)} %copy.36.weights, f32[17280,128]{1,0:T(8,128)} %bitcast.6.refs_1_.refs_0_.got, f32[12,384,192]{2,1,0:T(8,128)} %to_space.2.first, f32[12,384,192]{2,1,0:T(8,128)} %to_space.3.second, ...), custom_call_target="tpu_custom_call" | custom-call | flops 12230590464 | bytes 17694720 | tf_op jit(solution)/shard_map/apply_first/pallas_call | solution.py:521
  298.0 36.8 %all-to-all-done.2 = f32[16,432,128]{2,1,0:T(8,128)} async-done(((f32[16,432,128]{2,1,0:T(8,128)}), f32[16,432,128]{2,1,0:T(8,128)}, u32[]{:S(2)}, u32[]{:S(2)}) %all-to-all-start.2) | async-done | bytes 3538976 | tf_op jit(solution)/shard_map/all_to_all | solution.py:453
  334.8 4.9 all-to-all-start.3
  339.7 22.9 %apply_last.1 = (f32[16,6,2,24,128]{4,3,2,1,0:T(8,128)}, f32[16,6,24,128]{3,2,1,0:T(8,128)}, f32[2,2,8,192]{3,2,1,0:T(8,128)}, f32[12,192,192]{2,1,0:T(8,128)}) custom-call(f32[1]{0:T(128)S(6)} %copy.36.weights, f32[6912,128]{1,0:T(8,128)} %bitcast.4.got, f32[12,384,192]{2,1,0:T(8,128)} %to_space.2.first, f32[12,384,192]{2,1,0:T(8,128)} %to_space.3.second, ...), custom_call_target="tpu_custom_call" | custom-call | flops 12230590464 | bytes 17694720 | tf_op jit(solution)/shard_map/apply_last/pallas_call | solution.py:542
  362.6 0.0 copy-start.2
  362.6 0.0 copy-start.3
  362.6 0.0 copy-start.4
  362.6 5.3 pack.1
  367.9 1.2 collective-permute-start
  369.1 0.0 copy-done.2
  369.1 0.0 copy-done.3
  369.1 0.0 copy-done.4
  369.1 0.1 fusion
  369.2 0.1 copy.28
  369.4 0.1 reshape.71
  369.4 20.4 %collective-permute-done = f32[16,112,128]{2,1,0:T(8,128)S(1)} collective-permute-done((f32[16,112,128]{2,1,0:T(8,128)}, f32[16,112,128]{2,1,0:T(8,128)S(1)}, u32[]{:S(2)}, u32[]{:S(2)}) %collective-permute-start) | collective-permute-done | bytes 917536 | tf_op jit(solution)/shard_map/ppermute | solution.py:613
  389.8 1.3 add_select_fusion
  391.1 27.0 %all-to-all-done.3 = f32[16,432,128]{2,1,0:T(8,128)} async-done(((f32[16,432,128]{2,1,0:T(8,128)}), f32[16,432,128]{2,1,0:T(8,128)}, u32[]{:S(2)}, u32[]{:S(2)}) %all-to-all-start.3) | async-done | bytes 3538976 | tf_op jit(solution)/shard_map/all_to_all | solution.py:453
  418.1 26.7 %all_to_all.40 = f32[16,112,128]{2,1,0:T(8,128)S(1)} all-to-all(f32[16,112,128]{2,1,0:T(8,128)S(1)} %add_select_fusion), channel_id=1, replica_groups=mesh['pool'=2,'pw'=16] {'pw'}, dimensions={0} | all-to-all | bytes 1835008 | tf_op jit(solution)/shard_map/all_to_all | solution.py:453
  444.9 0.0 copy-start
  444.9 5.0 all-to-all-start.5
  449.9 0.7 reshape.75.inner
  450.6 12.3 %direct.1.base = f32[1,2,2,12,192,192]{5,4,3,2,1,0:T(8,128)} custom-call(s32[1]{0:T(128)} %bitcast.me, f32[1,2]{1,0:T(1,128)} %energies.3, f32[2,2,2]{2,1,0:T(2,128)} %reshape.75.inner, f32[1,2,2,12,192,192]{5,4,3,2,1,0:T(8,128)} %orbitals.3, f32[1,2,2,12,192,192]{5,4,3,2,1,0:T(8,128)} %responses.3), custom_call_target="tpu_custom_call" | custom-call | flops 113246208 | bytes 21233664 | tf_op jit(solution)/shard_map/direct/pallas_call | solution.py:617
  462.9 0.0 copy-done
  462.9 3.9 mirror.1
  466.8 11.0 %all-to-all-done.5 = f32[16,144,128]{2,1,0:T(8,128)} async-done(((f32[16,144,128]{2,1,0:T(8,128)}), f32[16,144,128]{2,1,0:T(8,128)}, u32[]{:S(2)}, u32[]{:S(2)}) %all-to-all-start.5) | async-done | bytes 1179680 | tf_op jit(solution)/shard_map/all_to_all | solution.py:453
  477.7 4.9 all-to-all-start.6
  482.6 7.2 %finish.4.base = f32[1,2,2,12,192,192]{5,4,3,2,1,0:T(8,128)} custom-call(s32[1]{0:T(128)} %bitcast.me, f32[6912,128]{1,0:T(8,128)} %bitcast.16.got, bf16[2,192,576]{2,1,0:T(8,128)(2,1)} %constant.46.clone.receive, f32[1,2,2,12,192,192]{5,4,3,2,1,0:T(8,128)} %direct.1.base), custom_call_target="tpu_custom_call", output_to_operand_aliasing={{}: (3, {})} | custom-call | flops 4076863488 | bytes 7077888 | tf_op jit(solution)/shard_map/finish/pallas_call | solution.py:563
  489.8 6.4 %all-to-all-done.6 = f32[16,64,128]{2,1,0:T(8,128)S(1)} async-done(((f32[16,64,128]{2,1,0:T(8,128)}), f32[16,64,128]{2,1,0:T(8,128)S(1)}, u32[]{:S(2)}, u32[]{:S(2)}) %all-to-all-start.6) | async-done | bytes 524320 | tf_op jit(solution)/shard_map/all_to_all | solution.py:453
  496.2 0.0 copy-start.1
  496.2 0.8 copy-done.1
  497.0 5.2 all-to-all-start.7
  502.2 4.8 swap.1
  507.0 1.2 collective-permute-start.1
  508.2 7.2 %finish.5.base = f32[1,2,2,12,192,192]{5,4,3,2,1,0:T(8,128)} custom-call(s32[1]{0:T(128)} %bitcast.me, f32[6912,128]{1,0:T(8,128)} %bitcast.16.got, bf16[2,192,576]{2,1,0:T(8,128)(2,1)} %constant.46.clone.receive, f32[1,2,2,12,192,192]{5,4,3,2,1,0:T(8,128)} %finish.4.base), custom_call_target="tpu_custom_call", output_to_operand_aliasing={{}: (3, {})} | custom-call | flops 4076863488 | bytes 7077888 | tf_op jit(solution)/shard_map/finish/pallas_call | solution.py:563
  515.4 6.5 %finish.6.base = f32[1,2,2,12,192,192]{5,4,3,2,1,0:T(8,128)} custom-call(s32[1]{0:T(128)} %bitcast.me, f32[2304,128]{1,0:T(8,128)} %bitcast.15.got, bf16[2,192,576]{2,1,0:T(8,128)(2,1)} %constant.46.clone.receive, f32[1,2,2,12,192,192]{5,4,3,2,1,0:T(8,128)} %finish.5.base), custom_call_target="tpu_custom_call", output_to_operand_aliasing={{}: (3, {})} | custom-call | flops 4076863488 | bytes 7077888 | tf_op jit(solution)/shard_map/finish/pallas_call | solution.py:563
  521.8 12.7 %collective-permute-done.1 = f32[12,192,128]{2,1,0:T(8,128)} collective-permute-done((f32[12,192,128]{2,1,0:T(8,128)}, f32[12,192,128]{2,1,0:T(8,128)}, u32[]{:S(2)}, u32[]{:S(2)}) %collective-permute-start.1) | collective-permute-done | bytes 1179680 | tf_op jit(solution)/shard_map/ppermute | solution.py:651
  534.5 1.8 slice_select_fusion.1
  536.3 2.1 pad_maximum_fusion
  538.4 17.0 %all-to-all-done.7 = f32[16,288,128]{2,1,0:T(8,128)} async-done(((f32[16,288,128]{2,1,0:T(8,128)}), f32[16,288,128]{2,1,0:T(8,128)}, u32[]{:S(2)}, u32[]{:S(2)}) %all-to-all-start.7) | async-done | bytes 2359328 | tf_op jit(solution)/shard_map/all_to_all | solution.py:453
  555.4 7.2 %finish.7 = f32[1,2,2,12,192,192]{5,4,3,2,1,0:T(8,128)} custom-call(s32[1]{0:T(128)} %bitcast.me, f32[4608,128]{1,0:T(8,128)} %bitcast.21.got, bf16[2,192,576]{2,1,0:T(8,128)(2,1)} %constant.46.clone.receive, f32[1,2,2,12,192,192]{5,4,3,2,1,0:T(8,128)} %finish.6.base), custom_call_target="tpu_custom_call", output_to_operand_aliasing={{}: (3, {})} | custom-call | flops 4076863488 | bytes 7077888 | tf_op jit(solution)/shard_map/finish/pallas_call | solution.py:563
  (3 shorter events, 0.0 us)
Async XLA Ops:
  7.3 47.0 %all-to-all-start = ((f32[16,216,128]{2,1,0:T(8,128)}), f32[16,216,128]{2,1,0:T(8,128)}, u32[]{:S(2)}, u32[]{:S(2)}) async-start(f32[16,216,128]{2,1,0:T(8,128)} %bitcast.27), calls=%async_computation | async-start | bytes 3538944 | tf_op jit(solution)/shard_map/all_to_all | solution.py:453
  54.4 197.1 %all-to-all-start.1 = ((f32[16,1080,128]{2,1,0:T(8,128)}), f32[16,1080,128]{2,1,0:T(8,128)}, u32[]{:S(2)}, u32[]{:S(2)}) async-start(f32[16,1080,128]{2,1,0:T(8,128)} %bitcast.23), calls=%async_computation.1 | async-start | bytes 17694720 | tf_op jit(solution)/shard_map/all_to_all | solution.py:453
  251.5 83.3 %all-to-all-start.2 = ((f32[16,432,128]{2,1,0:T(8,128)}), f32[16,432,128]{2,1,0:T(8,128)}, u32[]{:S(2)}, u32[]{:S(2)}) async-start(f32[16,432,128]{2,1,0:T(8,128)} %bitcast.25), calls=%async_computation.2 | async-start | bytes 7077888 | tf_op jit(solution)/shard_map/all_to_all | solution.py:453
  334.8 83.3 %all-to-all-start.3 = ((f32[16,432,128]{2,1,0:T(8,128)}), f32[16,432,128]{2,1,0:T(8,128)}, u32[]{:S(2)}, u32[]{:S(2)}) async-start(f32[16,432,128]{2,1,0:T(8,128)} %bitcast.24), calls=%async_computation.3 | async-start | bytes 7077888 | tf_op jit(solution)/shard_map/all_to_all | solution.py:453
  362.6 6.5 %copy-start.2 = (f32[2,2,2,8,192]{4,3,2,1,0:T(8,128)S(1)}, f32[2,2,2,8,192]{4,3,2,1,0:T(8,128)}, u32[]{:S(2)}) copy-start(f32[2,2,2,8,192]{4,3,2,1,0:T(8,128)} %inner.1) | copy-start | bytes 147460
  362.6 6.5 %copy-start.3 = (f32[2,2,8,192]{3,2,1,0:T(8,128)S(1)}, f32[2,2,8,192]{3,2,1,0:T(8,128)}, u32[]{:S(2)}) copy-start(f32[2,2,8,192]{3,2,1,0:T(8,128)} %get-tuple-element.30) | copy-start | bytes 73732
  362.6 6.5 %copy-start.4 = (f32[2,2,8,192]{3,2,1,0:T(8,128)S(1)}, f32[2,2,8,192]{3,2,1,0:T(8,128)}, u32[]{:S(2)}) copy-start(f32[2,2,8,192]{3,2,1,0:T(8,128)} %get-tuple-element.31) | copy-start | bytes 73732
  367.9 21.9 %collective-permute-start = (f32[16,112,128]{2,1,0:T(8,128)}, f32[16,112,128]{2,1,0:T(8,128)S(1)}, u32[]{:S(2)}, u32[]{:S(2)}) collective-permute-start(f32[16,112,128]{2,1,0:T(8,128)} %get-tuple-element.29), channel_id=1, source_target_pairs={{0,16},{16,0},{1,17},{17,1},{2,18},{18,2},{3,19},{19,3},{4,20},{20... | collective-permute-start | bytes 2752520 | tf_op jit(solution)/shard_map/ppermute | solution.py:613
  444.9 18.0 %copy-start = (f32[16,112,128]{2,1,0:T(8,128)}, f32[16,112,128]{2,1,0:T(8,128)S(1)}, u32[]{:S(2)}) copy-start(f32[16,112,128]{2,1,0:T(8,128)S(1)} %all_to_all.40) | copy-start | bytes 2752516
  444.9 32.9 %all-to-all-start.5 = ((f32[16,144,128]{2,1,0:T(8,128)}), f32[16,144,128]{2,1,0:T(8,128)}, u32[]{:S(2)}, u32[]{:S(2)}) async-start(f32[16,144,128]{2,1,0:T(8,128)} %bitcast.9), calls=%async_computation.5 | async-start | bytes 2359296 | tf_op jit(solution)/shard_map/all_to_all | solution.py:453
  477.7 18.5 %all-to-all-start.6 = ((f32[16,64,128]{2,1,0:T(8,128)}), f32[16,64,128]{2,1,0:T(8,128)S(1)}, u32[]{:S(2)}, u32[]{:S(2)}) async-start(f32[16,64,128]{2,1,0:T(8,128)} %get-tuple-element.37), calls=%async_computation.6 | async-start | bytes 1048576 | tf_op jit(solution)/shard_map/all_to_all | solution.py:453
  496.2 0.8 copy-start.1
  497.0 58.3 %all-to-all-start.7 = ((f32[16,288,128]{2,1,0:T(8,128)}), f32[16,288,128]{2,1,0:T(8,128)}, u32[]{:S(2)}, u32[]{:S(2)}) async-start(f32[16,288,128]{2,1,0:T(8,128)} %bitcast.26), calls=%async_computation.7 | async-start | bytes 4718592 | tf_op jit(solution)/shard_map/all_to_all | solution.py:453
  507.0 27.5 %collective-permute-start.1 = (f32[12,192,128]{2,1,0:T(8,128)}, f32[12,192,128]{2,1,0:T(8,128)}, u32[]{:S(2)}, u32[]{:S(2)}) collective-permute-start(f32[12,192,128]{2,1,0:T(8,128)} %swap.1), channel_id=1, source_target_pairs={{0,16},{16,0},{1,17},{17,1},{2,18},{18,2},{3,19},{19,3},{4,20},{20... | collective-permute-start | bytes 3538952 | tf_op jit(solution)/shard_map/ppermute | solution.py:651

commit v4 on v3

--- a/solution.py
+++ b/solution.py
@@ -118,8 +118,7 @@
 
 def dot_mirror(table, values):
     high, low = halves(values)
-    low_rest = (values - high.astype(jnp.float32) - low.astype(jnp.float32)).astype(jnp.bfloat16)
-    return dot(table, high) + (dot(table, low) + dot(table, low_rest))
+    return dot(table, high) + dot(table, low)
 
 
 def merge_tails(first, second):
@@ -275,10 +274,10 @@
     out[:, 12 * len(blocks) - 12 :] = dot_mirror(alone[...], blocks[-1]).reshape(members, 16, 128)
 
 
-def unpack(got, place, count, width, rows):
+def unpack(got, place, count, width, rows, row_at=lambda row: row):
     members = got.shape[0] // rows
     blocks = [
-        received(got, 12 * block + place, rows, members)
+        received(got, row_at(12 * block + place), rows, members)
         for block in range(-(-count * width // 128))
     ]
     found = []
@@ -361,25 +360,29 @@
 
 
 def finish_kernel(slab, starts, stride, tail, me, got, receive, base, out):
-    length = base.shape[4]
-    first = 2 * pl.program_id(0)
+    length, count = base.shape[4], base.shape[3]
     parts_of = [(got, start, stride) for start in starts]
-    planes = [plane(parts_of, first + one, slab, not tail, tail) for one in range(2)]
-    values = [jnp.concatenate(both, axis=1) for both in zip(*planes)]
-    applied = dot_receive(receive, values)
-    for one in range(2):
-        kinetic = frequencies(length, me[0] * slab + first + one, 128, 128 if tail else 0)
-        inverse = 1.0 / (1.0 + kinetic)
-        for part in range(2):
-            piece = applied[part][:, 128 * one : 128 * (one + 1)]
-            out[0, 0, part, one] = base[0, 0, part, one] - piece * inverse
-
-
-def mirror_kernel(me, got, single, pair, alone, out, natural, loose):
+    for pair in range(0, count, 2):
+        first = count * pl.program_id(0) + pair
+        planes = [plane(parts_of, first + one, slab, not tail, tail) for one in range(2)]
+        values = [jnp.concatenate(both, axis=1) for both in zip(*planes)]
+        applied = dot_receive(receive, values)
+        for one in range(2):
+            kinetic = frequencies(length, me[0] * slab + first + one, 128, 128 if tail else 0)
+            inverse = 1.0 / (1.0 + kinetic)
+            for part in range(2):
+                piece = applied[part][:, 128 * one : 128 * (one + 1)]
+                out[0, 0, part, pair + one] = base[0, 0, part, pair + one] - piece * inverse
+
+
+def mixed_row(row):
+    return row // 40 * 88 + 48 + row % 40
+
+
+def mirror_kernel(me, got, pair, alone, out, loose):
     below = me[0] < out.shape[0] // 2
     for place in range(12):
-        loose[place] = unpack(got, place, 12, 96, 112)
-        natural[place] = dot_mirror(single[...], loose[place])
+        loose[place] = unpack(got, place, 12, 96, 264, mixed_row)
 
     def planes(place):
         values = loose[place % 12]
@@ -389,13 +392,14 @@
     pack(planes, 13, 48, pair, alone, out)
 
 
-def swap_kernel(got, order, natural, out):
-    length = natural.shape[1]
+def swap_kernel(got, got_swapped, single, order, out):
+    length = out.shape[1]
     for place in range(12):
-        halves_of = dot_mirror(order[...], unpack(got, place, 13, 48, 64))
+        own = dot_mirror(single[...], unpack(got, place, 12, 96, 264, mixed_row))
+        halves_of = dot_mirror(order[...], unpack(got_swapped, place, 13, 48, 64))
         low, high = halves_of[:length], moved(halves_of[length:], 48)
         swapped = jnp.where(lanes_of(low) < 48, low, high)
-        out[place] = (natural[place] + swapped) * 0.125
+        out[place] = (own + swapped) * 0.125
 
 
 def cost(flops, moved):
@@ -558,12 +562,12 @@
     def finish(base, got, band, starts, stride, tail):
         lane_block = 1 if tail else 0
         one_spec = pl.BlockSpec(
-            (1, 1, 2, 2, length, 128), lambda p: (0, band, 0, p, 0, lane_block)
+            (1, 1, 2, slab // 2, length, 128), lambda p: (0, band, 0, p, 0, lane_block)
         )
         return call(
             functools.partial(finish_kernel, slab, starts, stride, tail),
             "finish",
-            pairs,
+            2,
             [scalars(), whole(), whole(), one_spec],
             one_spec,
             f32(*base.shape),
@@ -611,9 +615,10 @@
     riding = jnp.pad(riding, ((0, 0), (0, 0), (0, 120)))
     row = lax.broadcasted_iota(jnp.int32, block_shape.shape, 1)
     summed = jnp.where(row < 108, kept + lax.ppermute(given, "pool", swap), riding)
-    got_density = exchange(summed, back_first)
-    inner = jnp.sum(got_density[:, 108, :8], axis=0).reshape(2, 2, 2)
-    back_tail = exchange(last_tail, got_density)
+    summed = jnp.pad(summed, ((0, 0), (0, 8), (0, 0))).reshape(members, 3, 40, 128)
+    mixed = jnp.concatenate((last_tail.reshape(members, 3, 48, 128), summed), axis=2)
+    got_mixed = exchange(mixed, back_first)
+    inner = jnp.sum(got_mixed[:, mixed_row(108), :8], axis=0).reshape(2, 2, 2)
     base = call(
         functools.partial(direct_kernel, slab),
         "direct",
@@ -623,37 +628,37 @@
         f32(*responses.shape),
         cost(32 * field_bytes, 6 * field_bytes),
     )(me, energies, inner, orbitals, responses)
-    mirrored, natural = call(
+    mirrored = call(
         mirror_kernel,
         "mirror",
         1,
-        [scalars()] + [whole()] * 4,
-        [whole(), whole()],
-        [f32(members, 64, 128), f32(slab, length, 128)],
-        cost(4e9, 4e6),
+        [scalars()] + [whole()] * 3,
+        whole(),
+        f32(members, 64, 128),
+        cost(2e9, 3e6),
         scratch=[pltpu.VMEM((slab, length, 128), jnp.float32)],
-    )(
-        me, got_density.reshape(-1, 128),
-        table["loose_mirror"], table["loose_pair"], table["loose_alone"],
-    )
-    got_mirrored = exchange(mirrored, (back_tail, base))
+    )(me, got_mixed.reshape(-1, 128), table["loose_pair"], table["loose_alone"])
+    got_mirrored = exchange(mirrored)
     base = finish(base, back_first, 0, (0, 3 * rows), 6 * rows, False)
-    back_main = exchange(last_main, (got_mirrored, base))
+    back_main = exchange(last_main, got_mirrored)
     symmetric = call(
         swap_kernel,
         "swap",
         1,
-        [whole()] * 3,
+        [whole()] * 4,
         whole(),
         f32(slab, length, 128),
-        cost(1e9, 4e6),
-    )(got_mirrored.reshape(-1, 128), table["swapped"], natural)
+        cost(2e9, 5e6),
+    )(
+        got_mixed.reshape(-1, 128), got_mirrored.reshape(-1, 128),
+        table["loose_mirror"], table["swapped"],
+    )
     other = lax.ppermute(symmetric, "pool", swap)
     low = jnp.where(pool == 0, symmetric, other)
     high = jnp.where(pool == 0, other, symmetric)
     response_density = jnp.concatenate((low[..., :96], high[..., :96]), axis=2)
     base = finish(base, back_first, 0, (2 * rows, 5 * rows), 6 * rows, True)
-    base = finish(base, back_tail, 1, (0, rows), 2 * rows, True)
+    base = finish(base, got_mixed, 1, (0, rows), 88, True)
     base, response_density, back_main = lax.optimization_barrier(
         (base, response_density, back_main)
     )

time: 564 us -> 561 us (level)
  blocking collectives: 26.7 us -> 73.6 us
  waiting for transfers between devices: 313 us -> 280 us
  starting transfers between devices: 38.8 us -> 28.9 us
  Pallas kernels: 175 us -> 168 us
    all_to_all x1 -> x2, blocking collectives: 26.7 us -> 73.6 us  [exchange(): return lax.all_to_all(values, 'pw', split_axis=0, concat_axis=0, tiled=True)]
    all_to_all x7 -> x5, waiting for transfers between devices: 280 us -> 260 us  [exchange(): return lax.all_to_all(values, 'pw', split_axis=0, concat_axis=0, tiled=True)]
    ppermute x1, waiting for transfers between devices: 12.7 us -> 0.01 us  [packed_body(): other = lax.ppermute(symmetric, 'pool', swap)]
    all_to_all x7 -> x5, starting transfers between devices: 36.3 us -> 26.5 us  [exchange(): return lax.all_to_all(values, 'pw', split_axis=0, concat_axis=0, tiled=True)]
    pallas_call x4, Pallas kernels: 28.1 us -> 20.6 us  [finish(): call(functools.partial(finish_kernel, slab, starts, stride, tail), 'finis...]
  transfers between devices with their start and end apart: 9 -> 7, of which waited for: 9 -> 6; matrix products, arithmetic and copies ran while one was open for 1% -> 1% of each run, Pallas kernels for 29% -> 27%
where the time goes in v4:
time: 561 us; the launch traced here: 560 us
  waiting for transfers between devices  280 us (50%)
  Pallas kernels  168 us (30%)
  blocking collectives  73.6 us (13%)
  starting transfers between devices  28.9 us (5%)
  other arithmetic  6.33 us (1%)
    all_to_all x5, waiting for transfers between devices, exchange(): return lax.all_to_all(values, 'pw', split_axis=0, concat_axis=0, tiled=True)  260 us
    all_to_all x2, blocking collectives, exchange(): return lax.all_to_all(values, 'pw', split_axis=0, concat_axis=0, tiled=True)  73.6 us
    pallas_call x5, Pallas kernels, to_half(): call(kernel, 'to_half', grid, [pl.BlockSpec((1, 1, 2, 2, length, length),...  47 us
    all_to_all x5, starting transfers between devices, exchange(): return lax.all_to_all(values, 'pw', split_axis=0, concat_axis=0, tiled=True)  26.5 us
    pallas_call x1, Pallas kernels, apply_first(): call(kernel, 'apply_first', pairs, [scalars(), whole(), space_spec, space...  23.6 us
    pallas_call x1, Pallas kernels, apply_last(): call(kernel, 'apply_last', pairs, [scalars(), whole(), space_spec, space_...  22.9 us
    pallas_call x4, Pallas kernels, finish(): call(functools.partial(finish_kernel, slab, starts, stride, tail), 'finis...  20.6 us
    ppermute x1, waiting for transfers between devices, packed_body(): lax.ppermute(given, 'pool', swap)  20.4 us
  transfers between devices with their start and end apart: 7, of which 6 were waited for; matrix products, arithmetic and copies ran while one was open for 1% of the time, Pallas kernels for 27%

profile of v4, /device:TPU:13, one launch (start us, length us, event | category | flops | bytes accessed | tf_op | source)
XLA Modules:
  0.0 559.7 jit_solution(13702129883241012528)
XLA Ops:
  0.6 6.7 %to_half.9 = f32[16,3,1,3,24,128]{5,4,3,2,1,0:T(8,128)} custom-call(f32[1,2,2,12,192,192]{5,4,3,2,1,0:T(8,128)} %orbitals.3, bf16[2,192,256]{2,1,0:T(8,128)(2,1)} %constant.41.clone.cosine.tables_and_outs_1_, bf16[2,2,192,256]{3,2,1,0:T(8,128)(2,1)} %constant.42.clone.mixed.tables_and_outs_2_, bf16[2,192,576]{2,1,0:T(8,128)(2,1)} %constant.43.clone.send), custom_call_target="tpu_custom_call" | custom-call | flops 4076863488 | bytes 3538944 | tf_op jit(solution)/shard_map/to_half/pallas_call | solution.py:471
  7.3 6.5 %all-to-all-start = ((f32[16,216,128]{2,1,0:T(8,128)}), f32[16,216,128]{2,1,0:T(8,128)}, u32[]{:S(2)}, u32[]{:S(2)}) async-start(f32[16,216,128]{2,1,0:T(8,128)} %bitcast.33), calls=%async_computation | async-start | bytes 3538944 | tf_op jit(solution)/shard_map/all_to_all | solution.py:457
  13.9 6.7 %to_half.6.rest_0_ = f32[16,3,5,3,24,128]{5,4,3,2,1,0:T(8,128)} custom-call(f32[1,2,2,12,192,192]{5,4,3,2,1,0:T(8,128)} %orbitals.3, bf16[2,192,256]{2,1,0:T(8,128)(2,1)} %constant.41.clone.cosine.tables_and_outs_1_, bf16[2,2,192,256]{3,2,1,0:T(8,128)(2,1)} %constant.42.clone.mixed.tables_and_outs_2_, bf16[2,192,576]{2,1,0:T(8,128)(2,1)} %constant.43.clone.send), custom_call_target="tpu_custom_call" | custom-call | flops 4076863488 | bytes 3538944 | tf_op jit(solution)/shard_map/to_half/pallas_call | solution.py:471
  20.6 11.2 %to_half.7.rest_0_ = f32[16,3,5,3,24,128]{5,4,3,2,1,0:T(8,128)} custom-call(f32[1,2,2,12,192,192]{5,4,3,2,1,0:T(8,128)} %orbitals.3, bf16[2,192,256]{2,1,0:T(8,128)(2,1)} %constant.41.clone.cosine.tables_and_outs_1_, bf16[2,2,192,256]{3,2,1,0:T(8,128)(2,1)} %constant.42.clone.mixed.tables_and_outs_2_, ...), custom_call_target="tpu_custom_call", output_to_operand_aliasing={{}: (4, {})} | custom-call | flops 8153726976 | bytes 7077888 | tf_op jit(solution)/shard_map/to_half/pallas_call | solution.py:471
  31.8 11.2 %to_half.8 = f32[16,3,5,3,24,128]{5,4,3,2,1,0:T(8,128)} custom-call(f32[1,2,2,12,192,192]{5,4,3,2,1,0:T(8,128)} %responses.3, bf16[2,192,256]{2,1,0:T(8,128)(2,1)} %constant.41.clone.cosine.tables_and_outs_1_, bf16[2,2,192,256]{3,2,1,0:T(8,128)(2,1)} %constant.42.clone.mixed.tables_and_outs_2_, ...), custom_call_target="tpu_custom_call", output_to_operand_aliasing={{}: (4, {})} | custom-call | flops 8153726976 | bytes 7077888 | tf_op jit(solution)/shard_map/to_half/pallas_call | solution.py:471
  43.0 11.4 %all-to-all-done = f32[16,216,128]{2,1,0:T(8,128)} async-done(((f32[16,216,128]{2,1,0:T(8,128)}), f32[16,216,128]{2,1,0:T(8,128)}, u32[]{:S(2)}, u32[]{:S(2)}) %all-to-all-start) | async-done | bytes 1769504 | tf_op jit(solution)/shard_map/all_to_all | solution.py:457
  54.4 4.9 all-to-all-start.1
  59.3 10.1 %inner.1 = f32[2,2,2,8,192]{4,3,2,1,0:T(8,128)} custom-call(s32[1]{0:T(128)} %bitcast.me, f32[1,2]{1,0:T(1,128)} %energies.3, f32[1,2,2,12,192,192]{5,4,3,2,1,0:T(8,128)} %orbitals.3, f32[1,2,2,12,192,192]{5,4,3,2,1,0:T(8,128)} %responses.3), custom_call_target="tpu_custom_call" | custom-call | flops 113246208 | bytes 14155776 | tf_op jit(solution)/shard_map/inner/pallas_call | solution.py:584
  69.4 11.2 %to_half.5 = f32[16,3,2,3,24,128]{5,4,3,2,1,0:T(8,128)} custom-call(f32[1,2,2,12,192,192]{5,4,3,2,1,0:T(8,128)} %responses.3, bf16[2,192,256]{2,1,0:T(8,128)(2,1)} %constant.41.clone.cosine.tables_and_outs_1_, bf16[2,2,192,256]{3,2,1,0:T(8,128)(2,1)} %constant.42.clone.mixed.tables_and_outs_2_, bf16[2,192,576]{2,1,0:T(8,128)(2,1)} %constant.43.clone.send), custom_call_target="tpu_custom_call" | custom-call | flops 8153726976 | bytes 7077888 | tf_op jit(solution)/shard_map/to_half/pallas_call | solution.py:471
  80.7 170.8 %all-to-all-done.1 = f32[16,1080,128]{2,1,0:T(8,128)} async-done(((f32[16,1080,128]{2,1,0:T(8,128)}), f32[16,1080,128]{2,1,0:T(8,128)}, u32[]{:S(2)}, u32[]{:S(2)}) %all-to-all-start.1) | async-done | bytes 8847392 | tf_op jit(solution)/shard_map/all_to_all | solution.py:457
  251.5 4.9 all-to-all-start.2
  257.0 8.6 %to_space.3.second = f32[12,384,192]{2,1,0:T(8,128)} custom-call(f32[17280,128]{1,0:T(8,128)} %bitcast.6.refs_1_.refs_0_.got, bf16[2,192,576]{2,1,0:T(8,128)(2,1)} %constant.44.clone.refs_2_.refs_1_.tables_and_outs_0_), custom_call_target="tpu_custom_call" | custom-call | flops 4076863488 | bytes 7077888 | tf_op jit(solution)/shard_map/to_space/pallas_call | solution.py:495
  265.6 8.9 %to_space.2.first = f32[12,384,192]{2,1,0:T(8,128)} custom-call(f32[3456,128]{1,0:T(8,128)} %bitcast.5.refs_0_, f32[17280,128]{1,0:T(8,128)} %bitcast.6.refs_1_.refs_0_.got, bf16[2,192,576]{2,1,0:T(8,128)(2,1)} %constant.44.clone.refs_2_.refs_1_.tables_and_outs_0_), custom_call_target="tpu_custom_call" | custom-call | flops 4076863488 | bytes 7077888 | tf_op jit(solution)/shard_map/to_space/pallas_call | solution.py:495
  274.5 23.6 %apply_first.1 = (f32[16,6,3,24,128]{4,3,2,1,0:T(8,128)}, f32[2,2,8,192]{3,2,1,0:T(8,128)}, f32[12,192,192]{2,1,0:T(8,128)}) custom-call(f32[1]{0:T(128)S(6)} %copy.36.weights, f32[17280,128]{1,0:T(8,128)} %bitcast.6.refs_1_.refs_0_.got, f32[12,384,192]{2,1,0:T(8,128)} %to_space.2.first, f32[12,384,192]{2,1,0:T(8,128)} %to_space.3.second, ...), custom_call_target="tpu_custom_call" | custom-call | flops 12230590464 | bytes 17694720 | tf_op jit(solution)/shard_map/apply_first/pallas_call | solution.py:525
  298.1 36.7 %all-to-all-done.2 = f32[16,432,128]{2,1,0:T(8,128)} async-done(((f32[16,432,128]{2,1,0:T(8,128)}), f32[16,432,128]{2,1,0:T(8,128)}, u32[]{:S(2)}, u32[]{:S(2)}) %all-to-all-start.2) | async-done | bytes 3538976 | tf_op jit(solution)/shard_map/all_to_all | solution.py:457
  334.8 4.9 all-to-all-start.3
  339.7 22.9 %apply_last.1 = (f32[16,6,2,24,128]{4,3,2,1,0:T(8,128)}, f32[16,6,24,128]{3,2,1,0:T(8,128)}, f32[2,2,8,192]{3,2,1,0:T(8,128)}, f32[12,192,192]{2,1,0:T(8,128)}) custom-call(f32[1]{0:T(128)S(6)} %copy.36.weights, f32[6912,128]{1,0:T(8,128)} %bitcast.4.got, f32[12,384,192]{2,1,0:T(8,128)} %to_space.2.first, f32[12,384,192]{2,1,0:T(8,128)} %to_space.3.second, ...), custom_call_target="tpu_custom_call" | custom-call | flops 12230590464 | bytes 17694720 | tf_op jit(solution)/shard_map/apply_last/pallas_call | solution.py:546
  362.6 0.0 copy-start.1
  362.6 0.0 copy-start.2
  362.6 0.0 copy-start.3
  362.6 5.3 pack.1
  367.9 1.2 collective-permute-start
  369.1 0.0 copy-done.1
  369.1 0.0 copy-done.2
  369.1 0.0 copy-done.3
  369.1 0.1 fusion
  369.3 0.0 copy-start
  369.3 0.1 copy.28
  369.4 0.1 reshape.76
  369.4 20.4 %collective-permute-done = f32[16,112,128]{2,1,0:T(8,128)S(1)} collective-permute-done((f32[16,112,128]{2,1,0:T(8,128)}, f32[16,112,128]{2,1,0:T(8,128)S(1)}, u32[]{:S(2)}, u32[]{:S(2)}) %collective-permute-start) | collective-permute-done | bytes 917536 | tf_op jit(solution)/shard_map/ppermute | solution.py:617
  389.8 1.3 add_select_fusion
  391.1 0.1 pad.9
  391.2 0.0 copy-done
  391.2 0.1 pad_maximum_fusion.1
  391.4 26.8 %all-to-all-done.3 = f32[16,432,128]{2,1,0:T(8,128)} async-done(((f32[16,432,128]{2,1,0:T(8,128)}), f32[16,432,128]{2,1,0:T(8,128)}, u32[]{:S(2)}, u32[]{:S(2)}) %all-to-all-start.3) | async-done | bytes 3538976 | tf_op jit(solution)/shard_map/all_to_all | solution.py:457
  418.1 53.6 %all_to_all.35 = f32[16,264,128]{2,1,0:T(8,128)} all-to-all(f32[16,264,128]{2,1,0:T(8,128)S(1)} %bitcast.28), channel_id=1, replica_groups=mesh['pool'=2,'pw'=16] {'pw'}, dimensions={0} | all-to-all | bytes 4325376 | tf_op jit(solution)/shard_map/all_to_all | solution.py:457
  471.8 3.9 mirror.1
  475.7 20.0 %all_to_all.36 = f32[16,64,128]{2,1,0:T(8,128)} all-to-all(f32[16,64,128]{2,1,0:T(8,128)} %mirror.1), channel_id=1, replica_groups=mesh['pool'=2,'pw'=16] {'pw'}, dimensions={0} | all-to-all | bytes 1048576 | tf_op jit(solution)/shard_map/all_to_all | solution.py:457
  495.7 5.2 all-to-all-start.6
  500.9 5.0 swap.1
  505.9 1.2 collective-permute-start.1
  507.1 0.9 slice_reduce_fusion
  508.0 0.6 reshape.82.inner
  508.6 12.3 %direct.1.base = f32[1,2,2,12,192,192]{5,4,3,2,1,0:T(8,128)} custom-call(s32[1]{0:T(128)} %bitcast.me, f32[1,2]{1,0:T(1,128)} %energies.3, f32[2,2,2]{2,1,0:T(2,128)} %reshape.82.inner, f32[1,2,2,12,192,192]{5,4,3,2,1,0:T(8,128)} %orbitals.3, f32[1,2,2,12,192,192]{5,4,3,2,1,0:T(8,128)} %responses.3), custom_call_target="tpu_custom_call" | custom-call | flops 113246208 | bytes 21233664 | tf_op jit(solution)/shard_map/direct/pallas_call | solution.py:622
  520.9 5.3 finish.4.base
  526.2 5.1 finish.5.base
  531.3 4.5 finish.6.base
  535.8 0.0 collective-permute-done.1
  535.8 1.8 slice_select_fusion.1
  537.6 2.1 pad_maximum_fusion
  539.7 14.3 %all-to-all-done.6 = f32[16,288,128]{2,1,0:T(8,128)} async-done(((f32[16,288,128]{2,1,0:T(8,128)}), f32[16,288,128]{2,1,0:T(8,128)}, u32[]{:S(2)}, u32[]{:S(2)}) %all-to-all-start.6) | async-done | bytes 2359328 | tf_op jit(solution)/shard_map/all_to_all | solution.py:457
  554.0 5.7 %finish.7 = f32[1,2,2,12,192,192]{5,4,3,2,1,0:T(8,128)} custom-call(s32[1]{0:T(128)} %bitcast.me, f32[4608,128]{1,0:T(8,128)} %bitcast.22.got, bf16[2,192,576]{2,1,0:T(8,128)(2,1)} %constant.46.clone.receive, f32[1,2,2,12,192,192]{5,4,3,2,1,0:T(8,128)} %finish.6.base), custom_call_target="tpu_custom_call", output_to_operand_aliasing={{}: (3, {})} | custom-call | flops 4076863488 | bytes 7077888 | tf_op jit(solution)/shard_map/finish/pallas_call | solution.py:567
  (2 shorter events, 0.0 us)
Async XLA Ops:
  7.3 47.0 %all-to-all-start = ((f32[16,216,128]{2,1,0:T(8,128)}), f32[16,216,128]{2,1,0:T(8,128)}, u32[]{:S(2)}, u32[]{:S(2)}) async-start(f32[16,216,128]{2,1,0:T(8,128)} %bitcast.33), calls=%async_computation | async-start | bytes 3538944 | tf_op jit(solution)/shard_map/all_to_all | solution.py:457
  54.4 197.1 %all-to-all-start.1 = ((f32[16,1080,128]{2,1,0:T(8,128)}), f32[16,1080,128]{2,1,0:T(8,128)}, u32[]{:S(2)}, u32[]{:S(2)}) async-start(f32[16,1080,128]{2,1,0:T(8,128)} %bitcast.24), calls=%async_computation.1 | async-start | bytes 17694720 | tf_op jit(solution)/shard_map/all_to_all | solution.py:457
  251.5 83.3 %all-to-all-start.2 = ((f32[16,432,128]{2,1,0:T(8,128)}), f32[16,432,128]{2,1,0:T(8,128)}, u32[]{:S(2)}, u32[]{:S(2)}) async-start(f32[16,432,128]{2,1,0:T(8,128)} %bitcast.31), calls=%async_computation.2 | async-start | bytes 7077888 | tf_op jit(solution)/shard_map/all_to_all | solution.py:457
  334.8 83.3 %all-to-all-start.3 = ((f32[16,432,128]{2,1,0:T(8,128)}), f32[16,432,128]{2,1,0:T(8,128)}, u32[]{:S(2)}, u32[]{:S(2)}) async-start(f32[16,432,128]{2,1,0:T(8,128)} %bitcast.30), calls=%async_computation.3 | async-start | bytes 7077888 | tf_op jit(solution)/shard_map/all_to_all | solution.py:457
  362.6 6.6 %copy-start.1 = (f32[2,2,2,8,192]{4,3,2,1,0:T(8,128)S(1)}, f32[2,2,2,8,192]{4,3,2,1,0:T(8,128)}, u32[]{:S(2)}) copy-start(f32[2,2,2,8,192]{4,3,2,1,0:T(8,128)} %inner.1) | copy-start | bytes 147460
  362.6 6.5 %copy-start.2 = (f32[2,2,8,192]{3,2,1,0:T(8,128)S(1)}, f32[2,2,8,192]{3,2,1,0:T(8,128)}, u32[]{:S(2)}) copy-start(f32[2,2,8,192]{3,2,1,0:T(8,128)} %get-tuple-element.26) | copy-start | bytes 73732
  362.6 6.5 %copy-start.3 = (f32[2,2,8,192]{3,2,1,0:T(8,128)S(1)}, f32[2,2,8,192]{3,2,1,0:T(8,128)}, u32[]{:S(2)}) copy-start(f32[2,2,8,192]{3,2,1,0:T(8,128)} %get-tuple-element.27) | copy-start | bytes 73732
  367.9 21.9 %collective-permute-start = (f32[16,112,128]{2,1,0:T(8,128)}, f32[16,112,128]{2,1,0:T(8,128)S(1)}, u32[]{:S(2)}, u32[]{:S(2)}) collective-permute-start(f32[16,112,128]{2,1,0:T(8,128)} %get-tuple-element.25), channel_id=1, source_target_pairs={{0,16},{16,0},{1,17},{17,1},{2,18},{18,2},{3,19},{19,3},{4,20},{20... | collective-permute-start | bytes 2752520 | tf_op jit(solution)/shard_map/ppermute | solution.py:617
  369.3 22.0 %copy-start = (f32[16,6,24,128]{3,2,1,0:T(8,128)S(1)}, f32[16,6,24,128]{3,2,1,0:T(8,128)}, u32[]{:S(2)}) copy-start(f32[16,6,24,128]{3,2,1,0:T(8,128)} %get-tuple-element.22) | copy-start | bytes 3538948
  495.7 58.4 %all-to-all-start.6 = ((f32[16,288,128]{2,1,0:T(8,128)}), f32[16,288,128]{2,1,0:T(8,128)}, u32[]{:S(2)}, u32[]{:S(2)}) async-start(f32[16,288,128]{2,1,0:T(8,128)} %bitcast.32), calls=%async_computation.6 | async-start | bytes 4718592 | tf_op jit(solution)/shard_map/all_to_all | solution.py:457
  505.9 29.9 %collective-permute-start.1 = (f32[12,192,128]{2,1,0:T(8,128)}, f32[12,192,128]{2,1,0:T(8,128)}, u32[]{:S(2)}, u32[]{:S(2)}) collective-permute-start(f32[12,192,128]{2,1,0:T(8,128)} %swap.1), channel_id=1, source_target_pairs={{0,16},{16,0},{1,17},{17,1},{2,18},{18,2},{3,19},{19,3},{4,20},{20... | collective-permute-start | bytes 3538952 | tf_op jit(solution)/shard_map/ppermute | solution.py:656

commit v5 on v4

--- a/solution.py
+++ b/solution.py
@@ -25,6 +25,11 @@
     return np.concatenate((high, high, low), axis=1)
 
 
+def tall_table(table):
+    high, low = split_table(table)
+    return np.concatenate((high, high, low), axis=0)
+
+
 @functools.cache
 def matrices(length, slab, members):
     index = np.arange(length)
@@ -32,7 +37,7 @@
     cosine = np.cos(angles) / math.sqrt(length)
     sine = np.sin(angles) / math.sqrt(length)
     lanes = 128 * -(-length // 128)
-    pad = ((0, 0), (0, lanes - length))
+    pad = ((0, lanes - length), (0, lanes - length))
     inverse = np.block([[cosine, -sine], [sine, cosine]])
     forward = np.block([[cosine, sine], [-sine, cosine]])
     sent = np.arange(2 * length).reshape(2, members, slab).transpose(1, 0, 2).reshape(-1)
@@ -58,9 +63,9 @@
     swapped[1, 0] = 0.0
     swapped[1, 0, slab, 0] = 1.0
     return {
-        "cosine": split_table(np.pad(cosine, pad)),
+        "cosine": tall_table(np.pad(cosine, pad)),
         "mixed": np.stack(
-            [split_table(np.pad(sine + sign * cosine, pad)) for sign in (-1.0, 1.0)]
+            [tall_table(np.pad(sine + sign * cosine, pad)) for sign in (-1.0, 1.0)]
         ),
         "inverse_send": np.stack([long_table(inverse[sent[:length]][:, one]) for one in parity]),
         "inverse_receive": np.stack([long_table(inverse[first][:, one]) for one in got]),
@@ -87,8 +92,10 @@
 
 
 def dot_right(values, table):
-    high, low = halves(values)
-    return dot(high, table[0]) + (dot(high, table[1]) + dot(low, table[0]))
+    rows, length = values.shape
+    fill = jnp.zeros((rows, table.shape[0] // 3 - length), jnp.float32)
+    high, low = halves(jnp.concatenate((values, fill), axis=1))
+    return dot(jnp.concatenate((high, low, high), axis=1), table[...])
 
 
 def dot_left(table, values):

time: 561 us -> 561 us (level)
  no operation moved by 1% of the time
where the time goes in v5:
time: 561 us; the launch traced here: 560 us
  waiting for transfers between devices  280 us (50%)
  Pallas kernels  169 us (30%)
  blocking collectives  73.6 us (13%)
  starting transfers between devices  28.9 us (5%)
  other arithmetic  6.33 us (1%)
    all_to_all x5, waiting for transfers between devices, exchange(): return lax.all_to_all(values, 'pw', split_axis=0, concat_axis=0, tiled=True)  259 us
    all_to_all x2, blocking collectives, exchange(): return lax.all_to_all(values, 'pw', split_axis=0, concat_axis=0, tiled=True)  73.6 us
    pallas_call x5, Pallas kernels, to_half(): call(kernel, 'to_half', grid, [pl.BlockSpec((1, 1, 2, 2, length, length),...  48 us
    all_to_all x5, starting transfers between devices, exchange(): return lax.all_to_all(values, 'pw', split_axis=0, concat_axis=0, tiled=True)  26.5 us
    pallas_call x1, Pallas kernels, apply_first(): call(kernel, 'apply_first', pairs, [scalars(), whole(), space_spec, space...  23.5 us
    pallas_call x1, Pallas kernels, apply_last(): call(kernel, 'apply_last', pairs, [scalars(), whole(), space_spec, space_...  22.8 us
    pallas_call x4, Pallas kernels, finish(): call(functools.partial(finish_kernel, slab, starts, stride, tail), 'finis...  20.6 us
    ppermute x1, waiting for transfers between devices, packed_body(): lax.ppermute(given, 'pool', swap)  20.4 us
  transfers between devices with their start and end apart: 7, of which 6 were waited for; matrix products, arithmetic and copies ran while one was open for 1% of the time, Pallas kernels for 27%

profile of v5, /device:TPU:13, one launch (start us, length us, event | category | flops | bytes accessed | tf_op | source)
XLA Modules:
  0.0 559.9 jit_solution(7127821621624627276)
XLA Ops:
  0.6 6.9 %to_half.9 = f32[16,3,1,3,24,128]{5,4,3,2,1,0:T(8,128)} custom-call(f32[1,2,2,12,192,192]{5,4,3,2,1,0:T(8,128)} %orbitals.3, bf16[768,256]{1,0:T(8,128)(2,1)} %constant.41.clone.cosine.tables_and_outs_1_, bf16[2,768,256]{2,1,0:T(8,128)(2,1)} %constant.42.clone.mixed.tables_and_outs_2_, bf16[2,192,576]{2,1,0:T(8,128)(2,1)} %constant.43.clone.send), custom_call_target="tpu_custom_call" | custom-call | flops 4076863488 | bytes 3538944 | tf_op jit(solution)/shard_map/to_half/pallas_call | solution.py:478
  7.5 6.6 %all-to-all-start = ((f32[16,216,128]{2,1,0:T(8,128)}), f32[16,216,128]{2,1,0:T(8,128)}, u32[]{:S(2)}, u32[]{:S(2)}) async-start(f32[16,216,128]{2,1,0:T(8,128)} %bitcast.33), calls=%async_computation | async-start | bytes 3538944 | tf_op jit(solution)/shard_map/all_to_all | solution.py:464
  14.1 6.9 %to_half.6.rest_0_ = f32[16,3,5,3,24,128]{5,4,3,2,1,0:T(8,128)} custom-call(f32[1,2,2,12,192,192]{5,4,3,2,1,0:T(8,128)} %orbitals.3, bf16[768,256]{1,0:T(8,128)(2,1)} %constant.41.clone.cosine.tables_and_outs_1_, bf16[2,768,256]{2,1,0:T(8,128)(2,1)} %constant.42.clone.mixed.tables_and_outs_2_, bf16[2,192,576]{2,1,0:T(8,128)(2,1)} %constant.43.clone.send), custom_call_target="tpu_custom_call" | custom-call | flops 4076863488 | bytes 3538944 | tf_op jit(solution)/shard_map/to_half/pallas_call | solution.py:478
  21.0 11.4 %to_half.7.rest_0_ = f32[16,3,5,3,24,128]{5,4,3,2,1,0:T(8,128)} custom-call(f32[1,2,2,12,192,192]{5,4,3,2,1,0:T(8,128)} %orbitals.3, bf16[768,256]{1,0:T(8,128)(2,1)} %constant.41.clone.cosine.tables_and_outs_1_, bf16[2,768,256]{2,1,0:T(8,128)(2,1)} %constant.42.clone.mixed.tables_and_outs_2_, ...), custom_call_target="tpu_custom_call", output_to_operand_aliasing={{}: (4, {})} | custom-call | flops 8153726976 | bytes 7077888 | tf_op jit(solution)/shard_map/to_half/pallas_call | solution.py:478
  32.4 11.4 %to_half.8 = f32[16,3,5,3,24,128]{5,4,3,2,1,0:T(8,128)} custom-call(f32[1,2,2,12,192,192]{5,4,3,2,1,0:T(8,128)} %responses.3, bf16[768,256]{1,0:T(8,128)(2,1)} %constant.41.clone.cosine.tables_and_outs_1_, bf16[2,768,256]{2,1,0:T(8,128)(2,1)} %constant.42.clone.mixed.tables_and_outs_2_, ...), custom_call_target="tpu_custom_call", output_to_operand_aliasing={{}: (4, {})} | custom-call | flops 8153726976 | bytes 7077888 | tf_op jit(solution)/shard_map/to_half/pallas_call | solution.py:478
  43.8 10.8 %all-to-all-done = f32[16,216,128]{2,1,0:T(8,128)} async-done(((f32[16,216,128]{2,1,0:T(8,128)}), f32[16,216,128]{2,1,0:T(8,128)}, u32[]{:S(2)}, u32[]{:S(2)}) %all-to-all-start) | async-done | bytes 1769504 | tf_op jit(solution)/shard_map/all_to_all | solution.py:464
  54.6 4.9 all-to-all-start.1
  59.5 10.1 %inner.1 = f32[2,2,2,8,192]{4,3,2,1,0:T(8,128)} custom-call(s32[1]{0:T(128)} %bitcast.me, f32[1,2]{1,0:T(1,128)} %energies.3, f32[1,2,2,12,192,192]{5,4,3,2,1,0:T(8,128)} %orbitals.3, f32[1,2,2,12,192,192]{5,4,3,2,1,0:T(8,128)} %responses.3), custom_call_target="tpu_custom_call" | custom-call | flops 113246208 | bytes 14155776 | tf_op jit(solution)/shard_map/inner/pallas_call | solution.py:591
  69.6 11.4 %to_half.5 = f32[16,3,2,3,24,128]{5,4,3,2,1,0:T(8,128)} custom-call(f32[1,2,2,12,192,192]{5,4,3,2,1,0:T(8,128)} %responses.3, bf16[768,256]{1,0:T(8,128)(2,1)} %constant.41.clone.cosine.tables_and_outs_1_, bf16[2,768,256]{2,1,0:T(8,128)(2,1)} %constant.42.clone.mixed.tables_and_outs_2_, bf16[2,192,576]{2,1,0:T(8,128)(2,1)} %constant.43.clone.send), custom_call_target="tpu_custom_call" | custom-call | flops 8153726976 | bytes 7077888 | tf_op jit(solution)/shard_map/to_half/pallas_call | solution.py:478
  81.1 170.6 %all-to-all-done.1 = f32[16,1080,128]{2,1,0:T(8,128)} async-done(((f32[16,1080,128]{2,1,0:T(8,128)}), f32[16,1080,128]{2,1,0:T(8,128)}, u32[]{:S(2)}, u32[]{:S(2)}) %all-to-all-start.1) | async-done | bytes 8847392 | tf_op jit(solution)/shard_map/all_to_all | solution.py:464
  251.7 4.9 all-to-all-start.2
  257.2 8.6 %to_space.3.second = f32[12,384,192]{2,1,0:T(8,128)} custom-call(f32[17280,128]{1,0:T(8,128)} %bitcast.6.refs_1_.refs_0_.got, bf16[2,192,576]{2,1,0:T(8,128)(2,1)} %constant.44.clone.refs_2_.refs_1_.tables_and_outs_0_), custom_call_target="tpu_custom_call" | custom-call | flops 4076863488 | bytes 7077888 | tf_op jit(solution)/shard_map/to_space/pallas_call | solution.py:502
  265.8 8.9 %to_space.2.first = f32[12,384,192]{2,1,0:T(8,128)} custom-call(f32[3456,128]{1,0:T(8,128)} %bitcast.5.refs_0_, f32[17280,128]{1,0:T(8,128)} %bitcast.6.refs_1_.refs_0_.got, bf16[2,192,576]{2,1,0:T(8,128)(2,1)} %constant.44.clone.refs_2_.refs_1_.tables_and_outs_0_), custom_call_target="tpu_custom_call" | custom-call | flops 4076863488 | bytes 7077888 | tf_op jit(solution)/shard_map/to_space/pallas_call | solution.py:502
  274.7 23.5 %apply_first.1 = (f32[16,6,3,24,128]{4,3,2,1,0:T(8,128)}, f32[2,2,8,192]{3,2,1,0:T(8,128)}, f32[12,192,192]{2,1,0:T(8,128)}) custom-call(f32[1]{0:T(128)S(6)} %copy.36.weights, f32[17280,128]{1,0:T(8,128)} %bitcast.6.refs_1_.refs_0_.got, f32[12,384,192]{2,1,0:T(8,128)} %to_space.2.first, f32[12,384,192]{2,1,0:T(8,128)} %to_space.3.second, ...), custom_call_target="tpu_custom_call" | custom-call | flops 12230590464 | bytes 17694720 | tf_op jit(solution)/shard_map/apply_first/pallas_call | solution.py:532
  298.1 36.9 %all-to-all-done.2 = f32[16,432,128]{2,1,0:T(8,128)} async-done(((f32[16,432,128]{2,1,0:T(8,128)}), f32[16,432,128]{2,1,0:T(8,128)}, u32[]{:S(2)}, u32[]{:S(2)}) %all-to-all-start.2) | async-done | bytes 3538976 | tf_op jit(solution)/shard_map/all_to_all | solution.py:464
  335.0 4.9 all-to-all-start.3
  339.9 22.8 %apply_last.1 = (f32[16,6,2,24,128]{4,3,2,1,0:T(8,128)}, f32[16,6,24,128]{3,2,1,0:T(8,128)}, f32[2,2,8,192]{3,2,1,0:T(8,128)}, f32[12,192,192]{2,1,0:T(8,128)}) custom-call(f32[1]{0:T(128)S(6)} %copy.36.weights, f32[6912,128]{1,0:T(8,128)} %bitcast.4.got, f32[12,384,192]{2,1,0:T(8,128)} %to_space.2.first, f32[12,384,192]{2,1,0:T(8,128)} %to_space.3.second, ...), custom_call_target="tpu_custom_call" | custom-call | flops 12230590464 | bytes 17694720 | tf_op jit(solution)/shard_map/apply_last/pallas_call | solution.py:553
  362.7 0.0 copy-start.1
  362.7 0.0 copy-start.2
  362.7 0.0 copy-start.3
  362.7 5.3 pack.1
  368.0 1.2 collective-permute-start
  369.2 0.0 copy-done.1
  369.2 0.0 copy-done.2
  369.2 0.0 copy-done.3
  369.2 0.1 fusion
  369.4 0.0 copy-start
  369.4 0.1 copy.28
  369.5 0.1 reshape.76
  369.5 20.4 %collective-permute-done = f32[16,112,128]{2,1,0:T(8,128)S(1)} collective-permute-done((f32[16,112,128]{2,1,0:T(8,128)}, f32[16,112,128]{2,1,0:T(8,128)S(1)}, u32[]{:S(2)}, u32[]{:S(2)}) %collective-permute-start) | collective-permute-done | bytes 917536 | tf_op jit(solution)/shard_map/ppermute | solution.py:624
  389.9 1.3 add_select_fusion
  391.2 0.1 pad.9
  391.3 0.0 copy-done
  391.3 0.1 pad_maximum_fusion.1
  391.5 26.9 %all-to-all-done.3 = f32[16,432,128]{2,1,0:T(8,128)} async-done(((f32[16,432,128]{2,1,0:T(8,128)}), f32[16,432,128]{2,1,0:T(8,128)}, u32[]{:S(2)}, u32[]{:S(2)}) %all-to-all-start.3) | async-done | bytes 3538976 | tf_op jit(solution)/shard_map/all_to_all | solution.py:464
  418.3 53.6 %all_to_all.35 = f32[16,264,128]{2,1,0:T(8,128)} all-to-all(f32[16,264,128]{2,1,0:T(8,128)S(1)} %bitcast.28), channel_id=1, replica_groups=mesh['pool'=2,'pw'=16] {'pw'}, dimensions={0} | all-to-all | bytes 4325376 | tf_op jit(solution)/shard_map/all_to_all | solution.py:464
  472.0 3.9 mirror.1
  475.9 20.0 %all_to_all.36 = f32[16,64,128]{2,1,0:T(8,128)} all-to-all(f32[16,64,128]{2,1,0:T(8,128)} %mirror.1), channel_id=1, replica_groups=mesh['pool'=2,'pw'=16] {'pw'}, dimensions={0} | all-to-all | bytes 1048576 | tf_op jit(solution)/shard_map/all_to_all | solution.py:464
  495.8 5.2 all-to-all-start.6
  501.1 5.0 swap.1
  506.1 1.2 collective-permute-start.1
  507.3 0.9 slice_reduce_fusion
  508.2 0.6 reshape.82.inner
  508.8 12.3 %direct.1.base = f32[1,2,2,12,192,192]{5,4,3,2,1,0:T(8,128)} custom-call(s32[1]{0:T(128)} %bitcast.me, f32[1,2]{1,0:T(1,128)} %energies.3, f32[2,2,2]{2,1,0:T(2,128)} %reshape.82.inner, f32[1,2,2,12,192,192]{5,4,3,2,1,0:T(8,128)} %orbitals.3, f32[1,2,2,12,192,192]{5,4,3,2,1,0:T(8,128)} %responses.3), custom_call_target="tpu_custom_call" | custom-call | flops 113246208 | bytes 21233664 | tf_op jit(solution)/shard_map/direct/pallas_call | solution.py:629
  521.1 5.3 finish.4.base
  526.4 5.1 finish.5.base
  531.4 4.5 finish.6.base
  536.0 0.0 collective-permute-done.1
  536.0 1.8 slice_select_fusion.1
  537.8 2.1 pad_maximum_fusion
  539.9 14.3 %all-to-all-done.6 = f32[16,288,128]{2,1,0:T(8,128)} async-done(((f32[16,288,128]{2,1,0:T(8,128)}), f32[16,288,128]{2,1,0:T(8,128)}, u32[]{:S(2)}, u32[]{:S(2)}) %all-to-all-start.6) | async-done | bytes 2359328 | tf_op jit(solution)/shard_map/all_to_all | solution.py:464
  554.2 5.7 %finish.7 = f32[1,2,2,12,192,192]{5,4,3,2,1,0:T(8,128)} custom-call(s32[1]{0:T(128)} %bitcast.me, f32[4608,128]{1,0:T(8,128)} %bitcast.22.got, bf16[2,192,576]{2,1,0:T(8,128)(2,1)} %constant.46.clone.receive, f32[1,2,2,12,192,192]{5,4,3,2,1,0:T(8,128)} %finish.6.base), custom_call_target="tpu_custom_call", output_to_operand_aliasing={{}: (3, {})} | custom-call | flops 4076863488 | bytes 7077888 | tf_op jit(solution)/shard_map/finish/pallas_call | solution.py:574
  (2 shorter events, 0.0 us)
Async XLA Ops:
  7.5 47.1 %all-to-all-start = ((f32[16,216,128]{2,1,0:T(8,128)}), f32[16,216,128]{2,1,0:T(8,128)}, u32[]{:S(2)}, u32[]{:S(2)}) async-start(f32[16,216,128]{2,1,0:T(8,128)} %bitcast.33), calls=%async_computation | async-start | bytes 3538944 | tf_op jit(solution)/shard_map/all_to_all | solution.py:464
  54.6 197.1 %all-to-all-start.1 = ((f32[16,1080,128]{2,1,0:T(8,128)}), f32[16,1080,128]{2,1,0:T(8,128)}, u32[]{:S(2)}, u32[]{:S(2)}) async-start(f32[16,1080,128]{2,1,0:T(8,128)} %bitcast.24), calls=%async_computation.1 | async-start | bytes 17694720 | tf_op jit(solution)/shard_map/all_to_all | solution.py:464
  251.7 83.3 %all-to-all-start.2 = ((f32[16,432,128]{2,1,0:T(8,128)}), f32[16,432,128]{2,1,0:T(8,128)}, u32[]{:S(2)}, u32[]{:S(2)}) async-start(f32[16,432,128]{2,1,0:T(8,128)} %bitcast.31), calls=%async_computation.2 | async-start | bytes 7077888 | tf_op jit(solution)/shard_map/all_to_all | solution.py:464
  335.0 83.3 %all-to-all-start.3 = ((f32[16,432,128]{2,1,0:T(8,128)}), f32[16,432,128]{2,1,0:T(8,128)}, u32[]{:S(2)}, u32[]{:S(2)}) async-start(f32[16,432,128]{2,1,0:T(8,128)} %bitcast.30), calls=%async_computation.3 | async-start | bytes 7077888 | tf_op jit(solution)/shard_map/all_to_all | solution.py:464
  362.7 6.6 %copy-start.1 = (f32[2,2,2,8,192]{4,3,2,1,0:T(8,128)S(1)}, f32[2,2,2,8,192]{4,3,2,1,0:T(8,128)}, u32[]{:S(2)}) copy-start(f32[2,2,2,8,192]{4,3,2,1,0:T(8,128)} %inner.1) | copy-start | bytes 147460
  362.7 6.6 %copy-start.2 = (f32[2,2,8,192]{3,2,1,0:T(8,128)S(1)}, f32[2,2,8,192]{3,2,1,0:T(8,128)}, u32[]{:S(2)}) copy-start(f32[2,2,8,192]{3,2,1,0:T(8,128)} %get-tuple-element.26) | copy-start | bytes 73732
  362.7 6.6 %copy-start.3 = (f32[2,2,8,192]{3,2,1,0:T(8,128)S(1)}, f32[2,2,8,192]{3,2,1,0:T(8,128)}, u32[]{:S(2)}) copy-start(f32[2,2,8,192]{3,2,1,0:T(8,128)} %get-tuple-element.27) | copy-start | bytes 73732
  368.0 21.9 %collective-permute-start = (f32[16,112,128]{2,1,0:T(8,128)}, f32[16,112,128]{2,1,0:T(8,128)S(1)}, u32[]{:S(2)}, u32[]{:S(2)}) collective-permute-start(f32[16,112,128]{2,1,0:T(8,128)} %get-tuple-element.25), channel_id=1, source_target_pairs={{0,16},{16,0},{1,17},{17,1},{2,18},{18,2},{3,19},{19,3},{4,20},{20... | collective-permute-start | bytes 2752520 | tf_op jit(solution)/shard_map/ppermute | solution.py:624
  369.4 22.0 %copy-start = (f32[16,6,24,128]{3,2,1,0:T(8,128)S(1)}, f32[16,6,24,128]{3,2,1,0:T(8,128)}, u32[]{:S(2)}) copy-start(f32[16,6,24,128]{3,2,1,0:T(8,128)} %get-tuple-element.22) | copy-start | bytes 3538948
  495.8 58.4 %all-to-all-start.6 = ((f32[16,288,128]{2,1,0:T(8,128)}), f32[16,288,128]{2,1,0:T(8,128)}, u32[]{:S(2)}, u32[]{:S(2)}) async-start(f32[16,288,128]{2,1,0:T(8,128)} %bitcast.32), calls=%async_computation.6 | async-start | bytes 4718592 | tf_op jit(solution)/shard_map/all_to_all | solution.py:464
  506.1 29.9 %collective-permute-start.1 = (f32[12,192,128]{2,1,0:T(8,128)}, f32[12,192,128]{2,1,0:T(8,128)}, u32[]{:S(2)}, u32[]{:S(2)}) collective-permute-start(f32[12,192,128]{2,1,0:T(8,128)} %swap.1), channel_id=1, source_target_pairs={{0,16},{16,0},{1,17},{17,1},{2,18},{18,2},{3,19},{19,3},{4,20},{20... | collective-permute-start | bytes 3538952 | tf_op jit(solution)/shard_map/ppermute | solution.py:663
